TPU v7x, 32 devices: a whole 2x2x4 slice. The times are simulated.
32 devices in a mesh: grp: 4 (over x, core), row: 8 (over z, y).
Axes of the slice: x: 2, y: 2, z: 4, core: 2. Of those that a mesh axis runs over, the one named last changes fastest.
Arguments:
- pair_feats: bfloat16 [16, 6, 128, 128, 128], P('grp', None, 'row'), may hold values from -6 to 6
- block_cols: int32 [16, 6], replicated, may hold values from 0 to 15, as said below
- attn_mask: int32 [16, 6], replicated, may hold values from 0 to 1, as said below
- chain_of_row: int32 [16], replicated, may hold values from 0 to 3
- same_chain: float32 [16], replicated, may hold values from -2 to 2
- node_feats: bfloat16 [2048, 768], P('grp'), may hold values from -6 to 6
- node_cotangent: bfloat16 [2048, 768], P('grp'), may hold values from -6 to 6
- tri_weight: bfloat16 [128, 256], replicated, may hold values from -0.5 to 0.5
- gate_weight: bfloat16 [128, 128], replicated, may hold values from -0.5 to 0.5
- tri_out_weight: bfloat16 [64, 128], replicated, may hold values from -0.75 to 0.75
- bias_weight: bfloat16 [128, 16], replicated, may hold values from -0.5 to 0.5
- query_weight: bfloat16 [768, 768], P(None, 'row'), may hold values from -8 to 8
- key_weight: bfloat16 [768, 768], P(None, 'row'), may hold values from -8 to 8
- value_weight: bfloat16 [768, 768], P(None, 'row'), may hold values from -0.21875 to 0.21875
- out_weight: bfloat16 [768, 768], P('row'), may hold values from -0.21875 to 0.21875
Outputs:
- pair_out: bfloat16 [16, 6, 128, 128, 128], P('grp', None, 'row')
- node_out: bfloat16 [2048, 768], P(('grp', 'row'))
- pair_grad: bfloat16 [16, 6, 128, 128, 128], P('grp', None, 'row')
Inputs may be any that keep to these rules, and one draw needn't show every extreme that they name: `block_cols`: block row I belongs to chain group I // 4. Its 6 columns are distinct: itself in slot 0, the other block rows of its own group, and 2 block rows of other groups. The rows of one group name block rows of at most 3 other groups and at most 2 distinct block rows of any one other group; some pair of groups reaches 2. `attn_mask`: slot 0 of every block row is 1.
All inputs are finite; a program needn't handle non-finite values.
Results may differ from a plain program's by a relative error of at most 0.025.
Values may be sent and summed in bfloat16 or wider, within the bound.
No kernel may reach another device: no remote copies, remote signals or barrier semaphores. Data moves between devices by JAX's collectives and lax.ppermute only.
A program may use at most 192 MiB of HBM per device.

v0:
```python
import jax
import jax.numpy as jnp
from jax import lax
from jax.sharding import PartitionSpec as P

CAPX = 2


epsilon = 1e-05


def norm_parts(values, dimension):
    center = jnp.mean(values, axis=dimension, keepdims=True)
    shifted = values - center
    spread = jnp.mean(shifted * shifted, axis=dimension, keepdims=True)
    inverse = lax.rsqrt(spread + epsilon)
    return (shifted * inverse, inverse)


def per_device(
    pair_feats,
    block_cols,
    attn_mask,
    chain_of_row,
    same_chain,
    node_feats,
    node_cotangent,
    tri_weight,
    gate_weight,
    tri_out_weight,
    bias_weight,
    query_weight,
    key_weight,
    value_weight,
    out_weight,
):
    rows_split = lax.axis_size("row")
    group_count = lax.axis_size("grp")
    group_index = lax.axis_index("grp")
    row_index = lax.axis_index("row")
    block_rows = pair_feats.shape[0]
    slot_count = pair_feats.shape[1]
    block_size = pair_feats.shape[3]
    hidden = tri_weight.shape[1] // 4
    hid_part = hidden // rows_split
    head_count = bias_weight.shape[1]
    head_part = head_count // rows_split
    width_part = query_weight.shape[1]
    head_size = width_part // head_part
    total_rows = block_cols.shape[0]
    capacity = CAPX
    first_row = group_index * block_rows
    own_cols = lax.dynamic_slice_in_dim(block_cols, first_row, block_rows, 0)
    pair_float = pair_feats.astype(jnp.float32)
    normed, pair_scale = norm_parts(pair_float, 4)
    normed_short = normed.astype(jnp.bfloat16)
    projected = jnp.einsum(
        "rsijc,cx->rsxij", normed_short, tri_weight, preferred_element_type=jnp.float32
    )
    left_proj = (
        jax.nn.sigmoid(projected[:, :, hidden : 2 * hidden]) * projected[:, :, :hidden]
    ).astype(jnp.bfloat16)
    right_proj = (
        jax.nn.sigmoid(projected[:, :, 3 * hidden :]) * projected[:, :, 2 * hidden : 3 * hidden]
    ).astype(jnp.bfloat16)
    gate_values = jax.nn.sigmoid(
        jnp.einsum("rsijc,cy->rsijy", normed_short, gate_weight, preferred_element_type=jnp.float32)
    ).astype(jnp.bfloat16)
    bias_rows = jnp.einsum(
        "rsijc,ch->rshij", normed_short, bias_weight, preferred_element_type=jnp.float32
    ).astype(jnp.bfloat16)
    left_chan, right_chan, bias_chan = (
        lax.all_to_all(left_proj, "row", split_axis=2, concat_axis=3, tiled=True),
        lax.all_to_all(right_proj, "row", split_axis=2, concat_axis=3, tiled=True),
        lax.all_to_all(bias_rows, "row", split_axis=2, concat_axis=3, tiled=True),
    )
    targets = jnp.arange(total_rows, dtype=jnp.int32)
    group_cols = block_cols.reshape(group_count, block_rows * slot_count)
    named_rows = jnp.max(
        (group_cols[:, :, None] == targets[None, None, :]).astype(jnp.int32), axis=1
    )
    owner_group = targets // block_rows
    outside = (owner_group[None, :] != jnp.arange(group_count, dtype=jnp.int32)[:, None]).astype(
        jnp.int32
    )
    named_rows = named_rows * outside
    named_grouped = named_rows.reshape(group_count, group_count, block_rows)
    slot_rank = (jnp.cumsum(named_grouped, axis=2) - named_grouped).reshape(group_count, total_rows)
    sent_named = lax.dynamic_slice_in_dim(named_rows, first_row, block_rows, 1)
    sent_rank = lax.dynamic_slice_in_dim(slot_rank, first_row, block_rows, 1)
    slot_ids = jnp.arange(capacity, dtype=jnp.int32)
    selection = (
        sent_named[:, None, :]
        * (sent_rank[:, None, :] == slot_ids[None, :, None]).astype(jnp.int32)
    ).astype(jnp.bfloat16)
    my_rank = lax.dynamic_index_in_dim(slot_rank, group_index, 0, keepdims=False)
    outgoing = jnp.einsum(
        "hcl,lsdjk->hcsdjk", selection, right_chan, preferred_element_type=jnp.float32
    ).astype(jnp.bfloat16)
    arrived = lax.all_to_all(outgoing, "grp", split_axis=0, concat_axis=0, tiled=True)
    arrived = arrived.reshape(group_count * capacity, slot_count, hid_part, block_size, block_size)
    table = jnp.concatenate([right_chan, arrived], axis=0)
    local_place = jnp.clip(targets - first_row, 0, block_rows - 1)
    remote_place = block_rows + owner_group * capacity + jnp.clip(my_rank, 0, capacity - 1)
    table_place = jnp.where(owner_group == group_index, local_place, remote_place)

    def triangle_row(left_row, row_cols):
        places = jnp.take(table_place, row_cols, axis=0)
        far_rows = jnp.take(table, places, axis=0)
        far_cols = jnp.take(block_cols, row_cols, axis=0)
        matches = (row_cols[None, :, None] == far_cols[:, None, :]).astype(jnp.bfloat16)
        aligned = jnp.einsum(
            "stu,sudjk->stdjk", matches, far_rows, preferred_element_type=jnp.float32
        ).astype(jnp.bfloat16)
        return jnp.einsum(
            "tdik,stdjk->sdij", left_row, aligned, preferred_element_type=jnp.float32
        ).astype(jnp.bfloat16)

    tri_chan = jax.vmap(triangle_row)(left_chan, own_cols)
    node_norm = norm_parts(node_feats.astype(jnp.float32), 1)[0].astype(jnp.bfloat16)
    queries = jnp.dot(node_norm, query_weight, preferred_element_type=jnp.float32).astype(
        jnp.bfloat16
    )
    keys_here = jnp.dot(node_norm, key_weight, preferred_element_type=jnp.float32).astype(
        jnp.bfloat16
    )
    values_here = jnp.dot(node_norm, value_weight, preferred_element_type=jnp.float32).astype(
        jnp.bfloat16
    )
    keys_all, values_all = (
        lax.all_gather(keys_here, "grp", axis=0, tiled=True),
        lax.all_gather(values_here, "grp", axis=0, tiled=True),
    )
    keys_all = keys_all.reshape(total_rows, block_size, head_part, head_size)
    values_all = values_all.reshape(total_rows, block_size, head_part, head_size)
    queries = queries.reshape(block_rows, block_size, head_part, head_size)
    cot_heads = lax.dot_general(
        node_cotangent, out_weight, (((1,), (1,)), ((), ())), preferred_element_type=jnp.float32
    ).astype(jnp.bfloat16)
    cot_heads = cot_heads.reshape(block_rows, block_size, head_part, head_size)
    chain_bias = lax.dynamic_slice_in_dim(same_chain, row_index * head_part, head_part, 0)
    own_chain = lax.dynamic_slice_in_dim(chain_of_row, first_row, block_rows, 0)
    own_mask = lax.dynamic_slice_in_dim(attn_mask, first_row, block_rows, 0)
    score_scale = head_size ** (-0.5)

    def attend_row(query_rows, cot_rows, bias_block, row_cols, row_chain, row_mask):
        near_keys = jnp.take(keys_all, row_cols, axis=0)
        near_values = jnp.take(values_all, row_cols, axis=0)
        same_flag = (jnp.take(chain_of_row, row_cols) == row_chain).astype(jnp.float32)
        scores = (
            jnp.einsum("ihd,sjhd->shij", query_rows, near_keys, preferred_element_type=jnp.float32)
            * score_scale
        )
        scores = (
            scores
            + bias_block.astype(jnp.float32)
            + chain_bias[None, :, None, None] * same_flag[:, None, None, None]
        )
        scores = jnp.where((row_mask > 0)[:, None, None, None], scores, -jnp.inf)
        row_top = jnp.max(scores, axis=(0, 3), keepdims=True)
        exp_scores = jnp.exp(scores - row_top)
        probabilities = exp_scores / jnp.sum(exp_scores, axis=(0, 3), keepdims=True)
        probs_low = probabilities.astype(jnp.bfloat16)
        mixed_heads = jnp.einsum(
            "shij,sjhd->ihd", probs_low, near_values, preferred_element_type=jnp.float32
        ).astype(jnp.bfloat16)
        grad_probs = jnp.einsum(
            "ihd,sjhd->shij", cot_rows, near_values, preferred_element_type=jnp.float32
        )
        row_total = jnp.sum(probabilities * grad_probs, axis=(0, 3), keepdims=True)
        grad_scores = (probabilities * (grad_probs - row_total)).astype(jnp.bfloat16)
        return (mixed_heads.reshape(block_size, width_part), grad_scores)

    mixed_rows, grad_blocks = jax.vmap(attend_row)(
        queries, cot_heads, bias_chan, own_cols, own_chain, own_mask
    )
    node_rows = block_rows * block_size // rows_split
    mixed_nodes = mixed_rows.reshape(block_rows * block_size, width_part)
    summed = lax.psum_scatter(
        jnp.dot(mixed_nodes, out_weight, preferred_element_type=jnp.float32).astype(jnp.bfloat16),
        "row",
        scatter_dimension=0,
        tiled=True,
    ).astype(jnp.float32)
    own_nodes = lax.dynamic_slice_in_dim(node_feats, row_index * node_rows, node_rows, 0)
    node_out = (own_nodes.astype(jnp.float32) + summed).astype(jnp.bfloat16)
    tri_rows, grad_rows = (
        lax.all_to_all(tri_chan, "row", split_axis=3, concat_axis=2, tiled=True),
        lax.all_to_all(grad_blocks, "row", split_axis=3, concat_axis=2, tiled=True),
    )
    tri_norm = norm_parts(tri_rows.astype(jnp.float32), 2)[0].astype(jnp.bfloat16)
    update = jnp.einsum(
        "rsxij,xc->rsijc", tri_norm, tri_out_weight, preferred_element_type=jnp.float32
    )
    pair_out = (pair_float + gate_values.astype(jnp.float32) * update).astype(jnp.bfloat16)
    grad_normed = jnp.einsum(
        "rshij,ch->rsijc", grad_rows, bias_weight, preferred_element_type=jnp.float32
    )
    centre_grad = grad_normed - jnp.mean(grad_normed, axis=4, keepdims=True)
    projection_mean = jnp.mean(grad_normed * normed, axis=4, keepdims=True)
    pair_grad = (pair_scale * (centre_grad - normed * projection_mean)).astype(jnp.bfloat16)
    return (pair_out, node_out, pair_grad)


def solution(mesh):
    in_specs = (
        P("grp", None, "row", None, None),
        P(),
        P(),
        P(),
        P(),
        P("grp", None),
        P("grp", None),
        P(),
        P(),
        P(),
        P(),
        P(None, "row"),
        P(None, "row"),
        P(None, "row"),
        P("row", None),
    )
    out_specs = (
        P("grp", None, "row", None, None),
        P(("grp", "row"), None),
        P("grp", None, "row", None, None),
    )
    return jax.shard_map(
        per_device, mesh=mesh, in_specs=in_specs, out_specs=out_specs, check_vma=False
    )
```

profile of v0, /device:TPU:0, one launch (start us, length us, event | category | flops | bytes accessed | tf_op | source)
XLA Modules:
  0.0 1086.3 jit_solution(5492168557899008726)
XLA Ops:
  7.2 9.0 convert_reduce_fusion
  16.3 14.8 %fusion.14 = f32[4,6,16,128]{3,2,1,0:T(8,128)S(1)} fusion(bf16[4,6,16,128,128]{4,3,2,1,0:T(8,128)(2,1)S(1)} %copy-done.3, f32[4,6,16,128]{3,2,1,0:T(8,128)S(1)} %broadcast_multiply_fusion.3), kind=kLoop, calls=%fused_computation.24 | loop fusion | flops 25116672 | bytes 12976128 | tf_op jit(solution)/shard_map/reduce_sum | solution.py:15
  31.2 19.1 %fusion.52 = bf16[4,6,16,16,128]{4,2,3,1,0:T(8,128)(2,1)S(1)} fusion(bf16[4,6,16,128,128]{4,3,2,1,0:T(8,128)(2,1)S(1)} %copy-done.3, f32[4,6,16,128]{3,2,1,0:T(8,128)S(1)} %add_rsqrt_fusion.1, f32[4,6,16,128]{3,2,1,0:T(8,128)S(1)} %broadcast_multiply_fusion.3, bf16[128,16]{0,1:T(8,128)(2,1)S(1)} %copy-done.22), kind=kOutput, calls=%fused_computation.73 | convolution fusion | flops 227278848 | bytes 14553088 | tf_op jit(solution)/shard_map/rsijc,ch->rshij/dot_general | solution.py:69
  51.8 7.3 all-to-all-start.4
  59.1 21.2 %fusion.31 = f32[4,6,16,128,256]{4,3,2,1,0:T(8,128)} fusion(bf16[4,6,16,128,128]{4,3,2,1,0:T(8,128)(2,1)} %param.17, f32[4,6,16,128]{3,2,1,0:T(8,128)S(1)} %add_rsqrt_fusion.1, f32[4,6,16,128]{3,2,1,0:T(8,128)S(1)} %broadcast_multiply_fusion.3, bf16[128,256]{1,0:T(8,128)(2,1)S(1)} %copy-done.18), kind=kOutput, calls=%fused_computation.51 | convolution fusion | flops 3246391296 | bytes 63373312 | tf_op jit(solution)/shard_map/rsijc,cx->rsxij/dot_general | solution.py:57
  80.3 49.7 %copy.249 = f32[4,6,16,128,256]{3,2,4,1,0:T(8,128)} copy(f32[4,6,16,128,256]{4,3,2,1,0:T(8,128)} %fusion.31) | data formatting | bytes 100663296 | tf_op jit(solution)/shard_map/rsijc,cx->rsxij/dot_general | solution.py:57
  130.0 20.5 %fusion.21 = (bf16[4,6,64,16,128]{4,3,2,1,0:T(8,128)(2,1)S(1)}, bf16[4,6,64,16,128]{4,3,2,1,0:T(8,128)(2,1)}) fusion(f32[4,6,256,16,128]{4,3,2,1,0:T(8,128)} %bitcast.155), kind=kLoop, calls=%fused_computation.36 | loop fusion | flops 31457280 | bytes 62914560 | tf_op jit(solution)/shard_map/convert_element_type | solution.py:65
  150.5 4.5 copy.250
  154.9 6.0 all-to-all-start
  160.9 7.3 copy.256
  168.3 130.3 %all-to-all-done = bf16[4,6,64,16,128]{4,3,1,0,2:T(8,128)(2,1)} async-done(((bf16[4,6,64,16,128]{4,3,1,0,2:T(8,128)(2,1)}), bf16[4,6,64,16,128]{4,3,1,0,2:T(8,128)(2,1)}, u32[]{:S(2)}, u32[]{:S(2)}) %all-to-all-start) | async-done | bytes 6291488 | tf_op jit(solution)/shard_map/all_to_all | solution.py:74
  298.6 5.0 all-to-all-start.2
  304.9 10.3 copy.252
  315.2 6.6 convolution_convert_fusion
  321.8 6.6 copy.253
  328.5 112.4 %all-to-all-done.2 = bf16[4,6,64,16,128]{4,3,1,0,2:T(8,128)(2,1)} async-done(((bf16[4,6,64,16,128]{4,3,1,0,2:T(8,128)(2,1)}), bf16[4,6,64,16,128]{4,3,1,0,2:T(8,128)(2,1)}, u32[]{:S(2)}, u32[]{:S(2)}) %all-to-all-start.2) | async-done | bytes 6291488 | tf_op jit(solution)/shard_map/all_to_all | solution.py:73
  440.9 6.4 all-to-all-start.1
  451.5 136.7 %all_gather.7 = bf16[2048,96]{0,1:T(8,128)(2,1)S(1)} all-gather(bf16[512,96]{0,1:T(8,128)(2,1)S(1)} %convolution_convert_fusion.4), channel_id=1, replica_groups=mesh['grp'=4,'row'=8] {'grp'}, dimensions={0}, use_global_device_ids=true | all-gather | bytes 491520 | tf_op jit(solution)/shard_map/all_gather | solution.py:131
  589.4 7.0 all_gather.6
  598.5 2.1 copy.270
  601.0 2.1 copy.271
  603.1 3.5 copy.272
  606.6 2.9 fusion.100
  611.1 2.0 fusion.38
  613.1 3.9 copy.278
  617.0 7.5 copy.258
  624.5 4.4 copy.254
  628.9 3.8 all-to-all-start.5
  632.8 14.9 %pad_maximum_fusion = bf16[12,6,8,128,128]{4,3,2,1,0:T(8,128)(2,1)} fusion(bf16[8,6,8,128,128]{4,3,2,1,0:T(8,128)(2,1)} %bitcast.15, bf16[4,6,8,128,128]{4,3,2,1,0:T(8,128)(2,1)} %copy.254), kind=kLoop, calls=%fused_computation.28 | loop fusion | flops 9437184 | bytes 37748736 | tf_op jit(solution)/shard_map/concatenate | solution.py:102
  647.7 20.3 %gather_fusion.2 = bf16[24,6,8,128,128]{4,3,2,1,0:T(8,128)(2,1)} fusion(bf16[12,6,8,128,128]{4,3,2,1,0:T(8,128)(2,1)} %pad_maximum_fusion, s32[1024]{0:T(1024)S(1)} %pad_clamp_fusion), kind=kCustom, calls=%fused_computation.4 | custom fusion | bytes 75497568 | tf_op jit(solution)/shard_map/vmap(jit(_take))/gather | solution.py:109
  667.9 41.9 %fusion.9 = bf16[4,6,6,8,128,128]{5,2,4,3,1,0:T(8,128)(2,1)} fusion(bf16[4,6,6,8,128,128]{5,4,3,2,1,0:T(8,128)(2,1)} %bitcast.163, pred[4,6]{1,0:T(4,128)(4,1)S(1)} %get-tuple-element.6, s32[4,6,6]{2,1,0:T(8,128)S(1)} %copy.247, s32[4,6]{1,0:T(4,128)S(1)} %get-tuple-element.9), kind=kOutput, calls=%fused_computation.19 | convolution fusion | flops 264242016 | bytes 75498168 | tf_op jit(solution)/shard_map/vmap(stu,sudjk->stdjk)/dot_general | solution.py:112
  709.9 23.9 %fusion.25 = bf16[4,6,8,128,128]{3,4,1,2,0:T(8,128)(2,1)} fusion(bf16[4,6,8,128,128,1]{4,3,1,5,2,0:T(8,128)(2,1)} %bitcast.167, bf16[4,6,6,8,128,128]{5,2,4,3,1,0:T(8,128)(2,1)} %fusion.9), kind=kOutput, calls=%fused_computation.46 | convolution fusion | flops 4834983936 | bytes 50331648 | tf_op jit(solution)/shard_map/vmap(tdik,stdjk->sdij)/dot_general | solution.py:115
  733.7 9.0 copy.260
  742.8 6.0 all-to-all-start.3
  749.1 2.6 fusion.61
  753.1 152.6 %reduce-scatter.2.cloned.1.call-done = bf16[64,768]{1,0:T(8,128)(2,1)} async-done(((bf16[512,768]{1,0:T(8,128)(2,1)}), bf16[64,768]{1,0:T(8,128)(2,1)}) %reduce-scatter.2.cloned.1.call-update) | async-done | bytes 98320 | tf_op jit(solution)/shard_map/reduce_scatter | solution.py:179
  907.6 1.6 copy.280
  909.3 10.1 fusion.101
  919.4 24.8 %copy.281 = f32[4,6,16,128,128]{4,3,2,1,0:T(8,128)} copy(f32[4,6,16,128,128]{3,4,2,1,0:T(8,128)} %get-tuple-element.23) | data formatting | bytes 50331648 | tf_op jit(solution)/shard_map/rshij,ch->rsijc/dot_general | solution.py:196
  944.2 25.1 %fusion.10 = f32[4,6,16,128]{3,2,1,0:T(8,128)S(1)} fusion(f32[4,6,16,128,128]{4,3,2,1,0:T(8,128)} %copy.281, bf16[4,6,16,128,128]{4,3,2,1,0:T(8,128)(2,1)} %param.17, f32[4,6,16,128]{3,2,1,0:T(8,128)S(1)} %copy-done.11, f32[4,6,16,128]{3,2,1,0:T(8,128)S(1)} %copy-done.8), kind=kLoop, calls=%fused_computation.20 | loop fusion | flops 31408128 | bytes 38338560 | tf_op jit(solution)/shard_map/reduce_sum | solution.py:200
  969.4 32.8 %fusion.13 = bf16[4,6,16,128,128]{4,3,2,1,0:T(8,128)(2,1)} fusion(bf16[4,6,16,128,128]{4,3,2,1,0:T(8,128)(2,1)} %param.17, f32[4,6,16,128,128]{4,3,2,1,0:T(8,128)S(1)} %copy-done.4, f32[4,6,16,128]{3,2,1,0:T(8,128)S(1)} %broadcast_multiply_fusion.1, f32[4,6,16,128]{3,2,1,0:T(8,128)S(1)} %broadcast_multiply_fusion.2, f32[4,6,16,128]{3,2,1,0:T(8,128)S(1)} %copy-done.11, ...), kind=kLoop, calls=%fused_computation.23 | loop fusion | flops 50331648 | bytes 51118080 | tf_op jit(solution)/shard_map/convert_element_type | solution.py:201
  1002.2 13.6 %fusion.99 = (bf16[4,6,8,128,128]{4,3,2,1,0:T(8,128)(2,1)}, f32[4,6,8,8,16,128]{5,4,2,3,1,0:T(8,128)}) fusion(bf16[4,6,8,128,128]{4,2,1,0,3:T(8,128)(2,1)} %all-to-all-done.3), kind=kLoop, calls=%fused_computation.155 | loop fusion | flops 3145728 | bytes 25165824 | tf_op jit(solution)/shard_map/all_to_all | solution.py:188
  1015.8 11.1 %copy.262 = f32[4,6,8,8,16,128]{5,4,3,2,1,0:T(8,128)} copy(f32[4,6,8,8,16,128]{5,4,2,3,1,0:T(8,128)} %get-tuple-element.15) | data formatting | bytes 25165824 | tf_op jit(solution)/shard_map/convert_element_type | solution.py:191
  1026.8 3.9 fusion.26
  1030.8 4.5 multiply_reduce_fusion
  1035.4 9.1 multiply_convert_fusion
  1044.5 12.0 %fusion.27 = f32[4,6,16,128,128]{4,3,2,1,0:T(8,128)} fusion(bf16[4,6,64,16,128]{4,3,2,1,0:T(8,128)(2,1)} %multiply_convert_fusion, bf16[64,128]{1,0:T(8,128)(2,1)S(1)} %copy-done.19), kind=kOutput, calls=%fused_computation.48 | convolution fusion | flops 805306368 | bytes 31473664 | tf_op jit(solution)/shard_map/rsxij,xc->rsijc/dot_general | solution.py:192
  1056.5 22.5 %fusion.15 = bf16[4,6,16,128,128]{4,3,2,1,0:T(8,128)(2,1)} fusion(bf16[4,6,16,128,128]{4,3,2,1,0:T(8,128)(2,1)} %param.17, f32[4,6,16,128,128]{4,3,2,1,0:T(8,128)} %fusion.27, f32[4,6,16,128]{3,2,1,0:T(8,128)S(1)} %copy-done.11, f32[4,6,16,128]{3,2,1,0:T(8,128)S(1)} %copy-done.8, bf16[128,128]{1,0:T(8,128)(2,1)S(1)} %copy-done.24), kind=kOutput, calls=%fused_computation.25 | convolution fusion | flops 1692401664 | bytes 50757632 | tf_op jit(solution)/shard_map/rsijc,cy->rsijy/dot_general | solution.py:67
  (128 shorter events, 16.0 us)
Async XLA Ops:
  7.2 590.5 %copy-start = (bf16[512,768]{1,0:T(8,128)(2,1)S(1)}, bf16[512,768]{1,0:T(8,128)(2,1)}, u32[]{:S(2)}) copy-start(bf16[512,768]{1,0:T(8,128)(2,1)} %param.23) | copy-start | bytes 2359300
  7.2 9.1 copy-start.3
  7.2 24.0 %copy-start.22 = (bf16[128,16]{0,1:T(8,128)(2,1)S(1)}, bf16[128,16]{0,1:T(8,128)(2,1)}, u32[]{:S(2)}) copy-start(bf16[128,16]{0,1:T(8,128)(2,1)} %param.27) | copy-start | bytes 12292
  16.3 42.8 %copy-start.7 = (f32[4,6,16,128]{3,2,1,0:T(8,128)}, f32[4,6,16,128]{3,2,1,0:T(8,128)S(1)}, u32[]{:S(2)}) copy-start(f32[4,6,16,128]{3,2,1,0:T(8,128)S(1)} %broadcast_multiply_fusion.3) | copy-start | bytes 589828
  31.2 28.0 %copy-start.10 = (f32[4,6,16,128]{3,2,1,0:T(8,128)}, f32[4,6,16,128]{3,2,1,0:T(8,128)S(1)}, u32[]{:S(2)}) copy-start(f32[4,6,16,128]{3,2,1,0:T(8,128)S(1)} %add_rsqrt_fusion.1) | copy-start | bytes 589828
  31.2 28.0 %copy-start.18 = (bf16[128,256]{1,0:T(8,128)(2,1)S(1)}, bf16[128,256]{1,0:T(8,128)(2,1)}, u32[]{:S(2)}) copy-start(bf16[128,256]{1,0:T(8,128)(2,1)} %param.24) | copy-start | bytes 196612
  51.8 103.1 %all-to-all-start.4 = ((bf16[4,6,16,16,128]{4,3,1,0,2:T(8,128)(2,1)}), bf16[4,6,16,16,128]{4,3,1,0,2:T(8,128)(2,1)S(1)}, u32[]{:S(2)}, u32[]{:S(2)}) async-start(bf16[4,6,16,16,128]{4,3,1,0,2:T(8,128)(2,1)} %copy.269), calls=%async_computation.4 | async-start | bytes 3145728 | tf_op jit(solution)/shard_map/all_to_all | solution.py:75
  154.9 13.3 %copy-start.9 = (bf16[4,6,16,16,128]{4,3,1,0,2:T(8,128)(2,1)}, bf16[4,6,16,16,128]{4,3,1,0,2:T(8,128)(2,1)S(1)}, u32[]{:S(2)}) copy-start(bf16[4,6,16,16,128]{4,3,1,0,2:T(8,128)(2,1)S(1)} %all-to-all-done.4) | copy-start | bytes 4718596
  154.9 143.7 %all-to-all-start = ((bf16[4,6,64,16,128]{4,3,1,0,2:T(8,128)(2,1)}), bf16[4,6,64,16,128]{4,3,1,0,2:T(8,128)(2,1)}, u32[]{:S(2)}, u32[]{:S(2)}) async-start(bf16[4,6,64,16,128]{4,3,1,0,2:T(8,128)(2,1)} %copy.250), calls=%async_computation | async-start | bytes 12582912 | tf_op jit(solution)/shard_map/all_to_all | solution.py:74
  160.9 142.7 %copy-start.20 = (s32[16,6]{0,1:T(8,128)S(1)}, s32[16,6]{0,1:T(8,128)}, u32[]{:S(2)}) copy-start(s32[16,6]{0,1:T(8,128)} %param.18) | copy-start | bytes 1156
  298.6 142.2 %all-to-all-start.2 = ((bf16[4,6,64,16,128]{4,3,1,0,2:T(8,128)(2,1)}), bf16[4,6,64,16,128]{4,3,1,0,2:T(8,128)(2,1)}, u32[]{:S(2)}, u32[]{:S(2)}) async-start(bf16[4,6,64,16,128]{4,3,1,0,2:T(8,128)(2,1)} %copy.256), calls=%async_computation.2 | async-start | bytes 12582912 | tf_op jit(solution)/shard_map/all_to_all | solution.py:73
  328.5 118.9 %copy-start.2 = (s32[16]{0:T(128)S(1)}, s32[16]{0:T(128)}, u32[]{:S(2)}) copy-start(s32[16]{0:T(128)} %param.20) | copy-start | bytes 196
  328.5 121.1 %copy-start.21 = (s32[16,6]{0,1:T(8,128)S(1)}, s32[16,6]{0,1:T(8,128)}, u32[]{:S(2)}) copy-start(s32[16,6]{0,1:T(8,128)} %param.19) | copy-start | bytes 1156
  328.5 121.8 %copy-start.6 = (bf16[512,768]{1,0:T(8,128)(2,1)S(1)}, bf16[512,768]{1,0:T(8,128)(2,1)}, u32[]{:S(2)}) copy-start(bf16[512,768]{1,0:T(8,128)(2,1)} %param.22) | copy-start | bytes 2359300
  328.5 122.6 %copy-start.15 = (bf16[768,96]{0,1:T(8,128)(2,1)S(1)}, bf16[768,96]{0,1:T(8,128)(2,1)}, u32[]{:S(2)}) copy-start(bf16[768,96]{0,1:T(8,128)(2,1)} %param.29) | copy-start | bytes 442372
  440.9 188.1 %all-to-all-start.1 = ((bf16[4,2,6,8,128,128]{5,4,3,2,1,0:T(8,128)(2,1)}), bf16[4,2,6,8,128,128]{5,4,3,2,1,0:T(8,128)(2,1)}, u32[]{:S(2)}, u32[]{:S(2)}) async-start(bf16[4,2,6,8,128,128]{5,4,3,2,1,0:T(8,128)(2,1)} %copy.253), calls=%async_computation.1 | async-start | bytes 25165824 | tf_op jit(solution)/shard_map/all_to_all | solution.py:100
  447.2 141.8 %copy-start.16 = (bf16[768,96]{0,1:T(8,128)(2,1)S(1)}, bf16[768,96]{0,1:T(8,128)(2,1)}, u32[]{:S(2)}) copy-start(bf16[768,96]{0,1:T(8,128)(2,1)} %param.30) | copy-start | bytes 442372
  447.2 150.0 %copy-start.17 = (bf16[768,96]{0,1:T(8,128)(2,1)S(1)}, bf16[768,96]{0,1:T(8,128)(2,1)}, u32[]{:S(2)}) copy-start(bf16[768,96]{0,1:T(8,128)(2,1)} %param.28) | copy-start | bytes 442372
  447.2 150.5 %copy-start.14 = (bf16[96,768]{1,0:T(8,128)(2,1)S(1)}, bf16[96,768]{1,0:T(8,128)(2,1)}, u32[]{:S(2)}) copy-start(bf16[96,768]{1,0:T(8,128)(2,1)} %param.31) | copy-start | bytes 442372
  447.3 150.9 %copy-start.25 = (f32[16]{0:T(128)S(1)}, f32[16]{0:T(128)}, u32[]{:S(2)}) copy-start(f32[16]{0:T(128)} %param.21) | copy-start | bytes 196
  598.5 11.5 %copy-start.12 = (bf16[4,6,128,2,48]{2,4,3,1,0:T(8,128)(2,1)}, bf16[4,6,128,2,48]{2,4,3,1,0:T(8,128)(2,1)S(1)}, u32[]{:S(2)}) copy-start(bf16[4,6,128,2,48]{2,4,3,1,0:T(8,128)(2,1)S(1)} %get-tuple-element.17) | copy-start | bytes 1769476
  609.5 1.6 copy-start.5
  610.9 13.6 %slice-start = ((s8[6291456]{0:T(1024)(128)(4,1)}), s8[2097152]{0:T(1024)(128)(4,1)S(1)}, s32[]{:S(2)}) async-start(s8[6291456]{0:T(1024)(128)(4,1)} %bitcast.157), calls=%async_computation.8 | async-start | bytes 4194304
  617.0 7.5 slice-start.1
  628.9 113.8 %all-to-all-start.5 = ((bf16[4,6,2,128,128]{4,0,2,1,3:T(4,128)(2,1)}), bf16[4,6,2,128,128]{4,0,2,1,3:T(4,128)(2,1)S(1)}, u32[]{:S(2)}, u32[]{:S(2)}) async-start(bf16[4,6,2,128,128]{4,0,2,1,3:T(4,128)(2,1)} %copy.278), calls=%async_computation.6 | async-start | bytes 3145728 | tf_op jit(solution)/shard_map/all_to_all | solution.py:189
  733.7 15.3 %copy-start.13 = (bf16[4,6,128,2,48]{2,4,3,1,0:T(8,128)(2,1)S(1)}, bf16[4,6,128,2,48]{2,4,3,1,0:T(8,128)(2,1)}, u32[]{:S(2)}) copy-start(bf16[4,6,128,2,48]{2,4,3,1,0:T(8,128)(2,1)} %copy-done.12) | copy-start | bytes 1769476
  742.8 259.4 %all-to-all-start.3 = ((bf16[4,6,8,128,128]{4,2,1,0,3:T(8,128)(2,1)}), bf16[4,6,8,128,128]{4,2,1,0,3:T(8,128)(2,1)}, u32[]{:S(2)}, u32[]{:S(2)}) async-start(bf16[4,6,8,128,128]{4,2,1,0,3:T(8,128)(2,1)} %copy.260), calls=%async_computation.3 | async-start | bytes 12582912 | tf_op jit(solution)/shard_map/all_to_all | solution.py:188
  748.8 160.5 %copy-start.23 = (bf16[128,16]{0,1:T(8,128)(2,1)S(1)}, bf16[128,16]{0,1:T(8,128)(2,1)}, u32[]{:S(2)}) copy-start(bf16[128,16]{0,1:T(8,128)(2,1)} %param.27) | copy-start | bytes 12292
  748.8 156.8 %reduce-scatter.2.cloned.1.call-start = ((), (), s32[]{:S(2)}) async-start(), calls=%async_computation.7 | async-start | bytes 884736 | tf_op jit(solution)/shard_map/reduce_scatter | solution.py:179
  919.4 24.8 %copy-start.8 = (f32[4,6,16,128]{3,2,1,0:T(8,128)S(1)}, f32[4,6,16,128]{3,2,1,0:T(8,128)}, u32[]{:S(2)}) copy-start(f32[4,6,16,128]{3,2,1,0:T(8,128)} %copy-done.7) | copy-start | bytes 589828
  919.4 24.8 %copy-start.11 = (f32[4,6,16,128]{3,2,1,0:T(8,128)S(1)}, f32[4,6,16,128]{3,2,1,0:T(8,128)}, u32[]{:S(2)}) copy-start(f32[4,6,16,128]{3,2,1,0:T(8,128)} %copy-done.10) | copy-start | bytes 589828
  944.2 25.2 %copy-start.4 = (f32[4,6,16,128,128]{4,3,2,1,0:T(8,128)S(1)}, f32[4,6,16,128,128]{4,3,2,1,0:T(8,128)}, u32[]{:S(2)}) copy-start(f32[4,6,16,128,128]{4,3,2,1,0:T(8,128)} %copy.281) | copy-start | bytes 75497472
  1030.8 13.7 %copy-start.19 = (bf16[64,128]{1,0:T(8,128)(2,1)S(1)}, bf16[64,128]{1,0:T(8,128)(2,1)}, u32[]{:S(2)}) copy-start(bf16[64,128]{1,0:T(8,128)(2,1)} %param.26) | copy-start | bytes 49156
  1044.5 12.0 %copy-start.24 = (bf16[128,128]{1,0:T(8,128)(2,1)S(1)}, bf16[128,128]{1,0:T(8,128)(2,1)}, u32[]{:S(2)}) copy-start(bf16[128,128]{1,0:T(8,128)(2,1)} %param.25) | copy-start | bytes 98308
  1056.5 22.5 %copy-start.1 = (bf16[512,768]{1,0:T(8,128)(2,1)S(1)}, bf16[512,768]{1,0:T(8,128)(2,1)}, u32[]{:S(2)}) copy-start(bf16[512,768]{1,0:T(8,128)(2,1)} %param.23) | copy-start | bytes 2359300
Sparse Core Ops, SparseCore 0:
  753.5 152.0 reduce-scatter.1
where the time goes:
time: 1100 us; the launch traced here: 1090 us
  waiting for transfers between devices  395 us (36%)
  local copies, waits for them, and re-layouts  176 us (16%)
  matrix products  166 us (15%)
  other arithmetic  155 us (14%)
  blocking collectives  144 us (13%)
  starting transfers between devices  34.7 us (3%)
  between operations  15.1 us (1%)
    reduce_scatter x1, waiting for transfers between devices, per_device(): lax.psum_scatter(jnp.dot(mixed_nodes, out_weight, preferred_element_type=...  153 us
    all_gather x1, blocking collectives, per_device(): lax.all_gather(keys_here, 'grp', axis=0, tiled=True)  137 us
    all_to_all x1, waiting for transfers between devices, per_device(): lax.all_to_all(right_proj, 'row', split_axis=2, concat_axis=3, tiled=True)  130 us
    all_to_all x1, waiting for transfers between devices, per_device(): lax.all_to_all(left_proj, 'row', split_axis=2, concat_axis=3, tiled=True)  112 us
    dot_general x1, local copies, waits for them, and re-layouts, per_device(): jnp.einsum('rsijc,cx->rsxij', normed_short, tri_weight, preferred_element...  49.7 us
    dot_general x1, matrix products, triangle_row(): jnp.einsum('stu,sudjk->stdjk', matches, far_rows, preferred_element_type=...  41.9 us
    convert_element_type x1, other arithmetic, per_device(): (pair_scale * (centre_grad - normed * projection_mean)).astype(jnp.bfloat16)  32.8 us
    reduce_sum x1, other arithmetic, per_device(): projection_mean = jnp.mean(grad_normed * normed, axis=4, keepdims=True)  25.1 us
  transfers between devices with their start and end apart: 7, of which 3 were waited for; matrix products, arithmetic and copies ran while one was open for 35% of the time, Pallas kernels for 0%

commit v1 on v0

v1 whole, which is shorter than its diff:
```python
import jax
import jax.numpy as jnp
from jax import lax
from jax.experimental import pallas as pl
from jax.experimental.pallas import tpu as pltpu
from jax.sharding import PartitionSpec as P

CAPX = 2
LEAD = 1
EPS = 1e-05
F32 = jnp.float32
BF16 = jnp.bfloat16
VMEM_BYTES = 56 * 1024 * 1024


def norm_parts(values, dimension):
    center = jnp.mean(values, axis=dimension, keepdims=True)
    shifted = values - center
    spread = jnp.mean(shifted * shifted, axis=dimension, keepdims=True)
    inverse = lax.rsqrt(spread + EPS)
    return (shifted * inverse, inverse)


def chunk_starts(chunks, dimension):
    spans, start = [], 0
    for chunk in chunks:
        spans.append((start, start + chunk.shape[dimension]))
        start = spans[-1][1]
    return spans


def params():
    return pltpu.CompilerParams(vmem_limit_bytes=VMEM_BYTES)


def project_rows(pair_feats, weights_t, parts, first, count, heads):
    slots, rows, block, channels = pair_feats.shape[1:]
    hidden = (weights_t.shape[0] - heads) // 4
    part = hidden // parts
    step_rows = 2

    def body(x_ref, w_ref, left_ref, right_ref, bias_ref, left_buf, right_buf):
        weights = w_ref[...]
        for start in range(0, rows, step_rows):
            x = x_ref[start : start + step_rows].astype(F32).reshape(step_rows * block, channels)
            normed = norm_parts(x, 1)[0].astype(BF16)
            projected = lax.dot_general(
                weights, normed, (((1,), (1,)), ((), ())), preferred_element_type=F32
            )
            left_half = projected[:hidden]
            left = left_half * jnp.tanh(projected[hidden : 2 * hidden]) + left_half
            right_half = projected[2 * hidden : 3 * hidden]
            right = right_half * jnp.tanh(projected[3 * hidden : 4 * hidden]) + right_half
            bias = projected[4 * hidden :].astype(BF16)
            for inner in range(step_rows):
                lanes = slice(inner * block, (inner + 1) * block)
                place = start + inner
                left_buf[:, place, :] = left[:, lanes]
                right_buf[:, place, :] = right[:, lanes]
                bias_ref[place * heads : (place + 1) * heads, :] = bias[:, lanes]
        shape = (parts, part, rows, block)
        left_ref[...] = left_buf[...].astype(BF16).reshape(shape)
        right_ref[...] = right_buf[...].astype(BF16).reshape(shape)

    shipped = jax.ShapeDtypeStruct((parts, count, slots, part, rows, block), BF16)
    shipped_spec = pl.BlockSpec(
        (parts, None, None, part, rows, block), lambda i, s: (0, i, s, 0, 0, 0)
    )
    return pl.pallas_call(
        body,
        grid=(count, slots),
        in_specs=[
            pl.BlockSpec((None, None, rows, block, channels), lambda i, s: (first + i, s, 0, 0, 0)),
            pl.BlockSpec(weights_t.shape, lambda i, s: (0, 0)),
        ],
        out_specs=[
            shipped_spec,
            shipped_spec,
            pl.BlockSpec((None, None, rows * heads, block), lambda i, s: (i, s, 0, 0)),
        ],
        out_shape=[
            shipped,
            shipped,
            jax.ShapeDtypeStruct((count, slots, rows * heads, block), BF16),
        ],
        scratch_shapes=[pltpu.VMEM((hidden, rows, block), F32)] * 2,
        compiler_params=params(),
        name=f"project_{first}",
    )(pair_feats, weights_t)


def pick_blocks(rights, send_row, send_slot, offsets):
    parts, _, _, part, rows, block = rights[0].shape
    _, cap_rows, cap_slots = send_slot.shape
    starts = chunk_starts(rights, 1)

    def body(row_ref, slot_ref, *refs):
        ins, out_refs = refs[: len(rights)], refs[len(rights) :]
        for offset in range(offsets):
            for a in range(cap_rows):
                which = row_ref[offset, a]
                for chunk, (begin, end) in enumerate(starts):

                    @pl.when((which >= begin) & (which < end))
                    def _(chunk=chunk, begin=begin, a=a, offset=offset, which=which):
                        for b in range(cap_slots):
                            slot = slot_ref[offset, a, b]
                            for d in range(parts):
                                out_refs[offset][a * cap_slots + b, d] = ins[chunk][
                                    d, which - begin, slot
                                ]

    out = jax.ShapeDtypeStruct((cap_rows * cap_slots, parts, part, rows, block), BF16)
    smem = pl.BlockSpec(memory_space=pltpu.SMEM)
    vmem = pl.BlockSpec(memory_space=pltpu.VMEM)
    return pl.pallas_call(
        body,
        in_specs=[smem, smem] + [vmem] * len(rights),
        out_specs=[vmem] * offsets,
        out_shape=[out] * offsets,
        compiler_params=params(),
        name="pick_blocks",
    )(send_row, send_slot, *rights)


def triangle_rows(left, rights, arrived, source, place, first, *earlier):
    far = len(arrived)
    parts, count, slots, part, rows, block = left.shape
    starts = chunk_starts(rights, 1)
    held = BF16 if rows % 16 == 0 else F32

    def body(source_ref, place_ref, left_ref, *refs):
        right_refs, refs = refs[: len(rights)], refs[len(rights) :]
        far_refs, (out_ref, table) = refs[:far], refs[far + len(earlier) :]
        at_row = first + pl.program_id(1)
        for s in range(slots):
            origin = source_ref[at_row, s]

            def fill(get, s=s):
                for t in range(slots):
                    there = slice(t * block, (t + 1) * block)
                    at = place_ref[at_row, s, t]

                    @pl.when(at >= 0)
                    def _():
                        for d in range(parts):
                            begin = s * block + d * rows
                            table[begin : begin + rows, there] = get(d, at).astype(held)

                    @pl.when(at < 0)
                    def _():
                        table[s * block : (s + 1) * block, there] = jnp.zeros((block, block), held)

            for chunk, (begin, end) in enumerate(starts):

                @pl.when((origin >= begin) & (origin < end))
                def _(chunk=chunk, begin=begin):
                    fill(lambda d, at: right_refs[chunk][d, origin - begin, at])

            for number in range(far):

                @pl.when(origin == starts[-1][1] + number)
                def _(number=number):
                    fill(lambda d, at: far_refs[number][at, d])

        near = jnp.concatenate(
            [
                jnp.concatenate([left_ref[d, t].astype(held) for d in range(parts)], axis=0)
                for t in range(slots)
            ],
            axis=1,
        ).astype(BF16)
        sums = lax.dot_general(
            near,
            table[...].astype(BF16),
            (((1,), (1,)), ((), ())),
            preferred_element_type=F32,
        )
        for d in range(parts):
            for s in range(slots):
                piece = sums[d * rows : (d + 1) * rows, s * block : (s + 1) * block]
                out_ref[d, s] = piece.astype(BF16)

    smem = pl.BlockSpec(memory_space=pltpu.SMEM)
    row_spec = pl.BlockSpec(
        (parts, None, slots, None, rows, block), lambda c, i: (0, i, 0, c, 0, 0)
    )
    far_spec = pl.BlockSpec(
        arrived[0].shape[:2] + (None, rows, block), lambda c, i: (0, 0, c, 0, 0)
    )
    return pl.pallas_call(
        body,
        grid=(part, count),
        in_specs=[smem] * 2
        + [row_spec]
        + [
            pl.BlockSpec(right.shape[:3] + (None, rows, block), lambda c, i: (0, 0, 0, c, 0, 0))
            for right in rights
        ]
        + [far_spec] * far
        + [pl.BlockSpec(memory_space=pl.ANY)] * len(earlier),
        out_specs=row_spec,
        out_shape=jax.ShapeDtypeStruct(left.shape, BF16),
        scratch_shapes=[pltpu.VMEM((slots * block, slots * block), held)],
        compiler_params=params(),
        name=f"triangle_{first}",
    )(source, place, left, *rights, *arrived, *earlier)


def attend(queries, cots, keys, values, bias_rows, places, masks, flags, chain_bias):
    block_rows, rows, width = queries.shape
    heads = chain_bias.shape[0]
    _, slots, _, block = bias_rows[0].shape
    chunks = len(bias_rows)
    chunk_of = [
        (chunk, I - begin)
        for chunk, (begin, end) in enumerate(chunk_starts(bias_rows, 0))
        for I in range(begin, end)
    ]
    head_size = width // heads
    score_scale = head_size ** (-0.5)

    def body(place_ref, mask_ref, flag_ref, q_ref, c_ref, k_ref, v_ref, chain_ref, *refs):
        bias_refs, (mixed_ref, grad_ref) = refs[:chunks], refs[chunks:]
        row_head = lax.broadcasted_iota(jnp.int32, (heads, width), 0)
        lane_head = lax.broadcasted_iota(jnp.int32, (heads, width), 1) // head_size
        own_head = (row_head == lane_head).astype(F32)
        chain = jnp.concatenate([chain_ref[...]] * rows, axis=0)
        for I, (chunk, inner) in enumerate(chunk_of):

            def spread(ref):
                wide = ref[I].astype(F32)
                return jnp.concatenate(
                    [
                        (jnp.broadcast_to(wide[i : i + 1], (heads, width)) * own_head).astype(BF16)
                        for i in range(rows)
                    ],
                    axis=0,
                )

            q_wide, c_wide = spread(q_ref), spread(c_ref)
            scores, grads = [], []
            for s in range(slots):
                near = place_ref[I, s]
                score = lax.dot_general(
                    q_wide, k_ref[near], (((1,), (1,)), ((), ())), preferred_element_type=F32
                )
                score = score * score_scale + bias_refs[chunk][inner, s].astype(F32) + chain * flag_ref[I, s]
                scores.append(jnp.where(mask_ref[I, s] > 0, score, -jnp.inf))
                grads.append(
                    lax.dot_general(
                        c_wide, v_ref[near], (((1,), (1,)), ((), ())), preferred_element_type=F32
                    )
                )
            scores = jnp.concatenate(scores, axis=1)
            grads = jnp.concatenate(grads, axis=1)
            exps = jnp.exp(scores - jnp.max(scores, axis=1, keepdims=True))
            probs = exps / jnp.sum(exps, axis=1, keepdims=True)
            low = probs.astype(BF16)
            mixed = jnp.zeros((rows * heads, width), F32)
            for s in range(slots):
                mixed = mixed + jnp.dot(
                    low[:, s * block : (s + 1) * block],
                    v_ref[place_ref[I, s]],
                    preferred_element_type=F32,
                )
            mixed = mixed.reshape(rows, heads, width) * own_head[None]
            mixed_ref[I] = jnp.sum(mixed, axis=1).astype(BF16)
            total = jnp.sum(probs * grads, axis=1, keepdims=True)
            score_grads = (probs * (grads - total)).astype(BF16)
            for s in range(slots):
                grad_ref[I, s] = score_grads[:, s * block : (s + 1) * block]

    smem = pl.BlockSpec(memory_space=pltpu.SMEM)
    vmem = pl.BlockSpec(memory_space=pltpu.VMEM)
    return pl.pallas_call(
        body,
        in_specs=[smem] * 3 + [vmem] * (5 + chunks),
        out_specs=[vmem, vmem],
        out_shape=[
            jax.ShapeDtypeStruct((block_rows, rows, width), BF16),
            jax.ShapeDtypeStruct((block_rows, slots, rows * heads, block), BF16),
        ],
        compiler_params=params(),
        name="attend",
    )(places, masks, flags, queries, cots, keys, values, chain_bias, *bias_rows)


def gradient_rows(pair_feats, grads, bias_rows, gate_half, back_weight, heads, first, earlier):
    count = bias_rows.shape[0]
    slots, rows, block, channels = pair_feats.shape[1:]

    def body(x_ref, g_ref, b_ref, gate_ref, back_ref, *refs):
        out_ref, grad_ref = refs[-2:]
        gate_weight, back = gate_ref[...], back_ref[...]
        for i in range(rows):
            xhat, scale = norm_parts(x_ref[i].astype(F32), 1)
            gate = jnp.dot(xhat.astype(BF16), gate_weight, preferred_element_type=F32)
            out_ref[i] = (0.5 * jnp.tanh(gate) + 0.5).astype(BF16)
            g = g_ref[i * heads : (i + 1) * heads]
            b = b_ref[i * heads : (i + 1) * heads]
            cross = jnp.sum(g.astype(F32) * b.astype(F32), axis=0, keepdims=True) / channels
            cross = jnp.broadcast_to(cross, (heads, block)).astype(BF16)
            both = lax.dot_general(
                jnp.concatenate([g, cross], axis=0),
                back,
                (((0,), (0,)), ((), ())),
                preferred_element_type=F32,
            )
            centred, projection = both[:, :channels], both[:, channels:]
            grad_ref[i] = (scale * (centred - xhat * projection)).astype(BF16)

    big = pl.BlockSpec((None, None, rows, block, channels), lambda i, s: (first + i, s, 0, 0, 0))
    whole = jax.ShapeDtypeStruct(pair_feats.shape, BF16)
    anywhere = pl.BlockSpec(memory_space=pl.ANY)
    return pl.pallas_call(
        body,
        grid=(count, slots),
        in_specs=[
            big,
            pl.BlockSpec((None, None, rows * heads, block), lambda i, s: (first + i, s, 0, 0)),
            pl.BlockSpec((None, None, rows * heads, block), lambda i, s: (i, s, 0, 0)),
            pl.BlockSpec(gate_half.shape, lambda i, s: (0, 0)),
            pl.BlockSpec(back_weight.shape, lambda i, s: (0, 0)),
        ]
        + [anywhere] * len(earlier),
        out_specs=[big, big],
        out_shape=[whole, whole],
        input_output_aliases={5 + n: n for n in range(len(earlier))},
        compiler_params=params(),
        name=f"gradient_{first}",
    )(pair_feats, grads, bias_rows, gate_half, back_weight, *earlier)


def finish_rows(pair_feats, gates, tri, tri_out_weight, first):
    slots, rows, block, channels = pair_feats.shape[1:]
    parts, count, _, part, _, _ = tri.shape
    hidden = parts * part

    def body(x_ref, gate_ref, tri_ref, w_ref, out_ref, buf):
        sums = tri_ref[...].astype(F32).reshape(hidden, rows, block)
        buf[...] = norm_parts(sums, 0)[0]
        weight = w_ref[...]
        for i in range(rows):
            update = lax.dot_general(
                buf[:, i, :].astype(BF16),
                weight,
                (((0,), (0,)), ((), ())),
                preferred_element_type=F32,
            )
            out_ref[i] = (x_ref[i].astype(F32) + gate_ref[i].astype(F32) * update).astype(BF16)

    big = pl.BlockSpec((None, None, rows, block, channels), lambda i, s: (first + i, s, 0, 0, 0))
    return pl.pallas_call(
        body,
        grid=(count, slots),
        in_specs=[
            big,
            big,
            pl.BlockSpec(
                (parts, None, None, part, rows, block), lambda i, s: (0, i, s, 0, 0, 0)
            ),
            pl.BlockSpec(tri_out_weight.shape, lambda i, s: (0, 0)),
        ],
        out_specs=big,
        out_shape=jax.ShapeDtypeStruct(pair_feats.shape, BF16),
        input_output_aliases={1: 0},
        scratch_shapes=[pltpu.VMEM((hidden, rows, block), F32)],
        compiler_params=params(),
        name=f"finish_{first}",
    )(pair_feats, gates, tri, tri_out_weight)


def after(values, *earlier):
    return lax.optimization_barrier((values,) + earlier)[0]


def doubling_steps(axis):
    size = lax.axis_size(axis)
    return [size >> n for n in range(1, size.bit_length())]


def doubled(stacked, axis, steps):
    size = lax.axis_size(axis)
    for step in steps:
        pairs = [(n, n ^ step) for n in range(size)]
        stacked = jnp.concatenate([stacked, lax.ppermute(stacked, axis, pairs)], axis=0)
    return stacked


def doubled_order(axis):
    away = jnp.arange(lax.axis_size(axis), dtype=jnp.int32) ^ lax.axis_index(axis)
    order = jnp.zeros_like(away)
    for number, step in enumerate(doubling_steps(axis)):
        order = order + jnp.where(away & step, 1 << number, 0)
    return order


def make_plan(block_cols, group_index, group_count, block_rows):
    total_rows, slots = block_cols.shape
    offsets = group_count - 1
    cap_slots = slots - block_rows + CAPX
    first_row = group_index * block_rows
    targets = jnp.arange(total_rows, dtype=jnp.int32)
    owner = targets // block_rows
    groups = jnp.arange(group_count, dtype=jnp.int32)
    hits = (block_cols[:, :, None] == targets).astype(jnp.int32)
    union = jnp.max(hits.reshape(group_count, block_rows * slots, total_rows), axis=1)
    named = union * (owner[None, :] != groups[:, None]).astype(jnp.int32)
    by_owner = named.reshape(group_count, group_count, block_rows)
    row_rank = (jnp.cumsum(by_owner, axis=2) - by_owner).reshape(group_count, total_rows)
    useful = jnp.max(union[:, None, None, :] * hits[None], axis=3)
    slot_rank = jnp.cumsum(useful, axis=2) - useful
    to_group = (group_index + 1 + jnp.arange(offsets, dtype=jnp.int32)) % group_count
    locals_ = jnp.arange(block_rows, dtype=jnp.int32)
    named_here = lax.dynamic_slice_in_dim(named, first_row, block_rows, 1)[to_group]
    rank_here = lax.dynamic_slice_in_dim(row_rank, first_row, block_rows, 1)[to_group]
    caps = jnp.arange(CAPX, dtype=jnp.int32)
    chosen = named_here[:, None, :] * (rank_here[:, None, :] == caps[None, :, None])
    send_row = jnp.sum(chosen * locals_, axis=2).astype(jnp.int32)
    useful_here = lax.dynamic_slice_in_dim(useful, first_row, block_rows, 1)[to_group]
    srank_here = lax.dynamic_slice_in_dim(slot_rank, first_row, block_rows, 1)[to_group]
    cap_ids = jnp.arange(cap_slots, dtype=jnp.int32)
    slot_ids = jnp.arange(slots, dtype=jnp.int32)
    picks = useful_here[:, :, None, :] * (
        srank_here[:, :, None, :] == cap_ids[None, None, :, None]
    )
    slot_of = jnp.sum(picks * slot_ids, axis=3)
    send_slot = jnp.sum(chosen[:, :, :, None] * slot_of[:, None, :, :], axis=2).astype(jnp.int32)
    my_rank = lax.dynamic_index_in_dim(row_rank, group_index, 0, keepdims=False)
    my_slot_rank = lax.dynamic_index_in_dim(slot_rank, group_index, 0, keepdims=False)
    distance = (group_index - owner) % group_count
    is_local = distance == 0
    row_source = jnp.where(is_local, targets - first_row, block_rows + distance - 1)
    node_place = jnp.where(
        is_local, targets - first_row, block_rows + (distance - 1) * CAPX + my_rank
    )
    own_cols = lax.dynamic_slice_in_dim(block_cols, first_row, block_rows, 0)
    near_cols = block_cols[own_cols]
    match = near_cols[:, :, None, :] == own_cols[:, None, :, None]
    found = jnp.max(match.astype(jnp.int32), axis=3)
    slot_place = jnp.where(
        is_local[:, None], slot_ids[None, :], my_rank[:, None] * cap_slots + my_slot_rank
    )
    place = jnp.sum(match.astype(jnp.int32) * slot_place[own_cols][:, :, None, :], axis=3)
    tri_place = jnp.where(found > 0, place, -1).astype(jnp.int32)
    tri_source = row_source[own_cols].astype(jnp.int32)
    return (send_row, send_slot, own_cols, tri_source, tri_place, node_place.astype(jnp.int32))


def per_device(
    pair_feats,
    block_cols,
    attn_mask,
    chain_of_row,
    same_chain,
    node_feats,
    node_cotangent,
    tri_weight,
    gate_weight,
    tri_out_weight,
    bias_weight,
    query_weight,
    key_weight,
    value_weight,
    out_weight,
):
    parts = lax.axis_size("row")
    group_count = lax.axis_size("grp")
    group_index = lax.axis_index("grp")
    row_index = lax.axis_index("row")
    block_rows, slots, rows, block, channels = pair_feats.shape
    hidden = tri_weight.shape[1] // 4
    heads = bias_weight.shape[1]
    width = node_feats.shape[1]
    offsets = group_count - 1
    first_row = group_index * block_rows
    send_row, send_slot, own_cols, tri_source, tri_place, node_place = make_plan(
        block_cols, group_index, group_count, block_rows
    )
    rings = [
        [(g, (g + d) % group_count) for g in range(group_count)] for d in range(1, group_count)
    ]

    weights_t = jnp.concatenate([tri_weight.T * 0.5, bias_weight.T], axis=0).astype(BF16)
    own_weights = jnp.stack([query_weight.T, key_weight.T, value_weight.T, out_weight])
    share = own_weights.shape[0] * own_weights.shape[1] // group_count
    own_share = lax.dynamic_slice_in_dim(
        own_weights.reshape(-1, width), group_index * share, share, 0
    )
    row_steps = doubling_steps("row")
    near_share = doubled(own_share[None], "row", row_steps[:1])

    def swap(values, *earlier):
        return lax.all_to_all(
            after(values, *earlier), "row", split_axis=0, concat_axis=0, tiled=True
        )

    groups = [(0, LEAD), (LEAD, block_rows - LEAD)]
    left_0, right_0, bias_0 = project_rows(pair_feats, weights_t, parts, *groups[0], heads)
    right_lead = swap(right_0, near_share)
    left_1, right_1, bias_1 = project_rows(pair_feats, weights_t, parts, *groups[1], heads)
    lefts, rights, biases = (left_0, left_1), (right_0, right_1), (bias_0, bias_1)
    half_share = doubled(near_share, "row", row_steps[1:-1])
    right_rest = swap(rights[1], right_lead, half_share)
    row_share = doubled(half_share, "row", row_steps[-1:])
    all_stack = jnp.swapaxes(doubled(row_share[None], "grp", doubling_steps("grp")), 0, 1)
    row_order, grp_order = doubled_order("row"), doubled_order("grp")
    rights = [right_lead, right_rest]
    left_rest = swap(
        lefts[1], right_rest, all_stack, send_row, send_slot, node_place, tri_source, tri_place
    )
    outgoing = pick_blocks(rights, send_row, send_slot, offsets)
    arrived = [lax.ppermute(v, "grp", ring) for v, ring in zip(outgoing, rings)]
    all_stack = after(all_stack, *outgoing)

    all_weights = all_stack[row_order[:, None], grp_order[None, :]].reshape(
        (parts,) + own_weights.shape
    )

    def full(number):
        return all_weights[:, number].reshape(width, width)

    node_norm = norm_parts(node_feats.astype(F32), 1)[0].astype(BF16)
    norm_blocks = node_norm.reshape(block_rows, block, width)
    far_nodes = [
        lax.ppermute(norm_blocks[send_row[d]], "grp", rings[d]) for d in range(offsets)
    ]
    near_nodes = jnp.concatenate([norm_blocks] + far_nodes, axis=0).reshape(-1, width)

    def times_t(values, weight):
        return lax.dot_general(
            values, weight, (((1,), (1,)), ((), ())), preferred_element_type=F32
        ).astype(BF16)

    keys = times_t(near_nodes, full(1)).reshape(-1, block, width)
    values = times_t(near_nodes, full(2)).reshape(-1, block, width)

    def own_rows(array):
        return lax.dynamic_slice_in_dim(
            array.reshape(block_rows, block, width), row_index * rows, rows, 1
        ).reshape(block_rows * rows, width)

    queries = times_t(own_rows(node_norm), full(0)).reshape(block_rows, rows, width)
    cots = times_t(own_rows(node_cotangent), full(3)).reshape(block_rows, rows, width)
    own_chain = lax.dynamic_slice_in_dim(chain_of_row, first_row, block_rows, 0)
    masks = lax.dynamic_slice_in_dim(attn_mask, first_row, block_rows, 0)
    flags = (chain_of_row[own_cols] == own_chain[:, None]).astype(F32)
    chain_bias = jnp.broadcast_to(same_chain[:, None], (heads, block))
    mixed, grads = attend(
        queries, cots, keys, values, biases, node_place[own_cols], masks, flags, chain_bias
    )
    bias_float = bias_weight.astype(F32)
    centred = (bias_float - jnp.mean(bias_float, axis=0, keepdims=True)).T
    zeros = jnp.zeros((heads, channels), F32)
    back_weight = jnp.concatenate(
        [
            jnp.concatenate([centred, zeros], axis=1),
            jnp.concatenate([zeros, zeros + 1.0 / heads], axis=1),
        ],
        axis=0,
    ).astype(BF16)
    gate_half = (gate_weight * 0.5).astype(BF16)
    whole = ()
    for (first, _), bias in zip(groups, biases):
        whole = gradient_rows(
            pair_feats, grads, bias, gate_half, back_weight, heads, first, whole
        )
    pair_out, pair_grad = whole

    left_lead = swap(lefts[0], left_rest, pair_grad, *arrived)
    sums = triangle_rows(left_rest, rights, arrived, tri_source, tri_place, LEAD)
    tri_rest = swap(sums, left_lead)
    near_mixed = after(mixed[None], sums)
    for step in [1 << n for n in range(block_rows.bit_length() - 1)]:
        other = lax.ppermute(near_mixed, "row", [(r, r ^ step) for r in range(parts)])
        swapped = (row_index & step) > 0
        near_mixed = jnp.concatenate(
            [jnp.where(swapped, other, near_mixed), jnp.where(swapped, near_mixed, other)], axis=0
        )
    sharers = parts // block_rows
    sent_mixed = lax.dynamic_index_in_dim(near_mixed, row_index % block_rows, 1, keepdims=False)
    senders = [((r % sharers) * block_rows + r // sharers, r) for r in range(parts)]
    node_rows = block_rows * block // parts
    mixed_own = lax.ppermute(sent_mixed, "row", senders).reshape(node_rows, width)
    sums = triangle_rows(left_lead, rights, arrived, tri_source, tri_place, 0, mixed_own)
    tri_lead = swap(sums, tri_rest)
    own_nodes = lax.dynamic_slice_in_dim(node_feats, row_index * node_rows, node_rows, 0)
    node_out = (
        own_nodes.astype(F32) + jnp.dot(mixed_own, full(3), preferred_element_type=F32)
    ).astype(BF16)
    tri_lead = after(tri_lead, node_out)
    pair_out = finish_rows(pair_feats, pair_out, tri_rest, tri_out_weight, LEAD)
    pair_out = finish_rows(pair_feats, pair_out, tri_lead, tri_out_weight, 0)
    return (pair_out, node_out, pair_grad)


def solution(mesh):
    pair_spec = P("grp", None, "row", None, None)
    in_specs = (
        (pair_spec,)
        + (P(),) * 4
        + (P("grp", None),) * 2
        + (P(),) * 4
        + (P(None, "row"),) * 3
        + (P("row", None),)
    )
    out_specs = (pair_spec, P(("grp", "row"), None), pair_spec)
    return jax.shard_map(
        per_device, mesh=mesh, in_specs=in_specs, out_specs=out_specs, check_vma=False
    )
```

time: 1100 us -> 508 us (0.46); the launches traced: 1090 us -> 506 us
  waiting for transfers between devices: 395 us -> 199 us
  Pallas kernels: 0 us -> 191 us
  matrix products: 166 us -> 9.3 us
  local copies, waits for them, and re-layouts: 176 us -> 24.3 us
  blocking collectives: 144 us -> 0 us
  other arithmetic: 155 us -> 18.7 us
  starting transfers between devices: 34.7 us -> 62.8 us
  between operations: 15.1 us -> 1.07 us
    all_to_all x6, waiting for transfers between devices: 243 us -> 35.4 us  [swap(): lax.all_to_all(after(values, *earlier), 'row', split_axis=0, concat_axis=...]
    pallas_call x0 -> x10, Pallas kernels: none -> 191 us  [the longest x2 50.7 us: triangle_rows(): pl.pallas_call(body, grid=(part, count), in_specs=[smem] * 2 + [row_spec]...]
    ppermute x0 -> x14, waiting for transfers between devices: none -> 163 us  [the longest x2 78.7 us: per_device(): lax.ppermute(near_mixed, 'row', [(r, r ^ step) for r in range(parts)])]
    dot_general x16 -> x5, matrix products: 166 us -> 9.3 us  [the longest x4 8.32 us: times_t(): lax.dot_general(values, weight, (((1,), (1,)), ((), ())), preferred_eleme...]
    reduce_scatter x1 -> x0, waiting for transfers between devices: 153 us -> none  [per_device(): lax.psum_scatter(jnp.dot(mixed_nodes, out_weight, preferred_element_type=...]
    all_gather x2 -> x0, blocking collectives: 144 us -> none  [the longest x1 137 us: per_device(): lax.all_gather(keys_here, 'grp', axis=0, tiled=True)]
    dot_general x2 -> x0, local copies, waits for them, and re-layouts: 74.5 us -> none  [the longest x1 49.7 us: per_device(): jnp.einsum('rsijc,cx->rsxij', normed_short, tri_weight, preferred_element...]
    convert_element_type x8 -> x3, other arithmetic: 66.7 us -> 0.99 us  [the longest x1 0.66 us: per_device(): flags = (chain_of_row[own_cols] == own_chain[:, None]).astype(F32)]
  transfers between devices with their start and end apart: 7 -> 20, of which waited for: 3 -> 12; matrix products, arithmetic and copies ran while one was open for 35% -> 10% of each run, Pallas kernels for 0% -> 36%
where the time goes in v1:
time: 508 us; the launch traced here: 506 us
  waiting for transfers between devices  199 us (39%)
  Pallas kernels  191 us (38%)
  starting transfers between devices  62.8 us (12%)
  local copies, waits for them, and re-layouts  24.3 us (5%)
  other arithmetic  18.7 us (4%)
  matrix products  9.3 us (2%)
    ppermute x2, waiting for transfers between devices, per_device(): lax.ppermute(near_mixed, 'row', [(r, r ^ step) for r in range(parts)])  78.7 us
    ppermute x5, waiting for transfers between devices, doubled(): lax.ppermute(stacked, axis, pairs)  74.9 us
    pallas_call x2, Pallas kernels, triangle_rows(): pl.pallas_call(body, grid=(part, count), in_specs=[smem] * 2 + [row_spec]...  50.7 us
    pallas_call x2, Pallas kernels, gradient_rows(): pl.pallas_call(body, grid=(count, slots), in_specs=[big, pl.BlockSpec((No...  47.5 us
    all_to_all x6, starting transfers between devices, swap(): lax.all_to_all(after(values, *earlier), 'row', split_axis=0, concat_axis=...  44.3 us
    pallas_call x2, Pallas kernels, project_rows(): pl.pallas_call(body, grid=(count, slots), in_specs=[pl.BlockSpec((None, N...  39.1 us
    all_to_all x6, waiting for transfers between devices, swap(): lax.all_to_all(after(values, *earlier), 'row', split_axis=0, concat_axis=...  35.4 us
    pallas_call x2, Pallas kernels, finish_rows(): pl.pallas_call(body, grid=(count, slots), in_specs=[big, big, pl.BlockSpe...  35 us
  transfers between devices with their start and end apart: 20, of which 12 were waited for; matrix products, arithmetic and copies ran while one was open for 10% of the time, Pallas kernels for 36%

profile of v1, /device:TPU:0, one launch (start us, length us, event | category | flops | bytes accessed | tf_op | source)
XLA Modules:
  0.0 505.6 jit_solution(9656505513164088771)
XLA Ops:
  0.7 1.3 pad_maximum_fusion.2
  2.0 4.1 collective-permute-start
  7.0 1.3 pad_maximum_fusion.6.w_ref
  8.4 10.6 %project_0.1 = (bf16[8,1,6,8,16,128]{5,4,3,2,1,0:T(8,128)(2,1)}, bf16[8,1,6,8,16,128]{5,4,3,2,1,0:T(8,128)(2,1)}, bf16[1,6,256,128]{3,2,1,0:T(8,128)(2,1)}) custom-call(bf16[4,6,16,128,128]{4,3,2,1,0:T(8,128)(2,1)} %x_ref.11, bf16[272,128]{1,0:T(8,128)(2,1)} %pad_maximum_fusion.6.w_ref), custom_call_target="tpu_custom_call" | custom-call | tf_op jit(solution)/shard_map/project_0/pallas_call | solution.py:69
  19.0 3.8 all-to-all-start
  22.8 2.0 collective-permute-start.1
  24.9 28.5 %project_1.1 = (bf16[8,3,6,8,16,128]{5,4,3,2,1,0:T(8,128)(2,1)}, bf16[8,3,6,8,16,128]{5,4,3,2,1,0:T(8,128)(2,1)}, bf16[3,6,256,128]{3,2,1,0:T(8,128)(2,1)}) custom-call(bf16[4,6,16,128,128]{4,3,2,1,0:T(8,128)(2,1)} %x_ref.11, bf16[272,128]{1,0:T(8,128)(2,1)} %pad_maximum_fusion.6.w_ref), custom_call_target="tpu_custom_call" | custom-call | tf_op jit(solution)/shard_map/project_1/pallas_call | solution.py:69
  53.3 1.4 collective-permute-done.1
  54.8 4.8 all-to-all-done.refs_0_
  59.6 1.2 copy-done.3
  60.8 4.6 all-to-all-start.1
  65.4 1.9 collective-permute-start.2
  67.3 49.6 %collective-permute-done.2 = bf16[4,96,768]{2,1,0:T(8,128)(2,1)S(1)} collective-permute-done((bf16[4,96,768]{2,1,0:T(8,128)(2,1)S(1)}, bf16[4,96,768]{2,1,0:T(8,128)(2,1)S(1)}, u32[]{:S(2)}, u32[]{:S(2)}) %collective-permute-start.2) | collective-permute-done | bytes 589856 | tf_op jit(solution)/shard_map/ppermute | solution.py:387
  117.0 1.6 collective-permute-start.3
  119.9 23.9 %collective-permute-done.3 = bf16[1,8,96,768]{3,2,1,0:T(8,128)(2,1)S(1)} collective-permute-done((bf16[1,8,96,768]{3,2,1,0:T(8,128)(2,1)S(1)}, bf16[1,8,96,768]{3,2,1,0:T(8,128)(2,1)S(1)}, u32[]{:S(2)}, u32[]{:S(2)}) %collective-permute-start.3) | collective-permute-done | bytes 1179680 | tf_op jit(solution)/shard_map/ppermute | solution.py:387
  143.7 1.6 pad_maximum_fusion
  151.6 1.4 fusion.7
  155.0 3.7 maximum_bitcast_fusion
  158.7 10.5 %all-to-all-done.1.refs_1_ = bf16[8,3,6,8,16,128]{5,4,3,2,1,0:T(8,128)(2,1)} async-done(((bf16[8,3,6,8,16,128]{5,4,3,2,1,0:T(8,128)(2,1)}), bf16[8,3,6,8,16,128]{5,4,3,2,1,0:T(8,128)(2,1)}, u32[]{:S(2)}, u32[]{:S(2)}) %all-to-all-start.1) | async-done | bytes 4718624 | tf_op jit(solution)/shard_map/all_to_all | solution.py:495
  169.1 4.7 all-to-all-start.2
  176.0 1.6 collective-permute-start.6
  177.6 1.3 gather_fusion.9
  178.9 1.4 collective-permute-start.7
  186.1 6.1 %pick_blocks.1 = (bf16[8,8,8,16,128]{4,3,2,1,0:T(8,128)(2,1)}, bf16[8,8,8,16,128]{4,3,2,1,0:T(8,128)(2,1)}, bf16[8,8,8,16,128]{4,3,2,1,0:T(8,128)(2,1)}) custom-call(s32[3,2]{1,0:T(4,128)} %copy-done.14, s32[3,2,4]{2,1,0:T(2,128)} %multiply_reduce_fusion.2.slot_ref, bf16[8,1,6,8,16,128]{5,4,3,2,1,0:T(8,128)(2,1)} %copy-done.3, ...), custom_call_target="tpu_custom_call" | custom-call | tf_op jit(solution)/shard_map/pick_blocks/pallas_call | solution.py:116
  192.7 1.4 collective-permute-start.10
  195.2 2.8 pad_maximum_fusion.1
  197.9 5.4 %gather_fusion.6 = bf16[32,96,768]{2,1,0:T(8,128)(2,1)} fusion(bf16[8,4,96,768]{3,2,0,1:T(8,128)(2,1)} %maximum_bitcast_fusion, s32[32]{0:T(128)S(1)} %reshape.369), kind=kCustom, calls=%fused_computation.6 | custom fusion | bytes 9437440 | tf_op jit(solution)/shard_map/gather | solution.py:517
  203.3 2.7 fusion.33
  206.0 1.1 convolution_convert_fusion.3
  208.3 3.0 convolution_convert_fusion.1
  211.3 3.0 convolution_convert_fusion
  215.0 12.2 %attend.1 = (bf16[4,16,768]{2,1,0:T(8,128)(2,1)}, bf16[4,6,256,128]{3,2,1,0:T(8,128)(2,1)}) custom-call(s32[4,6]{1,0:T(4,128)} %reshape.322.place_ref, s32[4,6]{1,0:T(4,128)} %copy.64.mask_ref, f32[4,6]{1,0:T(4,128)} %compare_convert_fusion.1.flag_ref, bf16[4,16,768]{2,1,0:T(8,128)(2,1)} %bitcast.95, bf16[4,16,768]{2,1,0:T(8,128)(2,1)} %bitcast.96, ...), custom_call_target="tpu_custom_call" | custom-call | tf_op jit(solution)/shard_map/attend/pallas_call | solution.py:276
  227.2 13.0 %gradient_0.1 = (bf16[4,6,16,128,128]{4,3,2,1,0:T(8,128)(2,1)}, bf16[4,6,16,128,128]{4,3,2,1,0:T(8,128)(2,1)}) custom-call(bf16[4,6,16,128,128]{4,3,2,1,0:T(8,128)(2,1)} %x_ref.11, bf16[4,6,256,128]{3,2,1,0:T(8,128)(2,1)} %get-tuple-element.37.g_ref, bf16[1,6,256,128]{3,2,1,0:T(8,128)(2,1)} %get-tuple-element.35.refs_0_.b_ref, ...), custom_call_target="tpu_custom_call" | custom-call | tf_op jit(solution)/shard_map/gradient_0/pallas_call | solution.py:316
  240.2 34.5 %gradient_1.1 = (bf16[4,6,16,128,128]{4,3,2,1,0:T(8,128)(2,1)}, bf16[4,6,16,128,128]{4,3,2,1,0:T(8,128)(2,1)}) custom-call(bf16[4,6,16,128,128]{4,3,2,1,0:T(8,128)(2,1)} %x_ref.11, bf16[4,6,256,128]{3,2,1,0:T(8,128)(2,1)} %get-tuple-element.37.g_ref, ...), custom_call_target="tpu_custom_call", output_to_operand_aliasing={{0}: (5, {}), {1}: (6, {})} | custom-call | tf_op jit(solution)/shard_map/gradient_1/pallas_call | solution.py:316
  274.7 9.5 %collective-permute-done.10.refs_4_ = bf16[8,8,8,16,128]{4,3,2,1,0:T(8,128)(2,1)} collective-permute-done((bf16[8,8,8,16,128]{4,3,2,1,0:T(8,128)(2,1)}, bf16[8,8,8,16,128]{4,3,2,1,0:T(8,128)(2,1)}, u32[]{:S(2)}, u32[]{:S(2)}) %collective-permute-start.10) | collective-permute-done | bytes 2097184 | tf_op jit(solution)/shard_map/ppermute | solution.py:514
  284.3 5.9 %all-to-all-start.3 = ((bf16[8,1,6,8,16,128]{5,4,3,2,1,0:T(8,128)(2,1)}), bf16[8,1,6,8,16,128]{5,4,3,2,1,0:T(8,128)(2,1)}, u32[]{:S(2)}, u32[]{:S(2)}) async-start(bf16[8,1,6,8,16,128]{5,4,3,2,1,0:T(8,128)(2,1)} %get-tuple-element.45), calls=%async_computation.3 | async-start | bytes 3145728 | tf_op jit(solution)/shard_map/all_to_all | solution.py:495
  290.2 37.1 %triangle_1.1 = bf16[8,3,6,8,16,128]{5,4,3,2,1,0:T(8,128)(2,1)} custom-call(s32[4,6]{1,0:T(4,128)} %reshape.400.source_ref, s32[4,6,6]{2,1,0:T(8,128)} %compare_select_fusion.1.place_ref, bf16[8,3,6,8,16,128]{5,4,3,2,1,0:T(8,128)(2,1)} %all-to-all-done.2.left_ref, bf16[8,1,6,8,16,128]{5,4,3,2,1,0:T(8,128)(2,1)} %copy-done.3, ...), custom_call_target="tpu_custom_call" | custom-call | tf_op jit(solution)/shard_map/triangle_1/pallas_call | solution.py:191
  328.3 5.1 %all-to-all-start.4 = ((bf16[8,3,6,8,16,128]{5,4,3,2,1,0:T(8,128)(2,1)}), bf16[8,3,6,8,16,128]{5,4,3,2,1,0:T(8,128)(2,1)}, u32[]{:S(2)}, u32[]{:S(2)}) async-start(bf16[8,3,6,8,16,128]{5,4,3,2,1,0:T(8,128)(2,1)} %triangle_1.1), calls=%async_computation.4 | async-start | bytes 9437184 | tf_op jit(solution)/shard_map/all_to_all | solution.py:495
  333.4 2.0 collective-permute-start.11
  335.4 39.2 %collective-permute-done.11 = bf16[1,4,16,768]{3,2,1,0:T(8,128)(2,1)S(1)} collective-permute-done((bf16[1,4,16,768]{3,2,1,0:T(8,128)(2,1)S(1)}, bf16[1,4,16,768]{3,2,1,0:T(8,128)(2,1)S(1)}, u32[]{:S(2)}, u32[]{:S(2)}) %collective-permute-start.11) | collective-permute-done | bytes 98336 | tf_op jit(solution)/shard_map/ppermute | solution.py:576
  374.7 1.2 collective-permute-start.12
  375.9 39.5 %collective-permute-done.12 = bf16[2,4,16,768]{3,2,1,0:T(8,128)(2,1)S(1)} collective-permute-done((bf16[2,4,16,768]{3,2,1,0:T(8,128)(2,1)S(1)}, bf16[2,4,16,768]{3,2,1,0:T(8,128)(2,1)S(1)}, u32[]{:S(2)}, u32[]{:S(2)}) %collective-permute-start.12) | collective-permute-done | bytes 196640 | tf_op jit(solution)/shard_map/ppermute | solution.py:576
  416.8 13.5 %triangle_0.1 = bf16[8,1,6,8,16,128]{5,4,3,2,1,0:T(8,128)(2,1)} custom-call(s32[4,6]{1,0:T(4,128)} %reshape.400.source_ref, s32[4,6,6]{2,1,0:T(8,128)} %compare_select_fusion.1.place_ref, bf16[8,1,6,8,16,128]{5,4,3,2,1,0:T(8,128)(2,1)} %all-to-all-done.3.left_ref, bf16[8,1,6,8,16,128]{5,4,3,2,1,0:T(8,128)(2,1)} %copy-done.3, ...), custom_call_target="tpu_custom_call" | custom-call | tf_op jit(solution)/shard_map/triangle_0/pallas_call | solution.py:191
  430.3 9.0 %all-to-all-done.4.tri_ref = bf16[8,3,6,8,16,128]{5,4,3,2,1,0:T(8,128)(2,1)} async-done(((bf16[8,3,6,8,16,128]{5,4,3,2,1,0:T(8,128)(2,1)}), bf16[8,3,6,8,16,128]{5,4,3,2,1,0:T(8,128)(2,1)}, u32[]{:S(2)}, u32[]{:S(2)}) %all-to-all-start.4) | async-done | bytes 4718624 | tf_op jit(solution)/shard_map/all_to_all | solution.py:495
  439.3 20.2 %all-to-all-start.5 = ((bf16[8,1,6,8,16,128]{5,4,3,2,1,0:T(8,128)(2,1)}), bf16[8,1,6,8,16,128]{5,4,3,2,1,0:T(8,128)(2,1)}, u32[]{:S(2)}, u32[]{:S(2)}) async-start(bf16[8,1,6,8,16,128]{5,4,3,2,1,0:T(8,128)(2,1)} %triangle_0.1), calls=%async_computation.5 | async-start | bytes 3145728 | tf_op jit(solution)/shard_map/all_to_all | solution.py:495
  460.5 25.3 %finish_1.1.gate_ref = bf16[4,6,16,128,128]{4,3,2,1,0:T(8,128)(2,1)} custom-call(bf16[4,6,16,128,128]{4,3,2,1,0:T(8,128)(2,1)} %x_ref.11, bf16[4,6,16,128,128]{4,3,2,1,0:T(8,128)(2,1)} %get-tuple-element.40.gate_ref, bf16[8,3,6,8,16,128]{5,4,3,2,1,0:T(8,128)(2,1)} %all-to-all-done.4.tri_ref, bf16[64,128]{1,0:T(8,128)(2,1)} %w_ref.3), custom_call_target="tpu_custom_call", output_to_operand_aliasing={{}: (1, {})} | custom-call | tf_op jit(solution)/shard_map/finish_1/pallas_call | solution.py:354
  485.8 10.1 %all-to-all-done.5.tri_ref = bf16[8,1,6,8,16,128]{5,4,3,2,1,0:T(8,128)(2,1)} async-done(((bf16[8,1,6,8,16,128]{5,4,3,2,1,0:T(8,128)(2,1)}), bf16[8,1,6,8,16,128]{5,4,3,2,1,0:T(8,128)(2,1)}, u32[]{:S(2)}, u32[]{:S(2)}) %all-to-all-start.5) | async-done | bytes 1572896 | tf_op jit(solution)/shard_map/all_to_all | solution.py:495
  495.9 9.7 %finish_0.1 = bf16[4,6,16,128,128]{4,3,2,1,0:T(8,128)(2,1)} custom-call(bf16[4,6,16,128,128]{4,3,2,1,0:T(8,128)(2,1)} %x_ref.11, bf16[4,6,16,128,128]{4,3,2,1,0:T(8,128)(2,1)} %finish_1.1.gate_ref, bf16[8,1,6,8,16,128]{5,4,3,2,1,0:T(8,128)(2,1)} %all-to-all-done.5.tri_ref, bf16[64,128]{1,0:T(8,128)(2,1)} %w_ref.3), custom_call_target="tpu_custom_call", output_to_operand_aliasing={{}: (1, {})} | custom-call | tf_op jit(solution)/shard_map/finish_0/pallas_call | solution.py:354
  (140 shorter events, 25.2 us)
Async XLA Ops:
  0.6 184.8 %copy-start = (bf16[512,768]{1,0:T(8,128)(2,1)S(1)}, bf16[512,768]{1,0:T(8,128)(2,1)}, u32[]{:S(2)}) copy-start(bf16[512,768]{1,0:T(8,128)(2,1)} %param.21) | copy-start | bytes 2359300
  2.0 17.0 %collective-permute-start = (bf16[1,96,768]{2,1,0:T(8,128)(2,1)S(1)}, bf16[1,96,768]{2,1,0:T(8,128)(2,1)S(1)}, u32[]{:S(2)}, u32[]{:S(2)}) collective-permute-start(bf16[1,96,768]{2,1,0:T(8,128)(2,1)S(1)} %dynamic-slice_bitcast_fusion), channel_id=1, source_target_pairs={{0,4},{1,5},{2,6},{3,7},{4,0},{5,1},{6,2},{7,3},{8,12},{9,13},{10,... | collective-permute-start | bytes 442376 | tf_op jit(solution)/shard_map/ppermute | solution.py:387
  19.0 40.5 %all-to-all-start = ((bf16[8,1,6,8,16,128]{5,4,3,2,1,0:T(8,128)(2,1)}), bf16[8,1,6,8,16,128]{5,4,3,2,1,0:T(8,128)(2,1)S(1)}, u32[]{:S(2)}, u32[]{:S(2)}) async-start(bf16[8,1,6,8,16,128]{5,4,3,2,1,0:T(8,128)(2,1)} %get-tuple-element.28), calls=%async_computation | async-start | bytes 3145728 | tf_op jit(solution)/shard_map/all_to_all | solution.py:495
  22.8 31.9 %collective-permute-start.1 = (bf16[2,96,768]{2,1,0:T(8,128)(2,1)S(1)}, bf16[2,96,768]{2,1,0:T(8,128)(2,1)S(1)}, u32[]{:S(2)}, u32[]{:S(2)}) collective-permute-start(bf16[2,96,768]{2,1,0:T(8,128)(2,1)S(1)} %pad_maximum_fusion.4), channel_id=1, source_target_pairs={{0,2},{1,3},{2,0},{3,1},{4,6},{5,7},{6,4},{7,5},{8,10},{9,11},{10,... | collective-permute-start | bytes 884744 | tf_op jit(solution)/shard_map/ppermute | solution.py:387
  59.6 1.2 copy-start.3
  60.8 108.4 %all-to-all-start.1 = ((bf16[8,3,6,8,16,128]{5,4,3,2,1,0:T(8,128)(2,1)}), bf16[8,3,6,8,16,128]{5,4,3,2,1,0:T(8,128)(2,1)}, u32[]{:S(2)}, u32[]{:S(2)}) async-start(bf16[8,3,6,8,16,128]{5,4,3,2,1,0:T(8,128)(2,1)} %get-tuple-element.30), calls=%async_computation.1 | async-start | bytes 9437184 | tf_op jit(solution)/shard_map/all_to_all | solution.py:495
  65.4 53.2 %copy-start.12 = (s32[16,6]{0,1:T(8,128)S(1)}, s32[16,6]{0,1:T(8,128)}, u32[]{:S(2)}) copy-start(s32[16,6]{0,1:T(8,128)} %param.16) | copy-start | bytes 1156
  65.4 51.5 %collective-permute-start.2 = (bf16[4,96,768]{2,1,0:T(8,128)(2,1)S(1)}, bf16[4,96,768]{2,1,0:T(8,128)(2,1)S(1)}, u32[]{:S(2)}, u32[]{:S(2)}) collective-permute-start(bf16[4,96,768]{2,1,0:T(8,128)(2,1)S(1)} %pad_maximum_fusion.3), channel_id=1, source_target_pairs={{0,1},{1,0},{2,3},{3,2},{4,5},{5,4},{6,7},{7,6},{8,9},{9,8},{10,11... | collective-permute-start | bytes 1769480 | tf_op jit(solution)/shard_map/ppermute | solution.py:387
  117.0 26.7 %collective-permute-start.3 = (bf16[1,8,96,768]{3,2,1,0:T(8,128)(2,1)S(1)}, bf16[1,8,96,768]{3,2,1,0:T(8,128)(2,1)S(1)}, u32[]{:S(2)}, u32[]{:S(2)}) collective-permute-start(bf16[1,8,96,768]{3,2,1,0:T(8,128)(2,1)S(1)} %maximum_bitcast_fusion.1), channel_id=1, source_target_pairs={{0,16},{8,24},{16,0},{24,8},{1,17},{9,25},{17,1},{25,9},{2,18},{10... | collective-permute-start | bytes 3538952 | tf_op jit(solution)/shard_map/ppermute | solution.py:387
  119.8 26.7 %copy-start.16 = (s32[16,6]{0,1:T(8,128)S(1)}, s32[16,6]{0,1:T(8,128)}, u32[]{:S(2)}) copy-start(s32[16,6]{0,1:T(8,128)} %param.17) | copy-start | bytes 1156
  145.4 9.6 %collective-permute-start.4 = (bf16[2,8,96,768]{3,2,1,0:T(8,128)(2,1)}, bf16[2,8,96,768]{3,2,1,0:T(8,128)(2,1)}, u32[]{:S(2)}, u32[]{:S(2)}) collective-permute-start(bf16[2,8,96,768]{3,2,1,0:T(8,128)(2,1)} %pad_maximum_fusion), channel_id=1, source_target_pairs={{0,8},{8,0},{16,24},{24,16},{1,9},{9,1},{17,25},{25,17},{2,10},{10... | collective-permute-start | bytes 7077896 | tf_op jit(solution)/shard_map/ppermute | solution.py:387
  153.7 20.2 %copy-start.14 = (s32[3,2]{1,0:T(4,128)}, s32[3,2]{1,0:T(4,128)S(1)}, u32[]{:S(2)}) copy-start(s32[3,2]{1,0:T(4,128)S(1)} %get-tuple-element.53.row_ref) | copy-start | bytes 76
  169.1 4.8 copy-start.4
  169.1 115.1 %all-to-all-start.2 = ((bf16[8,3,6,8,16,128]{5,4,3,2,1,0:T(8,128)(2,1)}), bf16[8,3,6,8,16,128]{5,4,3,2,1,0:T(8,128)(2,1)}, u32[]{:S(2)}, u32[]{:S(2)}) async-start(bf16[8,3,6,8,16,128]{5,4,3,2,1,0:T(8,128)(2,1)} %get-tuple-element.42), calls=%async_computation.2 | async-start | bytes 9437184 | tf_op jit(solution)/shard_map/all_to_all | solution.py:495
  174.5 5.9 %copy-start.11 = (bf16[128,16]{0,1:T(8,128)(2,1)S(1)}, bf16[128,16]{0,1:T(8,128)(2,1)}, u32[]{:S(2)}) copy-start(bf16[128,16]{0,1:T(8,128)(2,1)} %param.25) | copy-start | bytes 12292
  174.5 6.1 %copy-start.13 = (bf16[128,128]{1,0:T(8,128)(2,1)S(1)}, bf16[128,128]{1,0:T(8,128)(2,1)}, u32[]{:S(2)}) copy-start(bf16[128,128]{1,0:T(8,128)(2,1)} %param.23) | copy-start | bytes 98308
  174.5 7.4 %copy-start.15 = (bf16[16,256]{1,0:T(8,128)(2,1)S(1)}, bf16[16,256]{1,0:T(8,128)(2,1)}, u32[]{:S(2)}) copy-start(bf16[16,256]{1,0:T(8,128)(2,1)} %constant.150.clone.1) | copy-start | bytes 24580
  174.5 8.0 %copy-start.2 = (s32[16]{0:T(128)S(1)}, s32[16]{0:T(128)}, u32[]{:S(2)}) copy-start(s32[16]{0:T(128)} %param.18) | copy-start | bytes 196
  175.4 17.4 %collective-permute-start.5 = (bf16[2,128,768]{2,1,0:T(8,128)(2,1)S(1)}, bf16[2,128,768]{2,1,0:T(8,128)(2,1)}, u32[]{:S(2)}, u32[]{:S(2)}) collective-permute-start(bf16[2,128,768]{2,1,0:T(8,128)(2,1)S(1)} %gather_fusion.7), channel_id=1, source_target_pairs={{0,8},{8,16},{16,24},{24,0},{1,9},{9,17},{17,25},{25,1},{2,10},{10... | collective-permute-start | bytes 1179656 | tf_op jit(solution)/shard_map/ppermute | solution.py:527
  176.0 18.8 %collective-permute-start.6 = (bf16[2,128,768]{2,1,0:T(8,128)(2,1)S(1)}, bf16[2,128,768]{2,1,0:T(8,128)(2,1)}, u32[]{:S(2)}, u32[]{:S(2)}) collective-permute-start(bf16[2,128,768]{2,1,0:T(8,128)(2,1)S(1)} %gather_fusion.8), channel_id=1, source_target_pairs={{0,16},{8,24},{16,0},{24,8},{1,17},{9,25},{17,1},{25,9},{2,18},{10... | collective-permute-start | bytes 1179656 | tf_op jit(solution)/shard_map/ppermute | solution.py:527
  178.9 16.3 %collective-permute-start.7 = (bf16[2,128,768]{2,1,0:T(8,128)(2,1)}, bf16[2,128,768]{2,1,0:T(8,128)(2,1)}, u32[]{:S(2)}, u32[]{:S(2)}) collective-permute-start(bf16[2,128,768]{2,1,0:T(8,128)(2,1)} %gather_fusion.9), channel_id=1, source_target_pairs={{0,24},{8,0},{16,8},{24,16},{1,25},{9,1},{17,9},{25,17},{2,26},{10... | collective-permute-start | bytes 1179656 | tf_op jit(solution)/shard_map/ppermute | solution.py:527
  192.2 82.6 %collective-permute-start.8 = (bf16[8,8,8,16,128]{4,3,2,1,0:T(8,128)(2,1)}, bf16[8,8,8,16,128]{4,3,2,1,0:T(8,128)(2,1)}, u32[]{:S(2)}, u32[]{:S(2)}) collective-permute-start(bf16[8,8,8,16,128]{4,3,2,1,0:T(8,128)(2,1)} %get-tuple-element.31), channel_id=1, source_target_pairs={{0,8},{8,16},{16,24},{24,0},{1,9},{9,17},{17,25},{25,1},{2,10},{10... | collective-permute-start | bytes 6291464 | tf_op jit(solution)/shard_map/ppermute | solution.py:514
  192.2 82.6 %collective-permute-start.9 = (bf16[8,8,8,16,128]{4,3,2,1,0:T(8,128)(2,1)}, bf16[8,8,8,16,128]{4,3,2,1,0:T(8,128)(2,1)}, u32[]{:S(2)}, u32[]{:S(2)}) collective-permute-start(bf16[8,8,8,16,128]{4,3,2,1,0:T(8,128)(2,1)} %get-tuple-element.32), channel_id=1, source_target_pairs={{0,16},{8,24},{16,0},{24,8},{1,17},{9,25},{17,1},{25,9},{2,18},{10... | collective-permute-start | bytes 6291464 | tf_op jit(solution)/shard_map/ppermute | solution.py:514
  192.7 91.5 %collective-permute-start.10 = (bf16[8,8,8,16,128]{4,3,2,1,0:T(8,128)(2,1)}, bf16[8,8,8,16,128]{4,3,2,1,0:T(8,128)(2,1)}, u32[]{:S(2)}, u32[]{:S(2)}) collective-permute-start(bf16[8,8,8,16,128]{4,3,2,1,0:T(8,128)(2,1)} %get-tuple-element.33), channel_id=1, source_target_pairs={{0,24},{8,0},{16,8},{24,16},{1,25},{9,1},{17,9},{25,17},{2,26},{10... | collective-permute-start | bytes 6291464 | tf_op jit(solution)/shard_map/ppermute | solution.py:514
  203.3 2.7 copy-start.8
  203.3 3.9 copy-start.9
  206.0 2.3 copy-start.5
  211.3 3.0 copy-start.17
  284.3 44.1 %all-to-all-start.3 = ((bf16[8,1,6,8,16,128]{5,4,3,2,1,0:T(8,128)(2,1)}), bf16[8,1,6,8,16,128]{5,4,3,2,1,0:T(8,128)(2,1)}, u32[]{:S(2)}, u32[]{:S(2)}) async-start(bf16[8,1,6,8,16,128]{5,4,3,2,1,0:T(8,128)(2,1)} %get-tuple-element.45), calls=%async_computation.3 | async-start | bytes 3145728 | tf_op jit(solution)/shard_map/all_to_all | solution.py:495
  327.3 6.2 %copy-start.10 = (bf16[4,16,768]{2,1,0:T(8,128)(2,1)S(1)}, bf16[4,16,768]{2,1,0:T(8,128)(2,1)}, u32[]{:S(2)}) copy-start(bf16[4,16,768]{2,1,0:T(8,128)(2,1)} %get-tuple-element.47) | copy-start | bytes 294916
  328.3 111.0 %all-to-all-start.4 = ((bf16[8,3,6,8,16,128]{5,4,3,2,1,0:T(8,128)(2,1)}), bf16[8,3,6,8,16,128]{5,4,3,2,1,0:T(8,128)(2,1)}, u32[]{:S(2)}, u32[]{:S(2)}) async-start(bf16[8,3,6,8,16,128]{5,4,3,2,1,0:T(8,128)(2,1)} %triangle_1.1), calls=%async_computation.4 | async-start | bytes 9437184 | tf_op jit(solution)/shard_map/all_to_all | solution.py:495
  333.4 41.2 %collective-permute-start.11 = (bf16[1,4,16,768]{3,2,1,0:T(8,128)(2,1)S(1)}, bf16[1,4,16,768]{3,2,1,0:T(8,128)(2,1)S(1)}, u32[]{:S(2)}, u32[]{:S(2)}) collective-permute-start(bf16[1,4,16,768]{3,2,1,0:T(8,128)(2,1)S(1)} %bitcast.101), channel_id=1, source_target_pairs={{0,1},{1,0},{2,3},{3,2},{4,5},{5,4},{6,7},{7,6},{8,9},{9,8},{10,11... | collective-permute-start | bytes 294920 | tf_op jit(solution)/shard_map/ppermute | solution.py:576
  374.7 40.7 %collective-permute-start.12 = (bf16[2,4,16,768]{3,2,1,0:T(8,128)(2,1)S(1)}, bf16[2,4,16,768]{3,2,1,0:T(8,128)(2,1)S(1)}, u32[]{:S(2)}, u32[]{:S(2)}) collective-permute-start(bf16[2,4,16,768]{3,2,1,0:T(8,128)(2,1)S(1)} %pad_maximum_fusion.5), channel_id=1, source_target_pairs={{0,2},{1,3},{2,0},{3,1},{4,6},{5,7},{6,4},{7,5},{8,10},{9,11},{10,... | collective-permute-start | bytes 589832 | tf_op jit(solution)/shard_map/ppermute | solution.py:576
  415.4 0.7 collective-permute-start.13
  416.1 0.6 copy-start.6
  430.3 29.2 %copy-start.7 = (bf16[4,16,768]{2,1,0:T(8,128)(2,1)S(1)}, bf16[4,16,768]{2,1,0:T(8,128)(2,1)}, u32[]{:S(2)}) copy-start(bf16[4,16,768]{2,1,0:T(8,128)(2,1)} %copy-done.6) | copy-start | bytes 294916
  439.3 56.6 %all-to-all-start.5 = ((bf16[8,1,6,8,16,128]{5,4,3,2,1,0:T(8,128)(2,1)}), bf16[8,1,6,8,16,128]{5,4,3,2,1,0:T(8,128)(2,1)}, u32[]{:S(2)}, u32[]{:S(2)}) async-start(bf16[8,1,6,8,16,128]{5,4,3,2,1,0:T(8,128)(2,1)} %triangle_0.1), calls=%async_computation.5 | async-start | bytes 3145728 | tf_op jit(solution)/shard_map/all_to_all | solution.py:495
  495.9 9.7 %copy-start.1 = (bf16[512,768]{1,0:T(8,128)(2,1)S(1)}, bf16[512,768]{1,0:T(8,128)(2,1)}, u32[]{:S(2)}) copy-start(bf16[512,768]{1,0:T(8,128)(2,1)} %param.21) | copy-start | bytes 2359300

commit v2 on v1

--- a/solution.py
+++ b/solution.py
@@ -36,10 +36,14 @@
 def project_rows(pair_feats, weights_t, parts, first, count, heads):
     slots, rows, block, channels = pair_feats.shape[1:]
     hidden = (weights_t.shape[0] - heads) // 4
-    part = hidden // parts
+    span = parts // 2
+    near, part = hidden // 2, hidden // 2 // parts
+    near_part = near // span
     step_rows = 2
 
-    def body(x_ref, w_ref, left_ref, right_ref, bias_ref, left_buf, right_buf):
+    def body(
+        x_ref, w_ref, left_near, left_ref, right_near, right_ref, bias_ref, left_buf, right_buf
+    ):
         weights = w_ref[...]
         for start in range(0, rows, step_rows):
             x = x_ref[start : start + step_rows].astype(F32).reshape(step_rows * block, channels)
@@ -58,14 +62,23 @@
                 left_buf[:, place, :] = left[:, lanes]
                 right_buf[:, place, :] = right[:, lanes]
                 bias_ref[place * heads : (place + 1) * heads, :] = bias[:, lanes]
-        shape = (parts, part, rows, block)
-        left_ref[...] = left_buf[...].astype(BF16).reshape(shape)
-        right_ref[...] = right_buf[...].astype(BF16).reshape(shape)
-
-    shipped = jax.ShapeDtypeStruct((parts, count, slots, part, rows, block), BF16)
-    shipped_spec = pl.BlockSpec(
-        (parts, None, None, part, rows, block), lambda i, s: (0, i, s, 0, 0, 0)
-    )
+        shape, near_shape = (parts, part, rows, block), (span, near_part, rows, block)
+        left_near[...] = left_buf[:near].astype(BF16).reshape(near_shape)
+        left_ref[...] = left_buf[near:].astype(BF16).reshape(shape)
+        right_half = right_buf[:near].astype(BF16).reshape(near_shape)
+        right_near[:span] = right_half
+        right_near[span:] = right_half
+        right_ref[...] = right_buf[near:].astype(BF16).reshape(shape)
+
+    shapes = [
+        (devices, count, slots, channels_here, rows, block)
+        for devices, channels_here in (
+            (span, near_part),
+            (parts, part),
+            (parts, near_part),
+            (parts, part),
+        )
+    ]
     return pl.pallas_call(
         body,
         grid=(count, slots),
@@ -74,15 +87,14 @@
             pl.BlockSpec(weights_t.shape, lambda i, s: (0, 0)),
         ],
         out_specs=[
-            shipped_spec,
-            shipped_spec,
-            pl.BlockSpec((None, None, rows * heads, block), lambda i, s: (i, s, 0, 0)),
-        ],
-        out_shape=[
-            shipped,
-            shipped,
-            jax.ShapeDtypeStruct((count, slots, rows * heads, block), BF16),
-        ],
+            pl.BlockSpec(
+                (shape[0], None, None) + shape[3:], lambda i, s: (0, i, s, 0, 0, 0)
+            )
+            for shape in shapes
+        ]
+        + [pl.BlockSpec((None, None, rows * heads, block), lambda i, s: (i, s, 0, 0))],
+        out_shape=[jax.ShapeDtypeStruct(shape, BF16) for shape in shapes]
+        + [jax.ShapeDtypeStruct((count, slots, rows * heads, block), BF16)],
         scratch_shapes=[pltpu.VMEM((hidden, rows, block), F32)] * 2,
         compiler_params=params(),
         name=f"project_{first}",
@@ -123,15 +135,19 @@
     )(send_row, send_slot, *rights)
 
 
-def triangle_rows(left, rights, arrived, source, place, first, *earlier):
-    far = len(arrived)
-    parts, count, slots, part, rows, block = left.shape
+def triangle_rows(lefts, rights, arrived, source, place, first, *earlier):
+    far, mine = len(arrived), len(lefts)
+    parts = rights[0].shape[0]
+    _, count, slots, part, rows, block = lefts[0].shape
+    pieces = [(number, n) for number, left in enumerate(lefts) for n in range(left.shape[0])]
     starts = chunk_starts(rights, 1)
     held = BF16 if rows % 16 == 0 else F32
 
-    def body(source_ref, place_ref, left_ref, *refs):
+    def body(source_ref, place_ref, *refs):
+        left_refs, refs = refs[:mine], refs[mine:]
         right_refs, refs = refs[: len(rights)], refs[len(rights) :]
-        far_refs, (out_ref, table) = refs[:far], refs[far + len(earlier) :]
+        far_refs, refs = refs[:far], refs[far + len(earlier) :]
+        out_refs, table = refs[:mine], refs[mine]
         at_row = first + pl.program_id(1)
         for s in range(slots):
             origin = source_ref[at_row, s]
@@ -165,7 +181,7 @@
 
         near = jnp.concatenate(
             [
-                jnp.concatenate([left_ref[d, t].astype(held) for d in range(parts)], axis=0)
+                jnp.concatenate([left_refs[m][n, t].astype(held) for m, n in pieces], axis=0)
                 for t in range(slots)
             ],
             axis=1,
@@ -176,15 +192,18 @@
             (((1,), (1,)), ((), ())),
             preferred_element_type=F32,
         )
-        for d in range(parts):
+        for d, (m, n) in enumerate(pieces):
             for s in range(slots):
                 piece = sums[d * rows : (d + 1) * rows, s * block : (s + 1) * block]
-                out_ref[d, s] = piece.astype(BF16)
+                out_refs[m][n, s] = piece.astype(BF16)
 
     smem = pl.BlockSpec(memory_space=pltpu.SMEM)
-    row_spec = pl.BlockSpec(
-        (parts, None, slots, None, rows, block), lambda c, i: (0, i, 0, c, 0, 0)
-    )
+    row_specs = [
+        pl.BlockSpec(
+            (left.shape[0], None, slots, None, rows, block), lambda c, i: (0, i, 0, c, 0, 0)
+        )
+        for left in lefts
+    ]
     far_spec = pl.BlockSpec(
         arrived[0].shape[:2] + (None, rows, block), lambda c, i: (0, 0, c, 0, 0)
     )
@@ -192,22 +211,22 @@
         body,
         grid=(part, count),
         in_specs=[smem] * 2
-        + [row_spec]
+        + row_specs
         + [
             pl.BlockSpec(right.shape[:3] + (None, rows, block), lambda c, i: (0, 0, 0, c, 0, 0))
             for right in rights
         ]
         + [far_spec] * far
         + [pl.BlockSpec(memory_space=pl.ANY)] * len(earlier),
-        out_specs=row_spec,
-        out_shape=jax.ShapeDtypeStruct(left.shape, BF16),
+        out_specs=row_specs,
+        out_shape=[jax.ShapeDtypeStruct(left.shape, BF16) for left in lefts],
         scratch_shapes=[pltpu.VMEM((slots * block, slots * block), held)],
         compiler_params=params(),
         name=f"triangle_{first}",
-    )(source, place, left, *rights, *arrived, *earlier)
-
-
-def attend(queries, cots, keys, values, bias_rows, places, masks, flags, chain_bias):
+    )(source, place, *lefts, *rights, *arrived, *earlier)
+
+
+def attend(queries, cots, keys, values, bias_rows, places, masks, flags, chain_bias, *earlier):
     block_rows, rows, width = queries.shape
     heads = chain_bias.shape[0]
     _, slots, _, block = bias_rows[0].shape
@@ -221,7 +240,7 @@
     score_scale = head_size ** (-0.5)
 
     def body(place_ref, mask_ref, flag_ref, q_ref, c_ref, k_ref, v_ref, chain_ref, *refs):
-        bias_refs, (mixed_ref, grad_ref) = refs[:chunks], refs[chunks:]
+        bias_refs, (mixed_ref, grad_ref) = refs[:chunks], refs[-2:]
         row_head = lax.broadcasted_iota(jnp.int32, (heads, width), 0)
         lane_head = lax.broadcasted_iota(jnp.int32, (heads, width), 1) // head_size
         own_head = (row_head == lane_head).astype(F32)
@@ -275,7 +294,9 @@
     vmem = pl.BlockSpec(memory_space=pltpu.VMEM)
     return pl.pallas_call(
         body,
-        in_specs=[smem] * 3 + [vmem] * (5 + chunks),
+        in_specs=[smem] * 3
+        + [vmem] * (5 + chunks)
+        + [pl.BlockSpec(memory_space=pl.ANY)] * len(earlier),
         out_specs=[vmem, vmem],
         out_shape=[
             jax.ShapeDtypeStruct((block_rows, rows, width), BF16),
@@ -283,7 +304,7 @@
         ],
         compiler_params=params(),
         name="attend",
-    )(places, masks, flags, queries, cots, keys, values, chain_bias, *bias_rows)
+    )(places, masks, flags, queries, cots, keys, values, chain_bias, *bias_rows, *earlier)
 
 
 def gradient_rows(pair_feats, grads, bias_rows, gate_half, back_weight, heads, first, earlier):
@@ -332,14 +353,20 @@
     )(pair_feats, grads, bias_rows, gate_half, back_weight, *earlier)
 
 
-def finish_rows(pair_feats, gates, tri, tri_out_weight, first):
+def finish_rows(pair_feats, gates, near_tris, tri, tri_out_weight, place, first):
     slots, rows, block, channels = pair_feats.shape[1:]
     parts, count, _, part, _, _ = tri.shape
-    hidden = parts * part
-
-    def body(x_ref, gate_ref, tri_ref, w_ref, out_ref, buf):
-        sums = tri_ref[...].astype(F32).reshape(hidden, rows, block)
-        buf[...] = norm_parts(sums, 0)[0]
+    span, near_part = len(near_tris), near_tris[0].shape[3]
+    near = span * near_part
+    hidden = near + parts * part
+
+    def body(place_ref, x_ref, gate_ref, *refs):
+        near_refs, (tri_ref, w_ref, out_ref, buf) = refs[:span], refs[span:]
+        for d in range(span):
+            here = pl.ds((place_ref[0] ^ d) * near_part, near_part)
+            buf[here] = near_refs[d][...].astype(F32)
+        buf[near:] = tri_ref[...].astype(F32).reshape(parts * part, rows, block)
+        buf[...] = norm_parts(buf[...], 0)[0]
         weight = w_ref[...]
         for i in range(rows):
             update = lax.dot_general(
@@ -354,9 +381,14 @@
     return pl.pallas_call(
         body,
         grid=(count, slots),
-        in_specs=[
-            big,
-            big,
+        in_specs=[pl.BlockSpec(memory_space=pltpu.SMEM), big, big]
+        + [
+            pl.BlockSpec(
+                (None, None, None, near_part, rows, block), lambda i, s: (0, i, s, 0, 0, 0)
+            )
+        ]
+        * span
+        + [
             pl.BlockSpec(
                 (parts, None, None, part, rows, block), lambda i, s: (0, i, s, 0, 0, 0)
             ),
@@ -364,11 +396,11 @@
         ],
         out_specs=big,
         out_shape=jax.ShapeDtypeStruct(pair_feats.shape, BF16),
-        input_output_aliases={1: 0},
+        input_output_aliases={2: 0},
         scratch_shapes=[pltpu.VMEM((hidden, rows, block), F32)],
         compiler_params=params(),
         name=f"finish_{first}",
-    )(pair_feats, gates, tri, tri_out_weight)
+    )(place, pair_feats, gates, *near_tris, tri, tri_out_weight)
 
 
 def after(values, *earlier):
@@ -497,22 +529,44 @@
         )
 
     groups = [(0, LEAD), (LEAD, block_rows - LEAD)]
-    left_0, right_0, bias_0 = project_rows(pair_feats, weights_t, parts, *groups[0], heads)
-    right_lead = swap(right_0, near_share)
-    left_1, right_1, bias_1 = project_rows(pair_feats, weights_t, parts, *groups[1], heads)
-    lefts, rights, biases = (left_0, left_1), (right_0, right_1), (bias_0, bias_1)
+    left_near_0, left_0, right_near_0, right_0, bias_0 = project_rows(
+        pair_feats, weights_t, parts, *groups[0], heads
+    )
+    right_near_0 = swap(right_near_0, near_share)
+    left_near_1, left_1, right_near_1, right_1, bias_1 = project_rows(
+        pair_feats, weights_t, parts, *groups[1], heads
+    )
+    biases = (bias_0, bias_1)
     half_share = doubled(near_share, "row", row_steps[1:-1])
-    right_rest = swap(rights[1], right_lead, half_share)
+    right_near_1 = swap(right_near_1, right_near_0, half_share)
+    rights_near = [right_near_0, right_near_1]
     row_share = doubled(half_share, "row", row_steps[-1:])
     all_stack = jnp.swapaxes(doubled(row_share[None], "grp", doubling_steps("grp")), 0, 1)
     row_order, grp_order = doubled_order("row"), doubled_order("grp")
-    rights = [right_lead, right_rest]
-    left_rest = swap(
-        lefts[1], right_rest, all_stack, send_row, send_slot, node_place, tri_source, tri_place
-    )
-    outgoing = pick_blocks(rights, send_row, send_slot, offsets)
-    arrived = [lax.ppermute(v, "grp", ring) for v, ring in zip(outgoing, rings)]
-    all_stack = after(all_stack, *outgoing)
+    plan_parts = (send_row, send_slot, node_place, tri_source, tri_place)
+    span = parts // 2
+    half_place = row_index % span
+
+    def pairwise(pieces):
+        return [pieces[0]] + [
+            lax.ppermute(pieces[d], "row", [(r, r ^ d) for r in range(parts)])
+            for d in range(1, span)
+        ]
+
+    def pieces_of(stacked):
+        return [
+            lax.dynamic_slice_in_dim(stacked, half_place ^ d, 1, 0) for d in range(span)
+        ]
+
+    left_near_1 = pairwise(pieces_of(left_near_1))
+    left_near_0 = pairwise(pieces_of(left_near_0))
+    right_all = swap(
+        jnp.concatenate([right_0, right_1], axis=1), right_near_1, all_stack, *plan_parts, *left_near_0, *left_near_1
+    )
+    rights = [right_all]
+    outgoing_near = pick_blocks(rights_near, send_row, send_slot, offsets)
+    arrived_near = [lax.ppermute(v, "grp", ring) for v, ring in zip(outgoing_near, rings)]
+    all_stack = after(all_stack, *outgoing_near)
 
     all_weights = all_stack[row_order[:, None], grp_order[None, :]].reshape(
         (parts,) + own_weights.shape
@@ -548,8 +602,18 @@
     flags = (chain_of_row[own_cols] == own_chain[:, None]).astype(F32)
     chain_bias = jnp.broadcast_to(same_chain[:, None], (heads, block))
     mixed, grads = attend(
-        queries, cots, keys, values, biases, node_place[own_cols], masks, flags, chain_bias
-    )
+        queries,
+        cots,
+        keys,
+        values,
+        biases,
+        node_place[own_cols],
+        masks,
+        flags,
+        chain_bias,
+        arrived_near[0],
+    )
+
     bias_float = bias_weight.astype(F32)
     centred = (bias_float - jnp.mean(bias_float, axis=0, keepdims=True)).T
     zeros = jnp.zeros((heads, channels), F32)
@@ -568,30 +632,43 @@
         )
     pair_out, pair_grad = whole
 
-    left_lead = swap(lefts[0], left_rest, pair_grad, *arrived)
-    sums = triangle_rows(left_rest, rights, arrived, tri_source, tri_place, LEAD)
-    tri_rest = swap(sums, left_lead)
-    near_mixed = after(mixed[None], sums)
+    left_rest = swap(left_1, right_all)
+    outgoing = pick_blocks(rights, send_row, send_slot, offsets)
+    arrived = [lax.ppermute(v, "grp", ring) for v, ring in zip(outgoing, rings)]
+    near_mixed, first_mixed = mixed[None], None
     for step in [1 << n for n in range(block_rows.bit_length() - 1)]:
         other = lax.ppermute(near_mixed, "row", [(r, r ^ step) for r in range(parts)])
         swapped = (row_index & step) > 0
         near_mixed = jnp.concatenate(
             [jnp.where(swapped, other, near_mixed), jnp.where(swapped, near_mixed, other)], axis=0
         )
+        first_mixed = near_mixed if first_mixed is None else first_mixed
+    left_lead = swap(left_0, left_rest, first_mixed, pair_grad, *outgoing)
     sharers = parts // block_rows
     sent_mixed = lax.dynamic_index_in_dim(near_mixed, row_index % block_rows, 1, keepdims=False)
     senders = [((r % sharers) * block_rows + r // sharers, r) for r in range(parts)]
     node_rows = block_rows * block // parts
     mixed_own = lax.ppermute(sent_mixed, "row", senders).reshape(node_rows, width)
-    sums = triangle_rows(left_lead, rights, arrived, tri_source, tri_place, 0, mixed_own)
+    near_args = (rights_near, arrived_near, tri_source, tri_place)
+    args = (rights, arrived, tri_source, tri_place)
+    near_sums_1 = triangle_rows(left_near_1, *near_args, LEAD, pair_grad, *outgoing)
+    near_rest = pairwise(near_sums_1)
+    sums = triangle_rows([left_rest], *args, LEAD, near_sums_1[0])[0]
+    tri_rest = swap(sums, left_lead)
+    near_sums_0 = triangle_rows(left_near_0, *near_args, 0, sums)
+    near_lead = pairwise(near_sums_0)
+    sums = triangle_rows([left_lead], *args, 0, near_sums_0[0], mixed_own)[0]
     tri_lead = swap(sums, tri_rest)
     own_nodes = lax.dynamic_slice_in_dim(node_feats, row_index * node_rows, node_rows, 0)
     node_out = (
         own_nodes.astype(F32) + jnp.dot(mixed_own, full(3), preferred_element_type=F32)
     ).astype(BF16)
     tri_lead = after(tri_lead, node_out)
-    pair_out = finish_rows(pair_feats, pair_out, tri_rest, tri_out_weight, LEAD)
-    pair_out = finish_rows(pair_feats, pair_out, tri_lead, tri_out_weight, 0)
+    place = half_place.reshape(1).astype(jnp.int32)
+    pair_out = finish_rows(
+        pair_feats, pair_out, near_rest, tri_rest, tri_out_weight, place, LEAD
+    )
+    pair_out = finish_rows(pair_feats, pair_out, near_lead, tri_lead, tri_out_weight, place, 0)
     return (pair_out, node_out, pair_grad)
 
 

time: 508 us -> 627 us (1.23); the launches traced: 506 us -> 616 us
  waiting for transfers between devices: 199 us -> 244 us
  Pallas kernels: 191 us -> 221 us
  starting transfers between devices: 62.8 us -> 84.7 us
  local copies, waits for them, and re-layouts: 24.3 us -> 31.3 us
    ppermute x0 -> x15, waiting for transfers between devices: none -> 59.7 us  [the longest x12 38.7 us: pairwise(): lax.ppermute(pieces[d], 'row', [(r, r ^ d) for r in range(parts)])]
    ppermute x2, waiting for transfers between devices: 78.7 us -> 42.5 us  [per_device(): lax.ppermute(near_mixed, 'row', [(r, r ^ step) for r in range(parts)])]
    all_to_all x6 -> x7, waiting for transfers between devices: 35.4 us -> 68 us  [swap(): lax.all_to_all(after(values, *earlier), 'row', split_axis=0, concat_axis=...]
    ppermute x0 -> x15, starting transfers between devices: none -> 28 us  [the longest x12 24.9 us: pairwise(): lax.ppermute(pieces[d], 'row', [(r, r ^ d) for r in range(parts)])]
    pallas_call x5 -> x7, Pallas kernels: 97.9 us -> 124 us  [the longest x4 76.2 us: triangle_rows(): pl.pallas_call(body, grid=(part, count), in_specs=[smem] * 2 + row_specs...]
    ppermute x5, waiting for transfers between devices: 74.9 us -> 66 us  [doubled(): lax.ppermute(stacked, axis, pairs)]
    all_to_all x6 -> x7, starting transfers between devices: 44.3 us -> 36.7 us  [swap(): lax.all_to_all(after(values, *earlier), 'row', split_axis=0, concat_axis=...]
  transfers between devices with their start and end apart: 20 -> 36, of which waited for: 12 -> 14; matrix products, arithmetic and copies ran while one was open for 10% -> 9% of each run, Pallas kernels for 36% -> 34%
where the time goes in v2:
time: 627 us; the launch traced here: 616 us
  waiting for transfers between devices  244 us (39%)
  Pallas kernels  221 us (35%)
  starting transfers between devices  84.7 us (14%)
  local copies, waits for them, and re-layouts  31.3 us (5%)
  other arithmetic  23.7 us (4%)
  matrix products  10.2 us (2%)
    pallas_call x4, Pallas kernels, triangle_rows(): pl.pallas_call(body, grid=(part, count), in_specs=[smem] * 2 + row_specs...  76.2 us
    all_to_all x7, waiting for transfers between devices, swap(): lax.all_to_all(after(values, *earlier), 'row', split_axis=0, concat_axis=...  68 us
    ppermute x5, waiting for transfers between devices, doubled(): lax.ppermute(stacked, axis, pairs)  66 us
    pallas_call x2, Pallas kernels, gradient_rows(): pl.pallas_call(body, grid=(count, slots), in_specs=[big, pl.BlockSpec((No...  47.5 us
    ppermute x2, waiting for transfers between devices, per_device(): lax.ppermute(near_mixed, 'row', [(r, r ^ step) for r in range(parts)])  42.5 us
    pallas_call x2, Pallas kernels, project_rows(): pl.pallas_call(body, grid=(count, slots), in_specs=[pl.BlockSpec((None, N...  39.7 us
    ppermute x12, waiting for transfers between devices, pairwise(): lax.ppermute(pieces[d], 'row', [(r, r ^ d) for r in range(parts)])  38.7 us
    all_to_all x7, starting transfers between devices, swap(): lax.all_to_all(after(values, *earlier), 'row', split_axis=0, concat_axis=...  36.7 us
  transfers between devices with their start and end apart: 36, of which 14 were waited for; matrix products, arithmetic and copies ran while one was open for 9% of the time, Pallas kernels for 34%

profile of v2, /device:TPU:0, one launch (start us, length us, event | category | flops | bytes accessed | tf_op | source)
XLA Modules:
  0.0 616.1 jit_solution(8711027679329838428)
XLA Ops:
  2.0 4.1 collective-permute-start
  8.4 10.9 %project_0.1 = (bf16[4,1,6,8,16,128]{5,4,3,2,1,0:T(8,128)(2,1)}, bf16[8,1,6,4,16,128]{5,4,3,2,1,0:T(8,128)(2,1)}, bf16[8,1,6,8,16,128]{5,4,3,2,1,0:T(8,128)(2,1)...) custom-call(bf16[4,6,16,128,128]{4,3,2,1,0:T(8,128)(2,1)} %x_ref.11, ...), custom_call_target="tpu_custom_call" | custom-call | tf_op jit(solution)/shard_map/project_0/pallas_call | solution.py:82
  19.3 3.8 all-to-all-start
  23.1 2.0 collective-permute-start.1
  25.1 28.8 %project_1.1 = (bf16[4,3,6,8,16,128]{5,4,3,2,1,0:T(8,128)(2,1)}, bf16[8,3,6,4,16,128]{5,4,3,2,1,0:T(8,128)(2,1)}, bf16[8,3,6,8,16,128]{5,4,3,2,1,0:T(8,128)(2,1)...) custom-call(bf16[4,6,16,128,128]{4,3,2,1,0:T(8,128)(2,1)} %x_ref.11, ...), custom_call_target="tpu_custom_call" | custom-call | tf_op jit(solution)/shard_map/project_1/pallas_call | solution.py:82
  55.0 4.8 all-to-all-done.refs_0_.refs_4_
  61.0 4.6 all-to-all-start.1
  67.5 49.6 %collective-permute-done.2 = bf16[4,96,768]{2,1,0:T(8,128)(2,1)} collective-permute-done((bf16[4,96,768]{2,1,0:T(8,128)(2,1)S(1)}, bf16[4,96,768]{2,1,0:T(8,128)(2,1)}, u32[]{:S(2)}, u32[]{:S(2)}) %collective-permute-start.2) | collective-permute-done | bytes 589856 | tf_op jit(solution)/shard_map/ppermute | solution.py:419
  121.7 3.8 collective-permute-start.11
  126.5 2.0 collective-permute-start.14
  129.6 15.4 %collective-permute-done.3 = bf16[1,8,96,768]{3,2,1,0:T(8,128)(2,1)S(1)} collective-permute-done((bf16[1,8,96,768]{3,2,1,0:T(8,128)(2,1)S(1)}, bf16[1,8,96,768]{3,2,1,0:T(8,128)(2,1)S(1)}, u32[]{:S(2)}, u32[]{:S(2)}) %collective-permute-start.3) | collective-permute-done | bytes 1179680 | tf_op jit(solution)/shard_map/ppermute | solution.py:419
  156.4 3.8 pad_maximum_fusion
  160.2 2.0 collective-permute-done.14.refs_1_
  162.2 11.3 %collective-permute-start.15 = (bf16[1,1,6,8,16,128]{5,4,3,2,1,0:T(8,128)(2,1)S(1)}, bf16[1,1,6,8,16,128]{5,4,3,2,1,0:T(8,128)(2,1)S(1)}, u32[]{:S(2)}, u32[]{:S(2)}) collective-permute-start(bf16[1,1,6,8,16,128]{5,4,3,2,1,0:T(8,128)(2,1)S(1)} %copy-done.26), channel_id=1, source_target_pairs={{0,2},{1,3},{2,0},{3,1},{4,6},{5,7},{6,4},{7,5},{8,10},{9,11},{10,... | collective-permute-start | bytes 589832 | tf_op jit(solution)/shard_map/ppermute | solution.py:552
  173.5 3.7 maximum_bitcast_fusion
  177.2 2.0 collective-permute-done.15.refs_2_
  179.9 2.2 collective-permute-done.16.refs_3_
  182.8 4.9 all-to-all-start.2
  194.7 63.2 %all-to-all-done.2.refs_0_.refs_1_ = bf16[8,4,6,4,16,128]{5,4,3,2,1,0:T(8,128)(2,1)} async-done(((bf16[8,4,6,4,16,128]{5,4,3,2,1,0:T(8,128)(2,1)}), bf16[8,4,6,4,16,128]{5,4,3,2,1,0:T(8,128)(2,1)}, u32[]{:S(2)}, u32[]{:S(2)}) %all-to-all-start.2) | async-done | bytes 3145760 | tf_op jit(solution)/shard_map/all_to_all | solution.py:527
  257.9 4.5 all-to-all-start.3
  266.4 6.0 pick_blocks.2
  273.1 2.8 pad_maximum_fusion.2
  279.0 5.4 gather_fusion.6
  284.4 2.8 fusion.34
  288.3 3.0 convolution_convert_fusion
  291.3 3.0 convolution_convert_fusion.1
  295.5 21.0 %collective-permute-done.8.refs_2_.refs_6_ = bf16[8,8,8,16,128]{4,3,2,1,0:T(8,128)(2,1)S(1)} collective-permute-done((bf16[8,8,8,16,128]{4,3,2,1,0:T(8,128)(2,1)}, bf16[8,8,8,16,128]{4,3,2,1,0:T(8,128)(2,1)S(1)}, u32[]{:S(2)}, u32[]{:S(2)}) %collective-permute-start.8) | collective-permute-done | bytes 2097184 | tf_op jit(solution)/shard_map/ppermute | solution.py:568
  317.8 12.3 %attend.1 = (bf16[4,16,768]{2,1,0:T(8,128)(2,1)}, bf16[4,6,256,128]{3,2,1,0:T(8,128)(2,1)}) custom-call(s32[4,6]{1,0:T(4,128)} %reshape.326.place_ref, s32[4,6]{1,0:T(4,128)} %copy.64.mask_ref, f32[4,6]{1,0:T(4,128)} %compare_convert_fusion.1.flag_ref, bf16[4,16,768]{2,1,0:T(8,128)(2,1)} %bitcast.97, bf16[4,16,768]{2,1,0:T(8,128)(2,1)} %bitcast.96, ...), custom_call_target="tpu_custom_call" | custom-call | tf_op jit(solution)/shard_map/attend/pallas_call | solution.py:295
  332.5 12.9 %gradient_0.1 = (bf16[4,6,16,128,128]{4,3,2,1,0:T(8,128)(2,1)}, bf16[4,6,16,128,128]{4,3,2,1,0:T(8,128)(2,1)}) custom-call(bf16[4,6,16,128,128]{4,3,2,1,0:T(8,128)(2,1)} %x_ref.11, bf16[4,6,256,128]{3,2,1,0:T(8,128)(2,1)} %get-tuple-element.52.g_ref, bf16[1,6,256,128]{3,2,1,0:T(8,128)(2,1)} %get-tuple-element.50.refs_0_.b_ref, ...), custom_call_target="tpu_custom_call" | custom-call | tf_op jit(solution)/shard_map/gradient_0/pallas_call | solution.py:337
  345.4 34.5 %gradient_1.1 = (bf16[4,6,16,128,128]{4,3,2,1,0:T(8,128)(2,1)}, bf16[4,6,16,128,128]{4,3,2,1,0:T(8,128)(2,1)}) custom-call(bf16[4,6,16,128,128]{4,3,2,1,0:T(8,128)(2,1)} %x_ref.11, bf16[4,6,256,128]{3,2,1,0:T(8,128)(2,1)} %get-tuple-element.52.g_ref, ...), custom_call_target="tpu_custom_call", output_to_operand_aliasing={{0}: (5, {}), {1}: (6, {})} | custom-call | tf_op jit(solution)/shard_map/gradient_1/pallas_call | solution.py:337
  380.1 3.9 pick_blocks.3
  384.0 4.6 all-to-all-start.4
  391.5 36.4 %triangle_1.2 = (bf16[1,3,6,8,16,128]{5,4,3,2,1,0:T(8,128)(2,1)}, bf16[1,3,6,8,16,128]{5,4,3,2,1,0:T(8,128)(2,1)}, bf16[1,3,6,8,16,128]{5,4,3,2,1,0:T(8,128)(2,1)}, bf16[1,3,6,8,16,128]{5,4,3,2,1,0:T(8,128)(2,1)}) custom-call(s32[4,6]{1,0:T(4,128)} %reshape.404.source_ref, s32[4,6,6]{2,1,0:T(8,128)} %compare_select_fusion.1.place_ref, ...), custom_call_target="tpu_custom_call" | custom-call | tf_op jit(solution)/shard_map/triangle_1/pallas_call | solution.py:210
  427.9 7.9 %collective-permute-done.22.refs_4_ = bf16[8,8,4,16,128]{4,3,2,1,0:T(8,128)(2,1)S(1)} collective-permute-done((bf16[8,8,4,16,128]{4,3,2,1,0:T(8,128)(2,1)}, bf16[8,8,4,16,128]{4,3,2,1,0:T(8,128)(2,1)S(1)}, u32[]{:S(2)}, u32[]{:S(2)}) %collective-permute-start.22) | collective-permute-done | bytes 1048608 | tf_op jit(solution)/shard_map/ppermute | solution.py:637
  436.8 18.8 %triangle_1.3.refs_9_ = bf16[8,3,6,4,16,128]{5,4,3,2,1,0:T(8,128)(2,1)} custom-call(s32[4,6]{1,0:T(4,128)} %reshape.404.source_ref, s32[4,6,6]{2,1,0:T(8,128)} %compare_select_fusion.1.place_ref, bf16[8,3,6,4,16,128]{5,4,3,2,1,0:T(8,128)(2,1)} %all-to-all-done.3.refs_0_, bf16[8,4,6,4,16,128]{5,4,3,2,1,0:T(8,128)(2,1)} %all-to-all-done.2.refs_0_.refs_1_, ...), custom_call_target="tpu_custom_call" | custom-call | tf_op jit(solution)/shard_map/triangle_1/pallas_call | solution.py:210
  456.5 6.0 all-to-all-start.5
  462.4 2.0 collective-permute-start.27
  464.5 42.5 %collective-permute-done.27 = bf16[2,4,16,768]{3,2,1,0:T(8,128)(2,1)S(1)} collective-permute-done((bf16[2,4,16,768]{3,2,1,0:T(8,128)(2,1)S(1)}, bf16[2,4,16,768]{3,2,1,0:T(8,128)(2,1)S(1)}, u32[]{:S(2)}, u32[]{:S(2)}) %collective-permute-start.27) | collective-permute-done | bytes 196640 | tf_op jit(solution)/shard_map/ppermute | solution.py:640
  507.7 13.4 %triangle_0.2 = (bf16[1,1,6,8,16,128]{5,4,3,2,1,0:T(8,128)(2,1)}, bf16[1,1,6,8,16,128]{5,4,3,2,1,0:T(8,128)(2,1)}, bf16[1,1,6,8,16,128]{5,4,3,2,1,0:T(8,128)(2,1)}, bf16[1,1,6,8,16,128]{5,4,3,2,1,0:T(8,128)(2,1)}) custom-call(s32[4,6]{1,0:T(4,128)} %reshape.404.source_ref, s32[4,6,6]{2,1,0:T(8,128)} %compare_select_fusion.1.place_ref, ...), custom_call_target="tpu_custom_call" | custom-call | tf_op jit(solution)/shard_map/triangle_0/pallas_call | solution.py:210
  521.7 7.7 %triangle_0.3 = bf16[8,1,6,4,16,128]{5,4,3,2,1,0:T(8,128)(2,1)} custom-call(s32[4,6]{1,0:T(4,128)} %reshape.404.source_ref, s32[4,6,6]{2,1,0:T(8,128)} %compare_select_fusion.1.place_ref, bf16[8,1,6,4,16,128]{5,4,3,2,1,0:T(8,128)(2,1)} %copy-done.13, bf16[8,4,6,4,16,128]{5,4,3,2,1,0:T(8,128)(2,1)} %all-to-all-done.2.refs_0_.refs_1_, ...), custom_call_target="tpu_custom_call" | custom-call | tf_op jit(solution)/shard_map/triangle_0/pallas_call | solution.py:210
  529.4 8.3 %all-to-all-start.6 = ((bf16[8,1,6,4,16,128]{5,4,3,2,1,0:T(8,128)(2,1)}), bf16[8,1,6,4,16,128]{5,4,3,2,1,0:T(8,128)(2,1)S(1)}, u32[]{:S(2)}, u32[]{:S(2)}) async-start(bf16[8,1,6,4,16,128]{5,4,3,2,1,0:T(8,128)(2,1)} %triangle_0.3), calls=%async_computation.6 | async-start | bytes 1572864 | tf_op jit(solution)/shard_map/all_to_all | solution.py:527
  537.6 2.0 collective-permute-start.17
  541.1 2.0 collective-permute-start.24
  544.6 17.9 %collective-permute-done.17.refs_1_ = bf16[1,3,6,8,16,128]{5,4,3,2,1,0:T(8,128)(2,1)S(1)} collective-permute-done((bf16[1,3,6,8,16,128]{5,4,3,2,1,0:T(8,128)(2,1)}, bf16[1,3,6,8,16,128]{5,4,3,2,1,0:T(8,128)(2,1)S(1)}, u32[]{:S(2)}, u32[]{:S(2)}) %collective-permute-start.17) | collective-permute-done | bytes 589856 | tf_op jit(solution)/shard_map/ppermute | solution.py:552
  563.1 1.9 fusion.4
  566.7 12.8 %collective-permute-done.19.refs_3_ = bf16[1,3,6,8,16,128]{5,4,3,2,1,0:T(8,128)(2,1)} collective-permute-done((bf16[1,3,6,8,16,128]{5,4,3,2,1,0:T(8,128)(2,1)}, bf16[1,3,6,8,16,128]{5,4,3,2,1,0:T(8,128)(2,1)}, u32[]{:S(2)}, u32[]{:S(2)}) %collective-permute-start.19) | collective-permute-done | bytes 589856 | tf_op jit(solution)/shard_map/ppermute | solution.py:552
  579.6 25.4 %finish_1.1.gate_ref = bf16[4,6,16,128,128]{4,3,2,1,0:T(8,128)(2,1)} custom-call(s32[1]{0:T(128)} %bitcast.place_ref, bf16[4,6,16,128,128]{4,3,2,1,0:T(8,128)(2,1)} %x_ref.11, bf16[4,6,16,128,128]{4,3,2,1,0:T(8,128)(2,1)} %get-tuple-element.55.gate_ref, ...), custom_call_target="tpu_custom_call", output_to_operand_aliasing={{}: (2, {})} | custom-call | tf_op jit(solution)/shard_map/finish_1/pallas_call | solution.py:381
  606.0 9.7 %finish_0.1 = bf16[4,6,16,128,128]{4,3,2,1,0:T(8,128)(2,1)} custom-call(s32[1]{0:T(128)} %bitcast.place_ref, bf16[4,6,16,128,128]{4,3,2,1,0:T(8,128)(2,1)} %x_ref.11, bf16[4,6,16,128,128]{4,3,2,1,0:T(8,128)(2,1)} %finish_1.1.gate_ref, bf16[1,1,6,8,16,128]{5,4,3,2,1,0:T(8,128)(2,1)} %get-tuple-element.75.refs_5_.refs_0_, ...), custom_call_target="tpu_custom_call", output_to_operand_aliasing={{}: (2, {})} | custom-call | tf_op jit(solution)/shard_map/finish_0/pallas_call | solution.py:381
  (213 shorter events, 60.3 us)
Async XLA Ops:
  0.6 265.8 %copy-start = (bf16[512,768]{1,0:T(8,128)(2,1)S(1)}, bf16[512,768]{1,0:T(8,128)(2,1)}, u32[]{:S(2)}) copy-start(bf16[512,768]{1,0:T(8,128)(2,1)} %param.21) | copy-start | bytes 2359300
  2.0 17.3 %collective-permute-start = (bf16[1,96,768]{2,1,0:T(8,128)(2,1)S(1)}, bf16[1,96,768]{2,1,0:T(8,128)(2,1)S(1)}, u32[]{:S(2)}, u32[]{:S(2)}) collective-permute-start(bf16[1,96,768]{2,1,0:T(8,128)(2,1)S(1)} %dynamic-slice_bitcast_fusion), channel_id=1, source_target_pairs={{0,4},{1,5},{2,6},{3,7},{4,0},{5,1},{6,2},{7,3},{8,12},{9,13},{10,... | collective-permute-start | bytes 442376 | tf_op jit(solution)/shard_map/ppermute | solution.py:419
  19.3 40.5 %all-to-all-start = ((bf16[8,1,6,8,16,128]{5,4,3,2,1,0:T(8,128)(2,1)}), bf16[8,1,6,8,16,128]{5,4,3,2,1,0:T(8,128)(2,1)S(1)}, u32[]{:S(2)}, u32[]{:S(2)}) async-start(bf16[8,1,6,8,16,128]{5,4,3,2,1,0:T(8,128)(2,1)} %get-tuple-element.43), calls=%async_computation | async-start | bytes 3145728 | tf_op jit(solution)/shard_map/all_to_all | solution.py:527
  23.1 31.9 %collective-permute-start.1 = (bf16[2,96,768]{2,1,0:T(8,128)(2,1)S(1)}, bf16[2,96,768]{2,1,0:T(8,128)(2,1)S(1)}, u32[]{:S(2)}, u32[]{:S(2)}) collective-permute-start(bf16[2,96,768]{2,1,0:T(8,128)(2,1)S(1)} %pad_maximum_fusion.5), channel_id=1, source_target_pairs={{0,2},{1,3},{2,0},{3,1},{4,6},{5,7},{6,4},{7,5},{8,10},{9,11},{10,... | collective-permute-start | bytes 884744 | tf_op jit(solution)/shard_map/ppermute | solution.py:419
  61.0 121.8 %all-to-all-start.1 = ((bf16[8,3,6,8,16,128]{5,4,3,2,1,0:T(8,128)(2,1)}), bf16[8,3,6,8,16,128]{5,4,3,2,1,0:T(8,128)(2,1)}, u32[]{:S(2)}, u32[]{:S(2)}) async-start(bf16[8,3,6,8,16,128]{5,4,3,2,1,0:T(8,128)(2,1)} %get-tuple-element.45), calls=%async_computation.1 | async-start | bytes 9437184 | tf_op jit(solution)/shard_map/all_to_all | solution.py:527
  65.6 51.5 %collective-permute-start.2 = (bf16[4,96,768]{2,1,0:T(8,128)(2,1)S(1)}, bf16[4,96,768]{2,1,0:T(8,128)(2,1)}, u32[]{:S(2)}, u32[]{:S(2)}) collective-permute-start(bf16[4,96,768]{2,1,0:T(8,128)(2,1)S(1)} %pad_maximum_fusion.4), channel_id=1, source_target_pairs={{0,1},{1,0},{2,3},{3,2},{4,5},{5,4},{6,7},{7,6},{8,9},{9,8},{10,11... | collective-permute-start | bytes 1769480 | tf_op jit(solution)/shard_map/ppermute | solution.py:419
  67.5 52.4 %copy-start.15 = (bf16[4,3,6,8,16,128]{5,4,3,2,1,0:T(8,128)(2,1)S(1)}, bf16[4,3,6,8,16,128]{5,4,3,2,1,0:T(8,128)(2,1)}, u32[]{:S(2)}) copy-start(bf16[4,3,6,8,16,128]{5,4,3,2,1,0:T(8,128)(2,1)} %get-tuple-element.56) | copy-start | bytes 7077892
  118.3 26.7 %collective-permute-start.3 = (bf16[1,8,96,768]{3,2,1,0:T(8,128)(2,1)S(1)}, bf16[1,8,96,768]{3,2,1,0:T(8,128)(2,1)S(1)}, u32[]{:S(2)}, u32[]{:S(2)}) collective-permute-start(bf16[1,8,96,768]{3,2,1,0:T(8,128)(2,1)S(1)} %maximum_bitcast_fusion.1), channel_id=1, source_target_pairs={{0,16},{8,24},{16,0},{24,8},{1,17},{9,25},{17,1},{25,9},{2,18},{10... | collective-permute-start | bytes 3538952 | tf_op jit(solution)/shard_map/ppermute | solution.py:419
  121.5 61.3 %collective-permute-start.10 = (bf16[1,3,6,8,16,128]{5,4,3,2,1,0:T(8,128)(2,1)}, bf16[1,3,6,8,16,128]{5,4,3,2,1,0:T(8,128)(2,1)}, u32[]{:S(2)}, u32[]{:S(2)}) collective-permute-start(bf16[1,3,6,8,16,128]{5,4,3,2,1,0:T(8,128)(2,1)} %get-tuple-element.94), channel_id=1, source_target_pairs={{0,2},{1,3},{2,0},{3,1},{4,6},{5,7},{6,4},{7,5},{8,10},{9,11},{10,... | collective-permute-start | bytes 1769480 | tf_op jit(solution)/shard_map/ppermute | solution.py:552
  121.7 61.1 %collective-permute-start.11 = (bf16[1,3,6,8,16,128]{5,4,3,2,1,0:T(8,128)(2,1)}, bf16[1,3,6,8,16,128]{5,4,3,2,1,0:T(8,128)(2,1)}, u32[]{:S(2)}, u32[]{:S(2)}) collective-permute-start(bf16[1,3,6,8,16,128]{5,4,3,2,1,0:T(8,128)(2,1)} %get-tuple-element.93), channel_id=1, source_target_pairs={{0,3},{1,2},{2,1},{3,0},{4,7},{5,6},{6,5},{7,4},{8,11},{9,10},{10,... | collective-permute-start | bytes 1769480 | tf_op jit(solution)/shard_map/ppermute | solution.py:552
  125.5 57.2 %collective-permute-start.9 = (bf16[1,3,6,8,16,128]{5,4,3,2,1,0:T(8,128)(2,1)}, bf16[1,3,6,8,16,128]{5,4,3,2,1,0:T(8,128)(2,1)}, u32[]{:S(2)}, u32[]{:S(2)}) collective-permute-start(bf16[1,3,6,8,16,128]{5,4,3,2,1,0:T(8,128)(2,1)} %get-tuple-element.95), channel_id=1, source_target_pairs={{0,1},{1,0},{2,3},{3,2},{4,5},{5,4},{6,7},{7,6},{8,9},{9,8},{10,11... | collective-permute-start | bytes 1769480 | tf_op jit(solution)/shard_map/ppermute | solution.py:552
  126.5 35.8 %collective-permute-start.14 = (bf16[1,1,6,8,16,128]{5,4,3,2,1,0:T(8,128)(2,1)}, bf16[1,1,6,8,16,128]{5,4,3,2,1,0:T(8,128)(2,1)S(1)}, u32[]{:S(2)}, u32[]{:S(2)}) collective-permute-start(bf16[1,1,6,8,16,128]{5,4,3,2,1,0:T(8,128)(2,1)} %get-tuple-element.99), channel_id=1, source_target_pairs={{0,1},{1,0},{2,3},{3,2},{4,5},{5,4},{6,7},{7,6},{8,9},{9,8},{10,11... | collective-permute-start | bytes 589832 | tf_op jit(solution)/shard_map/ppermute | solution.py:552
  146.6 26.9 %collective-permute-start.4 = (bf16[2,8,96,768]{3,2,1,0:T(8,128)(2,1)}, bf16[2,8,96,768]{3,2,1,0:T(8,128)(2,1)}, u32[]{:S(2)}, u32[]{:S(2)}) collective-permute-start(bf16[2,8,96,768]{3,2,1,0:T(8,128)(2,1)} %pad_maximum_fusion.1), channel_id=1, source_target_pairs={{0,8},{8,0},{16,24},{24,16},{1,9},{9,1},{17,25},{25,17},{2,10},{10... | collective-permute-start | bytes 7077896 | tf_op jit(solution)/shard_map/ppermute | solution.py:419
  153.7 34.1 %copy-start.31 = (s32[3,2]{1,0:T(4,128)}, s32[3,2]{1,0:T(4,128)S(1)}, u32[]{:S(2)}) copy-start(s32[3,2]{1,0:T(4,128)S(1)} %get-tuple-element.83.row_ref) | copy-start | bytes 76
  156.4 17.2 %copy-start.25 = (bf16[1,1,6,8,16,128]{5,4,3,2,1,0:T(8,128)(2,1)S(1)}, bf16[1,1,6,8,16,128]{5,4,3,2,1,0:T(8,128)(2,1)}, u32[]{:S(2)}) copy-start(bf16[1,1,6,8,16,128]{5,4,3,2,1,0:T(8,128)(2,1)} %get-tuple-element.97) | copy-start | bytes 589828
  162.2 15.0 %copy-start.21 = (bf16[1,1,6,8,16,128]{5,4,3,2,1,0:T(8,128)(2,1)}, bf16[1,1,6,8,16,128]{5,4,3,2,1,0:T(8,128)(2,1)S(1)}, u32[]{:S(2)}) copy-start(bf16[1,1,6,8,16,128]{5,4,3,2,1,0:T(8,128)(2,1)S(1)} %collective-permute-done.14.refs_1_) | copy-start | bytes 589828
  162.2 17.0 %collective-permute-start.15 = (bf16[1,1,6,8,16,128]{5,4,3,2,1,0:T(8,128)(2,1)S(1)}, bf16[1,1,6,8,16,128]{5,4,3,2,1,0:T(8,128)(2,1)S(1)}, u32[]{:S(2)}, u32[]{:S(2)}) collective-permute-start(bf16[1,1,6,8,16,128]{5,4,3,2,1,0:T(8,128)(2,1)S(1)} %copy-done.26), channel_id=1, source_target_pairs={{0,2},{1,3},{2,0},{3,1},{4,6},{5,7},{6,4},{7,5},{8,10},{9,11},{10,... | collective-permute-start | bytes 589832 | tf_op jit(solution)/shard_map/ppermute | solution.py:552
  173.5 8.5 %collective-permute-start.16 = (bf16[1,1,6,8,16,128]{5,4,3,2,1,0:T(8,128)(2,1)S(1)}, bf16[1,1,6,8,16,128]{5,4,3,2,1,0:T(8,128)(2,1)S(1)}, u32[]{:S(2)}, u32[]{:S(2)}) collective-permute-start(bf16[1,1,6,8,16,128]{5,4,3,2,1,0:T(8,128)(2,1)S(1)} %copy-done.25), channel_id=1, source_target_pairs={{0,3},{1,2},{2,1},{3,0},{4,7},{5,6},{6,5},{7,4},{8,11},{9,10},{10,... | collective-permute-start | bytes 589832 | tf_op jit(solution)/shard_map/ppermute | solution.py:552
  182.8 75.1 %all-to-all-start.2 = ((bf16[8,4,6,4,16,128]{5,4,3,2,1,0:T(8,128)(2,1)}), bf16[8,4,6,4,16,128]{5,4,3,2,1,0:T(8,128)(2,1)}, u32[]{:S(2)}, u32[]{:S(2)}) async-start(bf16[8,4,6,4,16,128]{5,4,3,2,1,0:T(8,128)(2,1)} %pad_maximum_fusion), calls=%async_computation.2 | async-start | bytes 6291456 | tf_op jit(solution)/shard_map/all_to_all | solution.py:527
  188.6 74.0 %copy-start.7 = (bf16[512,768]{1,0:T(8,128)(2,1)}, bf16[512,768]{1,0:T(8,128)(2,1)S(1)}, u32[]{:S(2)}) copy-start(bf16[512,768]{1,0:T(8,128)(2,1)S(1)} %fusion.3) | copy-start | bytes 2359300
  189.2 83.9 %collective-permute-start.5 = (bf16[2,128,768]{2,1,0:T(8,128)(2,1)S(1)}, bf16[2,128,768]{2,1,0:T(8,128)(2,1)}, u32[]{:S(2)}, u32[]{:S(2)}) collective-permute-start(bf16[2,128,768]{2,1,0:T(8,128)(2,1)S(1)} %gather_fusion.7), channel_id=1, source_target_pairs={{0,8},{8,16},{16,24},{24,0},{1,9},{9,17},{17,25},{25,1},{2,10},{10... | collective-permute-start | bytes 1179656 | tf_op jit(solution)/shard_map/ppermute | solution.py:581
  190.6 82.5 %collective-permute-start.6 = (bf16[2,128,768]{2,1,0:T(8,128)(2,1)}, bf16[2,128,768]{2,1,0:T(8,128)(2,1)}, u32[]{:S(2)}, u32[]{:S(2)}) collective-permute-start(bf16[2,128,768]{2,1,0:T(8,128)(2,1)} %gather_fusion.8), channel_id=1, source_target_pairs={{0,16},{8,24},{16,0},{24,8},{1,17},{9,25},{17,1},{25,9},{2,18},{10... | collective-permute-start | bytes 1179656 | tf_op jit(solution)/shard_map/ppermute | solution.py:581
  193.3 79.8 %collective-permute-start.7 = (bf16[2,128,768]{2,1,0:T(8,128)(2,1)}, bf16[2,128,768]{2,1,0:T(8,128)(2,1)}, u32[]{:S(2)}, u32[]{:S(2)}) collective-permute-start(bf16[2,128,768]{2,1,0:T(8,128)(2,1)} %gather_fusion.9), channel_id=1, source_target_pairs={{0,24},{8,0},{16,8},{24,16},{1,25},{9,1},{17,9},{25,17},{2,26},{10... | collective-permute-start | bytes 1179656 | tf_op jit(solution)/shard_map/ppermute | solution.py:581
  257.9 126.0 %all-to-all-start.3 = ((bf16[8,3,6,4,16,128]{5,4,3,2,1,0:T(8,128)(2,1)}), bf16[8,3,6,4,16,128]{5,4,3,2,1,0:T(8,128)(2,1)}, u32[]{:S(2)}, u32[]{:S(2)}) async-start(bf16[8,3,6,4,16,128]{5,4,3,2,1,0:T(8,128)(2,1)} %get-tuple-element.70), calls=%async_computation.3 | async-start | bytes 4718592 | tf_op jit(solution)/shard_map/all_to_all | solution.py:527
  272.4 44.0 %collective-permute-start.8 = (bf16[8,8,8,16,128]{4,3,2,1,0:T(8,128)(2,1)}, bf16[8,8,8,16,128]{4,3,2,1,0:T(8,128)(2,1)S(1)}, u32[]{:S(2)}, u32[]{:S(2)}) collective-permute-start(bf16[8,8,8,16,128]{4,3,2,1,0:T(8,128)(2,1)} %get-tuple-element.46), channel_id=1, source_target_pairs={{0,8},{8,16},{16,24},{24,0},{1,9},{9,17},{17,25},{25,1},{2,10},{10... | collective-permute-start | bytes 6291464 | tf_op jit(solution)/shard_map/ppermute | solution.py:568
  275.9 115.6 %collective-permute-start.12 = (bf16[8,8,8,16,128]{4,3,2,1,0:T(8,128)(2,1)}, bf16[8,8,8,16,128]{4,3,2,1,0:T(8,128)(2,1)}, u32[]{:S(2)}, u32[]{:S(2)}) collective-permute-start(bf16[8,8,8,16,128]{4,3,2,1,0:T(8,128)(2,1)} %get-tuple-element.47), channel_id=1, source_target_pairs={{0,16},{8,24},{16,0},{24,8},{1,17},{9,25},{17,1},{25,9},{2,18},{10... | collective-permute-start | bytes 6291464 | tf_op jit(solution)/shard_map/ppermute | solution.py:568
  277.4 114.1 %collective-permute-start.13 = (bf16[8,8,8,16,128]{4,3,2,1,0:T(8,128)(2,1)}, bf16[8,8,8,16,128]{4,3,2,1,0:T(8,128)(2,1)}, u32[]{:S(2)}, u32[]{:S(2)}) collective-permute-start(bf16[8,8,8,16,128]{4,3,2,1,0:T(8,128)(2,1)} %get-tuple-element.48), channel_id=1, source_target_pairs={{0,24},{8,0},{16,8},{24,16},{1,25},{9,1},{17,9},{25,17},{2,26},{10... | collective-permute-start | bytes 6291464 | tf_op jit(solution)/shard_map/ppermute | solution.py:568
  291.3 25.2 %copy-start.34 = (f32[16]{0:T(128)S(1)}, f32[16]{0:T(128)}, u32[]{:S(2)}) copy-start(f32[16]{0:T(128)} %param.19) | copy-start | bytes 196
  317.8 14.1 %copy-start.32 = (bf16[16,256]{1,0:T(8,128)(2,1)S(1)}, bf16[16,256]{1,0:T(8,128)(2,1)}, u32[]{:S(2)}) copy-start(bf16[16,256]{1,0:T(8,128)(2,1)} %constant.153.clone.1) | copy-start | bytes 24580
  330.0 50.0 %collective-permute-start.23 = (bf16[1,4,16,768]{3,2,1,0:T(8,128)(2,1)}, bf16[1,4,16,768]{3,2,1,0:T(8,128)(2,1)S(1)}, u32[]{:S(2)}, u32[]{:S(2)}) collective-permute-start(bf16[1,4,16,768]{3,2,1,0:T(8,128)(2,1)} %bitcast.104), channel_id=1, source_target_pairs={{0,1},{1,0},{2,3},{3,2},{4,5},{5,4},{6,7},{7,6},{8,9},{9,8},{10,11... | collective-permute-start | bytes 294920 | tf_op jit(solution)/shard_map/ppermute | solution.py:640
  345.4 34.6 %copy-start.27 = (bf16[4,16,768]{2,1,0:T(8,128)(2,1)S(1)}, bf16[4,16,768]{2,1,0:T(8,128)(2,1)}, u32[]{:S(2)}) copy-start(bf16[4,16,768]{2,1,0:T(8,128)(2,1)} %get-tuple-element.72) | copy-start | bytes 294916
  384.0 71.6 %all-to-all-start.4 = ((bf16[8,1,6,4,16,128]{5,4,3,2,1,0:T(8,128)(2,1)}), bf16[8,1,6,4,16,128]{5,4,3,2,1,0:T(8,128)(2,1)S(1)}, u32[]{:S(2)}, u32[]{:S(2)}) async-start(bf16[8,1,6,4,16,128]{5,4,3,2,1,0:T(8,128)(2,1)} %get-tuple-element.73), calls=%async_computation.4 | async-start | bytes 1572864 | tf_op jit(solution)/shard_map/all_to_all | solution.py:527
  388.5 39.3 %collective-permute-start.20 = (bf16[8,8,4,16,128]{4,3,2,1,0:T(8,128)(2,1)}, bf16[8,8,4,16,128]{4,3,2,1,0:T(8,128)(2,1)S(1)}, u32[]{:S(2)}, u32[]{:S(2)}) collective-permute-start(bf16[8,8,4,16,128]{4,3,2,1,0:T(8,128)(2,1)} %get-tuple-element.62.refs_10_), channel_id=1, source_target_pairs={{0,8},{8,16},{16,24},{24,0},{1,9},{9,17},{17,25},{25,1},{2,10},{10... | collective-permute-start | bytes 3145736 | tf_op jit(solution)/shard_map/ppermute | solution.py:637
  388.5 39.4 %collective-permute-start.21 = (bf16[8,8,4,16,128]{4,3,2,1,0:T(8,128)(2,1)}, bf16[8,8,4,16,128]{4,3,2,1,0:T(8,128)(2,1)S(1)}, u32[]{:S(2)}, u32[]{:S(2)}) collective-permute-start(bf16[8,8,4,16,128]{4,3,2,1,0:T(8,128)(2,1)} %get-tuple-element.63.refs_11_), channel_id=1, source_target_pairs={{0,16},{8,24},{16,0},{24,8},{1,17},{9,25},{17,1},{25,9},{2,18},{10... | collective-permute-start | bytes 3145736 | tf_op jit(solution)/shard_map/ppermute | solution.py:637
  390.1 45.7 %collective-permute-start.22 = (bf16[8,8,4,16,128]{4,3,2,1,0:T(8,128)(2,1)}, bf16[8,8,4,16,128]{4,3,2,1,0:T(8,128)(2,1)S(1)}, u32[]{:S(2)}, u32[]{:S(2)}) collective-permute-start(bf16[8,8,4,16,128]{4,3,2,1,0:T(8,128)(2,1)} %get-tuple-element.64.refs_12_), channel_id=1, source_target_pairs={{0,24},{8,0},{16,8},{24,16},{1,25},{9,1},{17,9},{25,17},{2,26},{10... | collective-permute-start | bytes 3145736 | tf_op jit(solution)/shard_map/ppermute | solution.py:637
  456.5 72.9 %all-to-all-start.5 = ((bf16[8,3,6,4,16,128]{5,4,3,2,1,0:T(8,128)(2,1)}), bf16[8,3,6,4,16,128]{5,4,3,2,1,0:T(8,128)(2,1)}, u32[]{:S(2)}, u32[]{:S(2)}) async-start(bf16[8,3,6,4,16,128]{5,4,3,2,1,0:T(8,128)(2,1)} %triangle_1.3.refs_9_), calls=%async_computation.5 | async-start | bytes 4718592 | tf_op jit(solution)/shard_map/all_to_all | solution.py:527
  462.4 44.5 %collective-permute-start.27 = (bf16[2,4,16,768]{3,2,1,0:T(8,128)(2,1)S(1)}, bf16[2,4,16,768]{3,2,1,0:T(8,128)(2,1)S(1)}, u32[]{:S(2)}, u32[]{:S(2)}) collective-permute-start(bf16[2,4,16,768]{3,2,1,0:T(8,128)(2,1)S(1)} %pad_maximum_fusion.6), channel_id=1, source_target_pairs={{0,2},{1,3},{2,0},{3,1},{4,6},{5,7},{6,4},{7,5},{8,10},{9,11},{10,... | collective-permute-start | bytes 589832 | tf_op jit(solution)/shard_map/ppermute | solution.py:640
  507.0 14.1 %collective-permute-start.28 = (bf16[4,16,768]{2,1,0:T(8,128)(2,1)S(1)}, bf16[4,16,768]{2,1,0:T(8,128)(2,1)S(1)}, u32[]{:S(2)}, u32[]{:S(2)}) collective-permute-start(bf16[4,16,768]{2,1,0:T(8,128)(2,1)S(1)} %fusion.6), channel_id=1, source_target_pairs={{0,0},{4,1},{1,2},{5,3},{2,4},{6,5},{3,6},{7,7},{8,8},{12,9},{9,10... | collective-permute-start | bytes 294920 | tf_op jit(solution)/shard_map/ppermute | solution.py:651
  521.7 41.4 %copy-start.6 = (bf16[8,1,96,768]{3,2,1,0:T(8,128)(2,1)S(1)}, bf16[8,1,96,768]{3,2,1,0:T(8,128)(2,1)}, u32[]{:S(2)}) copy-start(bf16[8,1,96,768]{3,2,1,0:T(8,128)(2,1)} %copy-done.5) | copy-start | bytes 3538948
  529.4 75.6 %all-to-all-start.6 = ((bf16[8,1,6,4,16,128]{5,4,3,2,1,0:T(8,128)(2,1)}), bf16[8,1,6,4,16,128]{5,4,3,2,1,0:T(8,128)(2,1)S(1)}, u32[]{:S(2)}, u32[]{:S(2)}) async-start(bf16[8,1,6,4,16,128]{5,4,3,2,1,0:T(8,128)(2,1)} %triangle_0.3), calls=%async_computation.6 | async-start | bytes 1572864 | tf_op jit(solution)/shard_map/all_to_all | solution.py:527
  537.6 24.9 %collective-permute-start.17 = (bf16[1,3,6,8,16,128]{5,4,3,2,1,0:T(8,128)(2,1)}, bf16[1,3,6,8,16,128]{5,4,3,2,1,0:T(8,128)(2,1)S(1)}, u32[]{:S(2)}, u32[]{:S(2)}) collective-permute-start(bf16[1,3,6,8,16,128]{5,4,3,2,1,0:T(8,128)(2,1)} %get-tuple-element.66), channel_id=1, source_target_pairs={{0,1},{1,0},{2,3},{3,2},{4,5},{5,4},{6,7},{7,6},{8,9},{9,8},{10,11... | collective-permute-start | bytes 1769480 | tf_op jit(solution)/shard_map/ppermute | solution.py:552
  539.6 27.1 %collective-permute-start.18 = (bf16[1,3,6,8,16,128]{5,4,3,2,1,0:T(8,128)(2,1)}, bf16[1,3,6,8,16,128]{5,4,3,2,1,0:T(8,128)(2,1)S(1)}, u32[]{:S(2)}, u32[]{:S(2)}) collective-permute-start(bf16[1,3,6,8,16,128]{5,4,3,2,1,0:T(8,128)(2,1)} %get-tuple-element.67), channel_id=1, source_target_pairs={{0,2},{1,3},{2,0},{3,1},{4,6},{5,7},{6,4},{7,5},{8,10},{9,11},{10,... | collective-permute-start | bytes 1769480 | tf_op jit(solution)/shard_map/ppermute | solution.py:552
  541.1 38.4 %collective-permute-start.19 = (bf16[1,3,6,8,16,128]{5,4,3,2,1,0:T(8,128)(2,1)}, bf16[1,3,6,8,16,128]{5,4,3,2,1,0:T(8,128)(2,1)}, u32[]{:S(2)}, u32[]{:S(2)}) collective-permute-start(bf16[1,3,6,8,16,128]{5,4,3,2,1,0:T(8,128)(2,1)} %get-tuple-element.68), channel_id=1, source_target_pairs={{0,3},{1,2},{2,1},{3,0},{4,7},{5,6},{6,5},{7,4},{8,11},{9,10},{10,... | collective-permute-start | bytes 1769480 | tf_op jit(solution)/shard_map/ppermute | solution.py:552
  541.1 63.9 %collective-permute-start.24 = (bf16[1,1,6,8,16,128]{5,4,3,2,1,0:T(8,128)(2,1)}, bf16[1,1,6,8,16,128]{5,4,3,2,1,0:T(8,128)(2,1)S(1)}, u32[]{:S(2)}, u32[]{:S(2)}) collective-permute-start(bf16[1,1,6,8,16,128]{5,4,3,2,1,0:T(8,128)(2,1)} %get-tuple-element.76), channel_id=1, source_target_pairs={{0,1},{1,0},{2,3},{3,2},{4,5},{5,4},{6,7},{7,6},{8,9},{9,8},{10,11... | collective-permute-start | bytes 589832 | tf_op jit(solution)/shard_map/ppermute | solution.py:552
  543.1 61.9 %collective-permute-start.25 = (bf16[1,1,6,8,16,128]{5,4,3,2,1,0:T(8,128)(2,1)}, bf16[1,1,6,8,16,128]{5,4,3,2,1,0:T(8,128)(2,1)}, u32[]{:S(2)}, u32[]{:S(2)}) collective-permute-start(bf16[1,1,6,8,16,128]{5,4,3,2,1,0:T(8,128)(2,1)} %get-tuple-element.77), channel_id=1, source_target_pairs={{0,2},{1,3},{2,0},{3,1},{4,6},{5,7},{6,4},{7,5},{8,10},{9,11},{10,... | collective-permute-start | bytes 589832 | tf_op jit(solution)/shard_map/ppermute | solution.py:552
  562.5 17.0 %copy-start.18 = (bf16[1,3,6,8,16,128]{5,4,3,2,1,0:T(8,128)(2,1)}, bf16[1,3,6,8,16,128]{5,4,3,2,1,0:T(8,128)(2,1)S(1)}, u32[]{:S(2)}) copy-start(bf16[1,3,6,8,16,128]{5,4,3,2,1,0:T(8,128)(2,1)S(1)} %collective-permute-done.17.refs_1_) | copy-start | bytes 1769476
  562.5 42.5 %collective-permute-start.26 = (bf16[1,1,6,8,16,128]{5,4,3,2,1,0:T(8,128)(2,1)}, bf16[1,1,6,8,16,128]{5,4,3,2,1,0:T(8,128)(2,1)}, u32[]{:S(2)}, u32[]{:S(2)}) collective-permute-start(bf16[1,1,6,8,16,128]{5,4,3,2,1,0:T(8,128)(2,1)} %get-tuple-element.78), channel_id=1, source_target_pairs={{0,3},{1,2},{2,1},{3,0},{4,7},{5,6},{6,5},{7,4},{8,11},{9,10},{10,... | collective-permute-start | bytes 589832 | tf_op jit(solution)/shard_map/ppermute | solution.py:552
  566.7 12.8 %copy-start.19 = (bf16[1,3,6,8,16,128]{5,4,3,2,1,0:T(8,128)(2,1)}, bf16[1,3,6,8,16,128]{5,4,3,2,1,0:T(8,128)(2,1)S(1)}, u32[]{:S(2)}) copy-start(bf16[1,3,6,8,16,128]{5,4,3,2,1,0:T(8,128)(2,1)S(1)} %collective-permute-done.18.refs_2_) | copy-start | bytes 1769476
  (23 other events, 90.4 us)

commit v3 on v1

--- a/solution.py
+++ b/solution.py
@@ -568,16 +568,16 @@
         )
     pair_out, pair_grad = whole
 
-    left_lead = swap(lefts[0], left_rest, pair_grad, *arrived)
-    sums = triangle_rows(left_rest, rights, arrived, tri_source, tri_place, LEAD)
-    tri_rest = swap(sums, left_lead)
-    near_mixed = after(mixed[None], sums)
+    near_mixed = mixed[None]
     for step in [1 << n for n in range(block_rows.bit_length() - 1)]:
         other = lax.ppermute(near_mixed, "row", [(r, r ^ step) for r in range(parts)])
         swapped = (row_index & step) > 0
         near_mixed = jnp.concatenate(
             [jnp.where(swapped, other, near_mixed), jnp.where(swapped, near_mixed, other)], axis=0
         )
+    left_lead = swap(lefts[0], left_rest, near_mixed, pair_grad, *arrived)
+    sums = triangle_rows(left_rest, rights, arrived, tri_source, tri_place, LEAD)
+    tri_rest = swap(sums, left_lead)
     sharers = parts // block_rows
     sent_mixed = lax.dynamic_index_in_dim(near_mixed, row_index % block_rows, 1, keepdims=False)
     senders = [((r % sharers) * block_rows + r // sharers, r) for r in range(parts)]

time: 508 us -> 508 us (level)
  no operation moved by 1% of the time
where the time goes in v3:
time: 508 us; the launch traced here: 506 us
  waiting for transfers between devices  199 us (39%)
  Pallas kernels  191 us (38%)
  starting transfers between devices  63 us (12%)
  local copies, waits for them, and re-layouts  24.3 us (5%)
  other arithmetic  18.7 us (4%)
  matrix products  9.3 us (2%)
    ppermute x2, waiting for transfers between devices, per_device(): lax.ppermute(near_mixed, 'row', [(r, r ^ step) for r in range(parts)])  78.7 us
    ppermute x5, waiting for transfers between devices, doubled(): lax.ppermute(stacked, axis, pairs)  74.9 us
    pallas_call x2, Pallas kernels, triangle_rows(): pl.pallas_call(body, grid=(part, count), in_specs=[smem] * 2 + [row_spec]...  50.7 us
    pallas_call x2, Pallas kernels, gradient_rows(): pl.pallas_call(body, grid=(count, slots), in_specs=[big, pl.BlockSpec((No...  47.5 us
    all_to_all x6, starting transfers between devices, swap(): lax.all_to_all(after(values, *earlier), 'row', split_axis=0, concat_axis=...  44.5 us
    pallas_call x2, Pallas kernels, project_rows(): pl.pallas_call(body, grid=(count, slots), in_specs=[pl.BlockSpec((None, N...  39.1 us
    all_to_all x6, waiting for transfers between devices, swap(): lax.all_to_all(after(values, *earlier), 'row', split_axis=0, concat_axis=...  35.4 us
    pallas_call x2, Pallas kernels, finish_rows(): pl.pallas_call(body, grid=(count, slots), in_specs=[big, big, pl.BlockSpe...  35 us
  transfers between devices with their start and end apart: 20, of which 12 were waited for; matrix products, arithmetic and copies ran while one was open for 10% of the time, Pallas kernels for 36%

profile of v3, /device:TPU:0, one launch (start us, length us, event | category | flops | bytes accessed | tf_op | source)
XLA Modules:
  0.0 505.9 jit_solution(2740706710434870625)
XLA Ops:
  0.7 1.3 pad_maximum_fusion.2
  2.0 4.1 collective-permute-start
  7.0 1.3 pad_maximum_fusion.7.w_ref
  8.4 10.6 %project_0.1 = (bf16[8,1,6,8,16,128]{5,4,3,2,1,0:T(8,128)(2,1)}, bf16[8,1,6,8,16,128]{5,4,3,2,1,0:T(8,128)(2,1)}, bf16[1,6,256,128]{3,2,1,0:T(8,128)(2,1)}) custom-call(bf16[4,6,16,128,128]{4,3,2,1,0:T(8,128)(2,1)} %x_ref.11, bf16[272,128]{1,0:T(8,128)(2,1)} %pad_maximum_fusion.7.w_ref), custom_call_target="tpu_custom_call" | custom-call | tf_op jit(solution)/shard_map/project_0/pallas_call | solution.py:69
  19.0 3.8 all-to-all-start
  22.8 2.0 collective-permute-start.1
  24.9 28.5 %project_1.1 = (bf16[8,3,6,8,16,128]{5,4,3,2,1,0:T(8,128)(2,1)}, bf16[8,3,6,8,16,128]{5,4,3,2,1,0:T(8,128)(2,1)}, bf16[3,6,256,128]{3,2,1,0:T(8,128)(2,1)}) custom-call(bf16[4,6,16,128,128]{4,3,2,1,0:T(8,128)(2,1)} %x_ref.11, bf16[272,128]{1,0:T(8,128)(2,1)} %pad_maximum_fusion.7.w_ref), custom_call_target="tpu_custom_call" | custom-call | tf_op jit(solution)/shard_map/project_1/pallas_call | solution.py:69
  53.3 1.4 collective-permute-done.1
  54.8 4.8 all-to-all-done.refs_0_
  59.6 1.2 copy-done.3
  60.8 4.6 all-to-all-start.1
  65.4 1.9 collective-permute-start.2
  67.3 49.6 %collective-permute-done.2 = bf16[4,96,768]{2,1,0:T(8,128)(2,1)S(1)} collective-permute-done((bf16[4,96,768]{2,1,0:T(8,128)(2,1)S(1)}, bf16[4,96,768]{2,1,0:T(8,128)(2,1)S(1)}, u32[]{:S(2)}, u32[]{:S(2)}) %collective-permute-start.2) | collective-permute-done | bytes 589856 | tf_op jit(solution)/shard_map/ppermute | solution.py:387
  117.0 1.6 collective-permute-start.3
  119.9 23.9 %collective-permute-done.3 = bf16[1,8,96,768]{3,2,1,0:T(8,128)(2,1)S(1)} collective-permute-done((bf16[1,8,96,768]{3,2,1,0:T(8,128)(2,1)S(1)}, bf16[1,8,96,768]{3,2,1,0:T(8,128)(2,1)S(1)}, u32[]{:S(2)}, u32[]{:S(2)}) %collective-permute-start.3) | collective-permute-done | bytes 1179680 | tf_op jit(solution)/shard_map/ppermute | solution.py:387
  143.7 1.6 pad_maximum_fusion
  151.6 1.4 fusion.7
  155.0 3.7 maximum_bitcast_fusion
  158.7 10.5 %all-to-all-done.1.refs_1_ = bf16[8,3,6,8,16,128]{5,4,3,2,1,0:T(8,128)(2,1)} async-done(((bf16[8,3,6,8,16,128]{5,4,3,2,1,0:T(8,128)(2,1)}), bf16[8,3,6,8,16,128]{5,4,3,2,1,0:T(8,128)(2,1)}, u32[]{:S(2)}, u32[]{:S(2)}) %all-to-all-start.1) | async-done | bytes 4718624 | tf_op jit(solution)/shard_map/all_to_all | solution.py:495
  169.1 4.7 all-to-all-start.2
  176.0 1.6 collective-permute-start.6
  177.6 1.3 gather_fusion.9
  178.9 1.4 collective-permute-start.7
  186.1 6.1 %pick_blocks.1 = (bf16[8,8,8,16,128]{4,3,2,1,0:T(8,128)(2,1)}, bf16[8,8,8,16,128]{4,3,2,1,0:T(8,128)(2,1)}, bf16[8,8,8,16,128]{4,3,2,1,0:T(8,128)(2,1)}) custom-call(s32[3,2]{1,0:T(4,128)} %copy-done.14, s32[3,2,4]{2,1,0:T(2,128)} %multiply_reduce_fusion.2.slot_ref, bf16[8,1,6,8,16,128]{5,4,3,2,1,0:T(8,128)(2,1)} %copy-done.3, ...), custom_call_target="tpu_custom_call" | custom-call | tf_op jit(solution)/shard_map/pick_blocks/pallas_call | solution.py:116
  192.7 1.4 collective-permute-start.10
  195.2 2.8 pad_maximum_fusion.1
  197.9 5.4 %gather_fusion.6 = bf16[32,96,768]{2,1,0:T(8,128)(2,1)} fusion(bf16[8,4,96,768]{3,2,0,1:T(8,128)(2,1)} %maximum_bitcast_fusion, s32[32]{0:T(128)S(1)} %reshape.369), kind=kCustom, calls=%fused_computation.6 | custom fusion | bytes 9437440 | tf_op jit(solution)/shard_map/gather | solution.py:517
  203.3 2.7 fusion.33
  206.0 1.1 convolution_convert_fusion.3
  208.3 3.0 convolution_convert_fusion.1
  211.3 3.0 convolution_convert_fusion
  215.0 12.2 %attend.1 = (bf16[4,16,768]{2,1,0:T(8,128)(2,1)}, bf16[4,6,256,128]{3,2,1,0:T(8,128)(2,1)}) custom-call(s32[4,6]{1,0:T(4,128)} %reshape.322.place_ref, s32[4,6]{1,0:T(4,128)} %copy.64.mask_ref, f32[4,6]{1,0:T(4,128)} %compare_convert_fusion.1.flag_ref, bf16[4,16,768]{2,1,0:T(8,128)(2,1)} %bitcast.97, bf16[4,16,768]{2,1,0:T(8,128)(2,1)} %bitcast.98, ...), custom_call_target="tpu_custom_call" | custom-call | tf_op jit(solution)/shard_map/attend/pallas_call | solution.py:276
  227.2 13.0 %gradient_0.1 = (bf16[4,6,16,128,128]{4,3,2,1,0:T(8,128)(2,1)}, bf16[4,6,16,128,128]{4,3,2,1,0:T(8,128)(2,1)}) custom-call(bf16[4,6,16,128,128]{4,3,2,1,0:T(8,128)(2,1)} %x_ref.11, bf16[4,6,256,128]{3,2,1,0:T(8,128)(2,1)} %get-tuple-element.36.g_ref, bf16[1,6,256,128]{3,2,1,0:T(8,128)(2,1)} %get-tuple-element.34.refs_0_.b_ref, ...), custom_call_target="tpu_custom_call" | custom-call | tf_op jit(solution)/shard_map/gradient_0/pallas_call | solution.py:316
  240.2 34.5 %gradient_1.1 = (bf16[4,6,16,128,128]{4,3,2,1,0:T(8,128)(2,1)}, bf16[4,6,16,128,128]{4,3,2,1,0:T(8,128)(2,1)}) custom-call(bf16[4,6,16,128,128]{4,3,2,1,0:T(8,128)(2,1)} %x_ref.11, bf16[4,6,256,128]{3,2,1,0:T(8,128)(2,1)} %get-tuple-element.36.g_ref, ...), custom_call_target="tpu_custom_call", output_to_operand_aliasing={{0}: (5, {}), {1}: (6, {})} | custom-call | tf_op jit(solution)/shard_map/gradient_1/pallas_call | solution.py:316
  274.7 9.5 %collective-permute-done.10.refs_4_ = bf16[8,8,8,16,128]{4,3,2,1,0:T(8,128)(2,1)} collective-permute-done((bf16[8,8,8,16,128]{4,3,2,1,0:T(8,128)(2,1)}, bf16[8,8,8,16,128]{4,3,2,1,0:T(8,128)(2,1)}, u32[]{:S(2)}, u32[]{:S(2)}) %collective-permute-start.10) | collective-permute-done | bytes 2097184 | tf_op jit(solution)/shard_map/ppermute | solution.py:514
  284.3 5.9 %all-to-all-start.3 = ((bf16[8,1,6,8,16,128]{5,4,3,2,1,0:T(8,128)(2,1)}), bf16[8,1,6,8,16,128]{5,4,3,2,1,0:T(8,128)(2,1)}, u32[]{:S(2)}, u32[]{:S(2)}) async-start(bf16[8,1,6,8,16,128]{5,4,3,2,1,0:T(8,128)(2,1)} %get-tuple-element.45), calls=%async_computation.3 | async-start | bytes 3145728 | tf_op jit(solution)/shard_map/all_to_all | solution.py:495
  290.2 37.2 %triangle_1.1 = bf16[8,3,6,8,16,128]{5,4,3,2,1,0:T(8,128)(2,1)} custom-call(s32[4,6]{1,0:T(4,128)} %reshape.400.source_ref, s32[4,6,6]{2,1,0:T(8,128)} %compare_select_fusion.1.place_ref, bf16[8,3,6,8,16,128]{5,4,3,2,1,0:T(8,128)(2,1)} %all-to-all-done.2.left_ref, bf16[8,1,6,8,16,128]{5,4,3,2,1,0:T(8,128)(2,1)} %copy-done.3, ...), custom_call_target="tpu_custom_call" | custom-call | tf_op jit(solution)/shard_map/triangle_1/pallas_call | solution.py:191
  328.3 5.2 %all-to-all-start.4 = ((bf16[8,3,6,8,16,128]{5,4,3,2,1,0:T(8,128)(2,1)}), bf16[8,3,6,8,16,128]{5,4,3,2,1,0:T(8,128)(2,1)}, u32[]{:S(2)}, u32[]{:S(2)}) async-start(bf16[8,3,6,8,16,128]{5,4,3,2,1,0:T(8,128)(2,1)} %triangle_1.1), calls=%async_computation.4 | async-start | bytes 9437184 | tf_op jit(solution)/shard_map/all_to_all | solution.py:495
  333.5 2.0 collective-permute-start.11
  335.5 39.3 %collective-permute-done.11 = bf16[1,4,16,768]{3,2,1,0:T(8,128)(2,1)S(1)} collective-permute-done((bf16[1,4,16,768]{3,2,1,0:T(8,128)(2,1)S(1)}, bf16[1,4,16,768]{3,2,1,0:T(8,128)(2,1)S(1)}, u32[]{:S(2)}, u32[]{:S(2)}) %collective-permute-start.11) | collective-permute-done | bytes 98336 | tf_op jit(solution)/shard_map/ppermute | solution.py:573
  374.8 1.2 collective-permute-start.12
  376.0 39.5 %collective-permute-done.12 = bf16[2,4,16,768]{3,2,1,0:T(8,128)(2,1)S(1)} collective-permute-done((bf16[2,4,16,768]{3,2,1,0:T(8,128)(2,1)S(1)}, bf16[2,4,16,768]{3,2,1,0:T(8,128)(2,1)S(1)}, u32[]{:S(2)}, u32[]{:S(2)}) %collective-permute-start.12) | collective-permute-done | bytes 196640 | tf_op jit(solution)/shard_map/ppermute | solution.py:573
  416.9 13.6 %triangle_0.1 = bf16[8,1,6,8,16,128]{5,4,3,2,1,0:T(8,128)(2,1)} custom-call(s32[4,6]{1,0:T(4,128)} %reshape.400.source_ref, s32[4,6,6]{2,1,0:T(8,128)} %compare_select_fusion.1.place_ref, bf16[8,1,6,8,16,128]{5,4,3,2,1,0:T(8,128)(2,1)} %all-to-all-done.3.left_ref, bf16[8,1,6,8,16,128]{5,4,3,2,1,0:T(8,128)(2,1)} %copy-done.3, ...), custom_call_target="tpu_custom_call" | custom-call | tf_op jit(solution)/shard_map/triangle_0/pallas_call | solution.py:191
  430.5 8.9 %all-to-all-done.4.tri_ref = bf16[8,3,6,8,16,128]{5,4,3,2,1,0:T(8,128)(2,1)} async-done(((bf16[8,3,6,8,16,128]{5,4,3,2,1,0:T(8,128)(2,1)}), bf16[8,3,6,8,16,128]{5,4,3,2,1,0:T(8,128)(2,1)}, u32[]{:S(2)}, u32[]{:S(2)}) %all-to-all-start.4) | async-done | bytes 4718624 | tf_op jit(solution)/shard_map/all_to_all | solution.py:495
  439.4 20.3 %all-to-all-start.5 = ((bf16[8,1,6,8,16,128]{5,4,3,2,1,0:T(8,128)(2,1)}), bf16[8,1,6,8,16,128]{5,4,3,2,1,0:T(8,128)(2,1)}, u32[]{:S(2)}, u32[]{:S(2)}) async-start(bf16[8,1,6,8,16,128]{5,4,3,2,1,0:T(8,128)(2,1)} %triangle_0.1), calls=%async_computation.5 | async-start | bytes 3145728 | tf_op jit(solution)/shard_map/all_to_all | solution.py:495
  460.7 25.3 %finish_1.1.gate_ref = bf16[4,6,16,128,128]{4,3,2,1,0:T(8,128)(2,1)} custom-call(bf16[4,6,16,128,128]{4,3,2,1,0:T(8,128)(2,1)} %x_ref.11, bf16[4,6,16,128,128]{4,3,2,1,0:T(8,128)(2,1)} %get-tuple-element.39.gate_ref, bf16[8,3,6,8,16,128]{5,4,3,2,1,0:T(8,128)(2,1)} %all-to-all-done.4.tri_ref, bf16[64,128]{1,0:T(8,128)(2,1)} %w_ref.3), custom_call_target="tpu_custom_call", output_to_operand_aliasing={{}: (1, {})} | custom-call | tf_op jit(solution)/shard_map/finish_1/pallas_call | solution.py:354
  486.0 10.2 %all-to-all-done.5.tri_ref = bf16[8,1,6,8,16,128]{5,4,3,2,1,0:T(8,128)(2,1)} async-done(((bf16[8,1,6,8,16,128]{5,4,3,2,1,0:T(8,128)(2,1)}), bf16[8,1,6,8,16,128]{5,4,3,2,1,0:T(8,128)(2,1)}, u32[]{:S(2)}, u32[]{:S(2)}) %all-to-all-start.5) | async-done | bytes 1572896 | tf_op jit(solution)/shard_map/all_to_all | solution.py:495
  496.2 9.7 %finish_0.1 = bf16[4,6,16,128,128]{4,3,2,1,0:T(8,128)(2,1)} custom-call(bf16[4,6,16,128,128]{4,3,2,1,0:T(8,128)(2,1)} %x_ref.11, bf16[4,6,16,128,128]{4,3,2,1,0:T(8,128)(2,1)} %finish_1.1.gate_ref, bf16[8,1,6,8,16,128]{5,4,3,2,1,0:T(8,128)(2,1)} %all-to-all-done.5.tri_ref, bf16[64,128]{1,0:T(8,128)(2,1)} %w_ref.3), custom_call_target="tpu_custom_call", output_to_operand_aliasing={{}: (1, {})} | custom-call | tf_op jit(solution)/shard_map/finish_0/pallas_call | solution.py:354
  (140 shorter events, 25.2 us)
Async XLA Ops:
  0.6 184.8 %copy-start = (bf16[512,768]{1,0:T(8,128)(2,1)S(1)}, bf16[512,768]{1,0:T(8,128)(2,1)}, u32[]{:S(2)}) copy-start(bf16[512,768]{1,0:T(8,128)(2,1)} %param.21) | copy-start | bytes 2359300
  2.0 17.0 %collective-permute-start = (bf16[1,96,768]{2,1,0:T(8,128)(2,1)S(1)}, bf16[1,96,768]{2,1,0:T(8,128)(2,1)S(1)}, u32[]{:S(2)}, u32[]{:S(2)}) collective-permute-start(bf16[1,96,768]{2,1,0:T(8,128)(2,1)S(1)} %dynamic-slice_bitcast_fusion), channel_id=1, source_target_pairs={{0,4},{1,5},{2,6},{3,7},{4,0},{5,1},{6,2},{7,3},{8,12},{9,13},{10,... | collective-permute-start | bytes 442376 | tf_op jit(solution)/shard_map/ppermute | solution.py:387
  19.0 40.5 %all-to-all-start = ((bf16[8,1,6,8,16,128]{5,4,3,2,1,0:T(8,128)(2,1)}), bf16[8,1,6,8,16,128]{5,4,3,2,1,0:T(8,128)(2,1)S(1)}, u32[]{:S(2)}, u32[]{:S(2)}) async-start(bf16[8,1,6,8,16,128]{5,4,3,2,1,0:T(8,128)(2,1)} %get-tuple-element.27), calls=%async_computation | async-start | bytes 3145728 | tf_op jit(solution)/shard_map/all_to_all | solution.py:495
  22.8 31.9 %collective-permute-start.1 = (bf16[2,96,768]{2,1,0:T(8,128)(2,1)S(1)}, bf16[2,96,768]{2,1,0:T(8,128)(2,1)S(1)}, u32[]{:S(2)}, u32[]{:S(2)}) collective-permute-start(bf16[2,96,768]{2,1,0:T(8,128)(2,1)S(1)} %pad_maximum_fusion.5), channel_id=1, source_target_pairs={{0,2},{1,3},{2,0},{3,1},{4,6},{5,7},{6,4},{7,5},{8,10},{9,11},{10,... | collective-permute-start | bytes 884744 | tf_op jit(solution)/shard_map/ppermute | solution.py:387
  59.6 1.2 copy-start.3
  60.8 108.4 %all-to-all-start.1 = ((bf16[8,3,6,8,16,128]{5,4,3,2,1,0:T(8,128)(2,1)}), bf16[8,3,6,8,16,128]{5,4,3,2,1,0:T(8,128)(2,1)}, u32[]{:S(2)}, u32[]{:S(2)}) async-start(bf16[8,3,6,8,16,128]{5,4,3,2,1,0:T(8,128)(2,1)} %get-tuple-element.29), calls=%async_computation.1 | async-start | bytes 9437184 | tf_op jit(solution)/shard_map/all_to_all | solution.py:495
  65.4 53.2 %copy-start.12 = (s32[16,6]{0,1:T(8,128)S(1)}, s32[16,6]{0,1:T(8,128)}, u32[]{:S(2)}) copy-start(s32[16,6]{0,1:T(8,128)} %param.16) | copy-start | bytes 1156
  65.4 51.5 %collective-permute-start.2 = (bf16[4,96,768]{2,1,0:T(8,128)(2,1)S(1)}, bf16[4,96,768]{2,1,0:T(8,128)(2,1)S(1)}, u32[]{:S(2)}, u32[]{:S(2)}) collective-permute-start(bf16[4,96,768]{2,1,0:T(8,128)(2,1)S(1)} %pad_maximum_fusion.3), channel_id=1, source_target_pairs={{0,1},{1,0},{2,3},{3,2},{4,5},{5,4},{6,7},{7,6},{8,9},{9,8},{10,11... | collective-permute-start | bytes 1769480 | tf_op jit(solution)/shard_map/ppermute | solution.py:387
  117.0 26.7 %collective-permute-start.3 = (bf16[1,8,96,768]{3,2,1,0:T(8,128)(2,1)S(1)}, bf16[1,8,96,768]{3,2,1,0:T(8,128)(2,1)S(1)}, u32[]{:S(2)}, u32[]{:S(2)}) collective-permute-start(bf16[1,8,96,768]{3,2,1,0:T(8,128)(2,1)S(1)} %maximum_bitcast_fusion.1), channel_id=1, source_target_pairs={{0,16},{8,24},{16,0},{24,8},{1,17},{9,25},{17,1},{25,9},{2,18},{10... | collective-permute-start | bytes 3538952 | tf_op jit(solution)/shard_map/ppermute | solution.py:387
  119.8 26.7 %copy-start.16 = (s32[16,6]{0,1:T(8,128)S(1)}, s32[16,6]{0,1:T(8,128)}, u32[]{:S(2)}) copy-start(s32[16,6]{0,1:T(8,128)} %param.17) | copy-start | bytes 1156
  145.4 9.6 %collective-permute-start.4 = (bf16[2,8,96,768]{3,2,1,0:T(8,128)(2,1)}, bf16[2,8,96,768]{3,2,1,0:T(8,128)(2,1)}, u32[]{:S(2)}, u32[]{:S(2)}) collective-permute-start(bf16[2,8,96,768]{3,2,1,0:T(8,128)(2,1)} %pad_maximum_fusion), channel_id=1, source_target_pairs={{0,8},{8,0},{16,24},{24,16},{1,9},{9,1},{17,25},{25,17},{2,10},{10... | collective-permute-start | bytes 7077896 | tf_op jit(solution)/shard_map/ppermute | solution.py:387
  153.7 20.2 %copy-start.14 = (s32[3,2]{1,0:T(4,128)}, s32[3,2]{1,0:T(4,128)S(1)}, u32[]{:S(2)}) copy-start(s32[3,2]{1,0:T(4,128)S(1)} %get-tuple-element.51.row_ref) | copy-start | bytes 76
  169.1 4.8 copy-start.4
  169.1 115.1 %all-to-all-start.2 = ((bf16[8,3,6,8,16,128]{5,4,3,2,1,0:T(8,128)(2,1)}), bf16[8,3,6,8,16,128]{5,4,3,2,1,0:T(8,128)(2,1)}, u32[]{:S(2)}, u32[]{:S(2)}) async-start(bf16[8,3,6,8,16,128]{5,4,3,2,1,0:T(8,128)(2,1)} %get-tuple-element.41), calls=%async_computation.2 | async-start | bytes 9437184 | tf_op jit(solution)/shard_map/all_to_all | solution.py:495
  174.5 5.9 %copy-start.11 = (bf16[128,16]{0,1:T(8,128)(2,1)S(1)}, bf16[128,16]{0,1:T(8,128)(2,1)}, u32[]{:S(2)}) copy-start(bf16[128,16]{0,1:T(8,128)(2,1)} %param.25) | copy-start | bytes 12292
  174.5 6.1 %copy-start.13 = (bf16[128,128]{1,0:T(8,128)(2,1)S(1)}, bf16[128,128]{1,0:T(8,128)(2,1)}, u32[]{:S(2)}) copy-start(bf16[128,128]{1,0:T(8,128)(2,1)} %param.23) | copy-start | bytes 98308
  174.5 7.4 %copy-start.15 = (bf16[16,256]{1,0:T(8,128)(2,1)S(1)}, bf16[16,256]{1,0:T(8,128)(2,1)}, u32[]{:S(2)}) copy-start(bf16[16,256]{1,0:T(8,128)(2,1)} %constant.150.clone.1) | copy-start | bytes 24580
  174.5 8.0 %copy-start.2 = (s32[16]{0:T(128)S(1)}, s32[16]{0:T(128)}, u32[]{:S(2)}) copy-start(s32[16]{0:T(128)} %param.18) | copy-start | bytes 196
  175.4 17.4 %collective-permute-start.5 = (bf16[2,128,768]{2,1,0:T(8,128)(2,1)S(1)}, bf16[2,128,768]{2,1,0:T(8,128)(2,1)}, u32[]{:S(2)}, u32[]{:S(2)}) collective-permute-start(bf16[2,128,768]{2,1,0:T(8,128)(2,1)S(1)} %gather_fusion.7), channel_id=1, source_target_pairs={{0,8},{8,16},{16,24},{24,0},{1,9},{9,17},{17,25},{25,1},{2,10},{10... | collective-permute-start | bytes 1179656 | tf_op jit(solution)/shard_map/ppermute | solution.py:527
  176.0 18.8 %collective-permute-start.6 = (bf16[2,128,768]{2,1,0:T(8,128)(2,1)S(1)}, bf16[2,128,768]{2,1,0:T(8,128)(2,1)}, u32[]{:S(2)}, u32[]{:S(2)}) collective-permute-start(bf16[2,128,768]{2,1,0:T(8,128)(2,1)S(1)} %gather_fusion.8), channel_id=1, source_target_pairs={{0,16},{8,24},{16,0},{24,8},{1,17},{9,25},{17,1},{25,9},{2,18},{10... | collective-permute-start | bytes 1179656 | tf_op jit(solution)/shard_map/ppermute | solution.py:527
  178.9 16.3 %collective-permute-start.7 = (bf16[2,128,768]{2,1,0:T(8,128)(2,1)}, bf16[2,128,768]{2,1,0:T(8,128)(2,1)}, u32[]{:S(2)}, u32[]{:S(2)}) collective-permute-start(bf16[2,128,768]{2,1,0:T(8,128)(2,1)} %gather_fusion.9), channel_id=1, source_target_pairs={{0,24},{8,0},{16,8},{24,16},{1,25},{9,1},{17,9},{25,17},{2,26},{10... | collective-permute-start | bytes 1179656 | tf_op jit(solution)/shard_map/ppermute | solution.py:527
  192.2 82.6 %collective-permute-start.8 = (bf16[8,8,8,16,128]{4,3,2,1,0:T(8,128)(2,1)}, bf16[8,8,8,16,128]{4,3,2,1,0:T(8,128)(2,1)}, u32[]{:S(2)}, u32[]{:S(2)}) collective-permute-start(bf16[8,8,8,16,128]{4,3,2,1,0:T(8,128)(2,1)} %get-tuple-element.30), channel_id=1, source_target_pairs={{0,8},{8,16},{16,24},{24,0},{1,9},{9,17},{17,25},{25,1},{2,10},{10... | collective-permute-start | bytes 6291464 | tf_op jit(solution)/shard_map/ppermute | solution.py:514
  192.2 82.6 %collective-permute-start.9 = (bf16[8,8,8,16,128]{4,3,2,1,0:T(8,128)(2,1)}, bf16[8,8,8,16,128]{4,3,2,1,0:T(8,128)(2,1)}, u32[]{:S(2)}, u32[]{:S(2)}) collective-permute-start(bf16[8,8,8,16,128]{4,3,2,1,0:T(8,128)(2,1)} %get-tuple-element.31), channel_id=1, source_target_pairs={{0,16},{8,24},{16,0},{24,8},{1,17},{9,25},{17,1},{25,9},{2,18},{10... | collective-permute-start | bytes 6291464 | tf_op jit(solution)/shard_map/ppermute | solution.py:514
  192.7 91.5 %collective-permute-start.10 = (bf16[8,8,8,16,128]{4,3,2,1,0:T(8,128)(2,1)}, bf16[8,8,8,16,128]{4,3,2,1,0:T(8,128)(2,1)}, u32[]{:S(2)}, u32[]{:S(2)}) collective-permute-start(bf16[8,8,8,16,128]{4,3,2,1,0:T(8,128)(2,1)} %get-tuple-element.32), channel_id=1, source_target_pairs={{0,24},{8,0},{16,8},{24,16},{1,25},{9,1},{17,9},{25,17},{2,26},{10... | collective-permute-start | bytes 6291464 | tf_op jit(solution)/shard_map/ppermute | solution.py:514
  203.3 2.7 copy-start.8
  203.3 3.9 copy-start.9
  206.0 2.3 copy-start.5
  211.3 3.0 copy-start.17
  284.3 44.1 %all-to-all-start.3 = ((bf16[8,1,6,8,16,128]{5,4,3,2,1,0:T(8,128)(2,1)}), bf16[8,1,6,8,16,128]{5,4,3,2,1,0:T(8,128)(2,1)}, u32[]{:S(2)}, u32[]{:S(2)}) async-start(bf16[8,1,6,8,16,128]{5,4,3,2,1,0:T(8,128)(2,1)} %get-tuple-element.45), calls=%async_computation.3 | async-start | bytes 3145728 | tf_op jit(solution)/shard_map/all_to_all | solution.py:495
  327.3 6.2 %copy-start.10 = (bf16[4,16,768]{2,1,0:T(8,128)(2,1)S(1)}, bf16[4,16,768]{2,1,0:T(8,128)(2,1)}, u32[]{:S(2)}) copy-start(bf16[4,16,768]{2,1,0:T(8,128)(2,1)} %get-tuple-element.43) | copy-start | bytes 294916
  328.3 111.1 %all-to-all-start.4 = ((bf16[8,3,6,8,16,128]{5,4,3,2,1,0:T(8,128)(2,1)}), bf16[8,3,6,8,16,128]{5,4,3,2,1,0:T(8,128)(2,1)}, u32[]{:S(2)}, u32[]{:S(2)}) async-start(bf16[8,3,6,8,16,128]{5,4,3,2,1,0:T(8,128)(2,1)} %triangle_1.1), calls=%async_computation.4 | async-start | bytes 9437184 | tf_op jit(solution)/shard_map/all_to_all | solution.py:495
  333.5 41.3 %collective-permute-start.11 = (bf16[1,4,16,768]{3,2,1,0:T(8,128)(2,1)S(1)}, bf16[1,4,16,768]{3,2,1,0:T(8,128)(2,1)S(1)}, u32[]{:S(2)}, u32[]{:S(2)}) collective-permute-start(bf16[1,4,16,768]{3,2,1,0:T(8,128)(2,1)S(1)} %bitcast.103), channel_id=1, source_target_pairs={{0,1},{1,0},{2,3},{3,2},{4,5},{5,4},{6,7},{7,6},{8,9},{9,8},{10,11... | collective-permute-start | bytes 294920 | tf_op jit(solution)/shard_map/ppermute | solution.py:573
  374.8 40.7 %collective-permute-start.12 = (bf16[2,4,16,768]{3,2,1,0:T(8,128)(2,1)S(1)}, bf16[2,4,16,768]{3,2,1,0:T(8,128)(2,1)S(1)}, u32[]{:S(2)}, u32[]{:S(2)}) collective-permute-start(bf16[2,4,16,768]{3,2,1,0:T(8,128)(2,1)S(1)} %pad_maximum_fusion.6), channel_id=1, source_target_pairs={{0,2},{1,3},{2,0},{3,1},{4,6},{5,7},{6,4},{7,5},{8,10},{9,11},{10,... | collective-permute-start | bytes 589832 | tf_op jit(solution)/shard_map/ppermute | solution.py:573
  415.6 0.7 collective-permute-start.13
  416.3 0.6 copy-start.6
  430.5 29.2 %copy-start.7 = (bf16[4,16,768]{2,1,0:T(8,128)(2,1)S(1)}, bf16[4,16,768]{2,1,0:T(8,128)(2,1)}, u32[]{:S(2)}) copy-start(bf16[4,16,768]{2,1,0:T(8,128)(2,1)} %copy-done.6) | copy-start | bytes 294916
  439.4 56.8 %all-to-all-start.5 = ((bf16[8,1,6,8,16,128]{5,4,3,2,1,0:T(8,128)(2,1)}), bf16[8,1,6,8,16,128]{5,4,3,2,1,0:T(8,128)(2,1)}, u32[]{:S(2)}, u32[]{:S(2)}) async-start(bf16[8,1,6,8,16,128]{5,4,3,2,1,0:T(8,128)(2,1)} %triangle_0.1), calls=%async_computation.5 | async-start | bytes 3145728 | tf_op jit(solution)/shard_map/all_to_all | solution.py:495
  496.2 9.7 %copy-start.1 = (bf16[512,768]{1,0:T(8,128)(2,1)S(1)}, bf16[512,768]{1,0:T(8,128)(2,1)}, u32[]{:S(2)}) copy-start(bf16[512,768]{1,0:T(8,128)(2,1)} %param.21) | copy-start | bytes 2359300

commit v4 on v2

--- a/solution.py
+++ b/solution.py
@@ -632,18 +632,17 @@
         )
     pair_out, pair_grad = whole
 
-    left_rest = swap(left_1, right_all)
+    left_rest = swap(left_1, right_all, mixed)
     outgoing = pick_blocks(rights, send_row, send_slot, offsets)
     arrived = [lax.ppermute(v, "grp", ring) for v, ring in zip(outgoing, rings)]
-    near_mixed, first_mixed = mixed[None], None
+    near_mixed = mixed[None]
     for step in [1 << n for n in range(block_rows.bit_length() - 1)]:
         other = lax.ppermute(near_mixed, "row", [(r, r ^ step) for r in range(parts)])
         swapped = (row_index & step) > 0
         near_mixed = jnp.concatenate(
             [jnp.where(swapped, other, near_mixed), jnp.where(swapped, near_mixed, other)], axis=0
         )
-        first_mixed = near_mixed if first_mixed is None else first_mixed
-    left_lead = swap(left_0, left_rest, first_mixed, pair_grad, *outgoing)
+    left_lead = swap(left_0, left_rest, near_mixed, pair_grad, *outgoing)
     sharers = parts // block_rows
     sent_mixed = lax.dynamic_index_in_dim(near_mixed, row_index % block_rows, 1, keepdims=False)
     senders = [((r % sharers) * block_rows + r // sharers, r) for r in range(parts)]
@@ -658,7 +657,7 @@
     near_sums_0 = triangle_rows(left_near_0, *near_args, 0, sums)
     near_lead = pairwise(near_sums_0)
     sums = triangle_rows([left_lead], *args, 0, near_sums_0[0], mixed_own)[0]
-    tri_lead = swap(sums, tri_rest)
+    tri_lead = swap(sums, tri_rest, *near_rest)
     own_nodes = lax.dynamic_slice_in_dim(node_feats, row_index * node_rows, node_rows, 0)
     node_out = (
         own_nodes.astype(F32) + jnp.dot(mixed_own, full(3), preferred_element_type=F32)

time: 627 us -> 542 us (0.86)
  waiting for transfers between devices: 244 us -> 154 us
    all_to_all x7, waiting for transfers between devices: 68 us -> 17.6 us  [swap(): lax.all_to_all(after(values, *earlier), 'row', split_axis=0, concat_axis=...]
    ppermute x12, waiting for transfers between devices: 38.7 us -> 10.8 us  [pairwise(): lax.ppermute(pieces[d], 'row', [(r, r ^ d) for r in range(parts)])]
    all_to_all x7, starting transfers between devices: 36.7 us -> 44.5 us  [swap(): lax.all_to_all(after(values, *earlier), 'row', split_axis=0, concat_axis=...]
    ppermute x3, waiting for transfers between devices: 7.89 us -> 1.23 us  [per_device(): arrived = [lax.ppermute(v, 'grp', ring) for v, ring in zip(outgoing, rings)]]
  transfers between devices with their start and end apart: 36 -> 36, of which waited for: 14 -> 15; matrix products, arithmetic and copies ran while one was open for 9% -> 11% of each run, Pallas kernels for 34% -> 40%
where the time goes in v4:
time: 542 us; the launch traced here: 532 us
  Pallas kernels  220 us (41%)
  waiting for transfers between devices  154 us (28%)
  starting transfers between devices  90.3 us (17%)
  local copies, waits for them, and re-layouts  31.3 us (6%)
  other arithmetic  23.6 us (4%)
  matrix products  10.3 us (2%)
    pallas_call x4, Pallas kernels, triangle_rows(): pl.pallas_call(body, grid=(part, count), in_specs=[smem] * 2 + row_specs...  76 us
    ppermute x5, waiting for transfers between devices, doubled(): lax.ppermute(stacked, axis, pairs)  66.1 us
    pallas_call x2, Pallas kernels, gradient_rows(): pl.pallas_call(body, grid=(count, slots), in_specs=[big, pl.BlockSpec((No...  47.2 us
    all_to_all x7, starting transfers between devices, swap(): lax.all_to_all(after(values, *earlier), 'row', split_axis=0, concat_axis=...  44.5 us
    pallas_call x2, Pallas kernels, project_rows(): pl.pallas_call(body, grid=(count, slots), in_specs=[pl.BlockSpec((None, N...  39.7 us
    ppermute x2, waiting for transfers between devices, per_device(): lax.ppermute(near_mixed, 'row', [(r, r ^ step) for r in range(parts)])  37.2 us
    pallas_call x2, Pallas kernels, finish_rows(): pl.pallas_call(body, grid=(count, slots), in_specs=[pl.BlockSpec(memory_s...  35.1 us
    ppermute x12, starting transfers between devices, pairwise(): lax.ppermute(pieces[d], 'row', [(r, r ^ d) for r in range(parts)])  24.9 us
  transfers between devices with their start and end apart: 36, of which 15 were waited for; matrix products, arithmetic and copies ran while one was open for 11% of the time, Pallas kernels for 40%

profile of v4, /device:TPU:0, one launch (start us, length us, event | category | flops | bytes accessed | tf_op | source)
XLA Modules:
  0.0 531.7 jit_solution(3329900579489726758)
XLA Ops:
  2.0 4.1 collective-permute-start
  8.4 10.9 %project_0.1 = (bf16[4,1,6,8,16,128]{5,4,3,2,1,0:T(8,128)(2,1)}, bf16[8,1,6,4,16,128]{5,4,3,2,1,0:T(8,128)(2,1)}, bf16[8,1,6,8,16,128]{5,4,3,2,1,0:T(8,128)(2,1)...) custom-call(bf16[4,6,16,128,128]{4,3,2,1,0:T(8,128)(2,1)} %x_ref.11, ...), custom_call_target="tpu_custom_call" | custom-call | tf_op jit(solution)/shard_map/project_0/pallas_call | solution.py:82
  19.3 3.8 all-to-all-start
  23.1 2.0 collective-permute-start.1
  25.1 28.8 %project_1.1 = (bf16[4,3,6,8,16,128]{5,4,3,2,1,0:T(8,128)(2,1)}, bf16[8,3,6,4,16,128]{5,4,3,2,1,0:T(8,128)(2,1)}, bf16[8,3,6,8,16,128]{5,4,3,2,1,0:T(8,128)(2,1)...) custom-call(bf16[4,6,16,128,128]{4,3,2,1,0:T(8,128)(2,1)} %x_ref.11, ...), custom_call_target="tpu_custom_call" | custom-call | tf_op jit(solution)/shard_map/project_1/pallas_call | solution.py:82
  55.0 4.8 all-to-all-done.refs_0_.refs_4_
  61.0 4.6 all-to-all-start.1
  67.5 49.6 %collective-permute-done.2 = bf16[4,96,768]{2,1,0:T(8,128)(2,1)} collective-permute-done((bf16[4,96,768]{2,1,0:T(8,128)(2,1)S(1)}, bf16[4,96,768]{2,1,0:T(8,128)(2,1)}, u32[]{:S(2)}, u32[]{:S(2)}) %collective-permute-start.2) | collective-permute-done | bytes 589856 | tf_op jit(solution)/shard_map/ppermute | solution.py:419
  121.6 3.8 collective-permute-start.11
  126.4 2.0 collective-permute-start.14
  129.6 15.4 %collective-permute-done.3 = bf16[1,8,96,768]{3,2,1,0:T(8,128)(2,1)S(1)} collective-permute-done((bf16[1,8,96,768]{3,2,1,0:T(8,128)(2,1)S(1)}, bf16[1,8,96,768]{3,2,1,0:T(8,128)(2,1)S(1)}, u32[]{:S(2)}, u32[]{:S(2)}) %collective-permute-start.3) | collective-permute-done | bytes 1179680 | tf_op jit(solution)/shard_map/ppermute | solution.py:419
  156.3 3.8 pad_maximum_fusion
  160.1 2.1 collective-permute-done.14.refs_1_
  162.3 11.3 %collective-permute-start.15 = (bf16[1,1,6,8,16,128]{5,4,3,2,1,0:T(8,128)(2,1)S(1)}, bf16[1,1,6,8,16,128]{5,4,3,2,1,0:T(8,128)(2,1)S(1)}, u32[]{:S(2)}, u32[]{:S(2)}) collective-permute-start(bf16[1,1,6,8,16,128]{5,4,3,2,1,0:T(8,128)(2,1)S(1)} %copy-done.27), channel_id=1, source_target_pairs={{0,2},{1,3},{2,0},{3,1},{4,6},{5,7},{6,4},{7,5},{8,10},{9,11},{10,... | collective-permute-start | bytes 589832 | tf_op jit(solution)/shard_map/ppermute | solution.py:552
  173.5 3.7 maximum_bitcast_fusion
  177.2 2.0 collective-permute-done.15.refs_2_
  179.9 2.2 collective-permute-done.16.refs_3_
  182.8 4.9 all-to-all-start.2
  198.0 6.1 %pick_blocks.2 = (bf16[8,8,8,16,128]{4,3,2,1,0:T(8,128)(2,1)}, bf16[8,8,8,16,128]{4,3,2,1,0:T(8,128)(2,1)}, bf16[8,8,8,16,128]{4,3,2,1,0:T(8,128)(2,1)}) custom-call(s32[3,2]{1,0:T(4,128)} %copy-done.32, s32[3,2,4]{2,1,0:T(2,128)} %multiply_reduce_fusion.2.slot_ref, bf16[8,1,6,8,16,128]{5,4,3,2,1,0:T(8,128)(2,1)} %copy-done.3, ...), custom_call_target="tpu_custom_call" | custom-call | tf_op jit(solution)/shard_map/pick_blocks/pallas_call | solution.py:128
  204.9 5.4 %collective-permute-done.7 = bf16[2,128,768]{2,1,0:T(8,128)(2,1)} collective-permute-done((bf16[2,128,768]{2,1,0:T(8,128)(2,1)}, bf16[2,128,768]{2,1,0:T(8,128)(2,1)}, u32[]{:S(2)}, u32[]{:S(2)}) %collective-permute-start.7) | collective-permute-done | bytes 393248 | tf_op jit(solution)/shard_map/ppermute | solution.py:581
  210.3 2.8 pad_maximum_fusion.2
  213.1 5.4 %gather_fusion.6 = bf16[32,96,768]{2,1,0:T(8,128)(2,1)} fusion(bf16[8,4,96,768]{3,2,0,1:T(8,128)(2,1)} %maximum_bitcast_fusion, s32[32]{0:T(128)S(1)} %reshape.373), kind=kCustom, calls=%fused_computation.6 | custom fusion | bytes 9437440 | tf_op jit(solution)/shard_map/gather | solution.py:571
  218.4 2.6 fusion.34
  223.4 3.0 convolution_convert_fusion
  226.4 3.0 convolution_convert_fusion.1
  229.5 2.1 collective-permute-done.8.refs_2_.refs_6_
  232.9 12.2 %attend.1 = (bf16[4,16,768]{2,1,0:T(8,128)(2,1)}, bf16[4,6,256,128]{3,2,1,0:T(8,128)(2,1)}) custom-call(s32[4,6]{1,0:T(4,128)} %reshape.326.place_ref, s32[4,6]{1,0:T(4,128)} %copy.64.mask_ref, f32[4,6]{1,0:T(4,128)} %compare_convert_fusion.1.flag_ref, bf16[4,16,768]{2,1,0:T(8,128)(2,1)} %bitcast.97, bf16[4,16,768]{2,1,0:T(8,128)(2,1)} %bitcast.96, ...), custom_call_target="tpu_custom_call" | custom-call | tf_op jit(solution)/shard_map/attend/pallas_call | solution.py:295
  245.1 12.8 %all-to-all-done.2.refs_0_.refs_1_ = bf16[8,4,6,4,16,128]{5,4,3,2,1,0:T(8,128)(2,1)} async-done(((bf16[8,4,6,4,16,128]{5,4,3,2,1,0:T(8,128)(2,1)}), bf16[8,4,6,4,16,128]{5,4,3,2,1,0:T(8,128)(2,1)}, u32[]{:S(2)}, u32[]{:S(2)}) %all-to-all-start.2) | async-done | bytes 3145760 | tf_op jit(solution)/shard_map/all_to_all | solution.py:527
  257.9 4.3 all-to-all-start.3
  265.4 12.7 %gradient_0.1 = (bf16[4,6,16,128,128]{4,3,2,1,0:T(8,128)(2,1)}, bf16[4,6,16,128,128]{4,3,2,1,0:T(8,128)(2,1)}) custom-call(bf16[4,6,16,128,128]{4,3,2,1,0:T(8,128)(2,1)} %x_ref.11, bf16[4,6,256,128]{3,2,1,0:T(8,128)(2,1)} %get-tuple-element.52.g_ref, bf16[1,6,256,128]{3,2,1,0:T(8,128)(2,1)} %get-tuple-element.50.refs_0_.b_ref, ...), custom_call_target="tpu_custom_call" | custom-call | tf_op jit(solution)/shard_map/gradient_0/pallas_call | solution.py:337
  278.1 34.5 %gradient_1.1 = (bf16[4,6,16,128,128]{4,3,2,1,0:T(8,128)(2,1)}, bf16[4,6,16,128,128]{4,3,2,1,0:T(8,128)(2,1)}) custom-call(bf16[4,6,16,128,128]{4,3,2,1,0:T(8,128)(2,1)} %x_ref.11, bf16[4,6,256,128]{3,2,1,0:T(8,128)(2,1)} %get-tuple-element.52.g_ref, ...), custom_call_target="tpu_custom_call", output_to_operand_aliasing={{0}: (5, {}), {1}: (6, {})} | custom-call | tf_op jit(solution)/shard_map/gradient_1/pallas_call | solution.py:337
  312.7 3.8 pick_blocks.3
  316.5 6.0 %all-to-all-start.4 = ((bf16[8,1,6,4,16,128]{5,4,3,2,1,0:T(8,128)(2,1)}), bf16[8,1,6,4,16,128]{5,4,3,2,1,0:T(8,128)(2,1)S(1)}, u32[]{:S(2)}, u32[]{:S(2)}) async-start(bf16[8,1,6,4,16,128]{5,4,3,2,1,0:T(8,128)(2,1)} %get-tuple-element.73), calls=%async_computation.4 | async-start | bytes 1572864 | tf_op jit(solution)/shard_map/all_to_all | solution.py:527
  324.7 14.0 %collective-permute-done.13.refs_8_ = bf16[8,8,8,16,128]{4,3,2,1,0:T(8,128)(2,1)} collective-permute-done((bf16[8,8,8,16,128]{4,3,2,1,0:T(8,128)(2,1)}, bf16[8,8,8,16,128]{4,3,2,1,0:T(8,128)(2,1)}, u32[]{:S(2)}, u32[]{:S(2)}) %collective-permute-start.13) | collective-permute-done | bytes 2097184 | tf_op jit(solution)/shard_map/ppermute | solution.py:568
  338.7 36.4 %triangle_1.2 = (bf16[1,3,6,8,16,128]{5,4,3,2,1,0:T(8,128)(2,1)}, bf16[1,3,6,8,16,128]{5,4,3,2,1,0:T(8,128)(2,1)}, bf16[1,3,6,8,16,128]{5,4,3,2,1,0:T(8,128)(2,1)}, bf16[1,3,6,8,16,128]{5,4,3,2,1,0:T(8,128)(2,1)}) custom-call(s32[4,6]{1,0:T(4,128)} %reshape.404.source_ref, s32[4,6,6]{2,1,0:T(8,128)} %compare_select_fusion.1.place_ref, ...), custom_call_target="tpu_custom_call" | custom-call | tf_op jit(solution)/shard_map/triangle_1/pallas_call | solution.py:210
  377.4 18.8 %triangle_1.3.refs_9_ = bf16[8,3,6,4,16,128]{5,4,3,2,1,0:T(8,128)(2,1)} custom-call(s32[4,6]{1,0:T(4,128)} %reshape.404.source_ref, s32[4,6,6]{2,1,0:T(8,128)} %compare_select_fusion.1.place_ref, bf16[8,3,6,4,16,128]{5,4,3,2,1,0:T(8,128)(2,1)} %copy-done.9, bf16[8,4,6,4,16,128]{5,4,3,2,1,0:T(8,128)(2,1)} %all-to-all-done.2.refs_0_.refs_1_, ...), custom_call_target="tpu_custom_call" | custom-call | tf_op jit(solution)/shard_map/triangle_1/pallas_call | solution.py:210
  397.0 5.7 %all-to-all-start.5 = ((bf16[8,3,6,4,16,128]{5,4,3,2,1,0:T(8,128)(2,1)}), bf16[8,3,6,4,16,128]{5,4,3,2,1,0:T(8,128)(2,1)}, u32[]{:S(2)}, u32[]{:S(2)}) async-start(bf16[8,3,6,4,16,128]{5,4,3,2,1,0:T(8,128)(2,1)} %triangle_1.3.refs_9_), calls=%async_computation.5 | async-start | bytes 4718592 | tf_op jit(solution)/shard_map/all_to_all | solution.py:527
  402.8 2.0 collective-permute-start.23
  404.8 20.4 %collective-permute-done.23 = bf16[1,4,16,768]{3,2,1,0:T(8,128)(2,1)S(1)} collective-permute-done((bf16[1,4,16,768]{3,2,1,0:T(8,128)(2,1)S(1)}, bf16[1,4,16,768]{3,2,1,0:T(8,128)(2,1)S(1)}, u32[]{:S(2)}, u32[]{:S(2)}) %collective-permute-start.23) | collective-permute-done | bytes 98336 | tf_op jit(solution)/shard_map/ppermute | solution.py:640
  426.7 2.5 collective-permute-start.17
  430.7 16.8 %collective-permute-done.24 = bf16[2,4,16,768]{3,2,1,0:T(8,128)(2,1)S(1)} collective-permute-done((bf16[2,4,16,768]{3,2,1,0:T(8,128)(2,1)S(1)}, bf16[2,4,16,768]{3,2,1,0:T(8,128)(2,1)S(1)}, u32[]{:S(2)}, u32[]{:S(2)}) %collective-permute-start.24) | collective-permute-done | bytes 196640 | tf_op jit(solution)/shard_map/ppermute | solution.py:640
  448.5 13.1 %triangle_0.2 = (bf16[1,1,6,8,16,128]{5,4,3,2,1,0:T(8,128)(2,1)}, bf16[1,1,6,8,16,128]{5,4,3,2,1,0:T(8,128)(2,1)}, bf16[1,1,6,8,16,128]{5,4,3,2,1,0:T(8,128)(2,1)}, bf16[1,1,6,8,16,128]{5,4,3,2,1,0:T(8,128)(2,1)}) custom-call(s32[4,6]{1,0:T(4,128)} %reshape.404.source_ref, s32[4,6,6]{2,1,0:T(8,128)} %compare_select_fusion.1.place_ref, ...), custom_call_target="tpu_custom_call" | custom-call | tf_op jit(solution)/shard_map/triangle_0/pallas_call | solution.py:210
  462.3 7.7 %triangle_0.3 = bf16[8,1,6,4,16,128]{5,4,3,2,1,0:T(8,128)(2,1)} custom-call(s32[4,6]{1,0:T(4,128)} %reshape.404.source_ref, s32[4,6,6]{2,1,0:T(8,128)} %compare_select_fusion.1.place_ref, bf16[8,1,6,4,16,128]{5,4,3,2,1,0:T(8,128)(2,1)} %copy-done.14, bf16[8,4,6,4,16,128]{5,4,3,2,1,0:T(8,128)(2,1)} %all-to-all-done.2.refs_0_.refs_1_, ...), custom_call_target="tpu_custom_call" | custom-call | tf_op jit(solution)/shard_map/triangle_0/pallas_call | solution.py:210
  470.0 4.5 collective-permute-done.19.refs_3_
  474.5 15.1 %all-to-all-start.6 = ((bf16[8,1,6,4,16,128]{5,4,3,2,1,0:T(8,128)(2,1)}), bf16[8,1,6,4,16,128]{5,4,3,2,1,0:T(8,128)(2,1)S(1)}, u32[]{:S(2)}, u32[]{:S(2)}) async-start(bf16[8,1,6,4,16,128]{5,4,3,2,1,0:T(8,128)(2,1)} %triangle_0.3), calls=%async_computation.6 | async-start | bytes 1572864 | tf_op jit(solution)/shard_map/all_to_all | solution.py:527
  489.6 2.0 collective-permute-start.25
  495.1 25.4 %finish_1.1.gate_ref = bf16[4,6,16,128,128]{4,3,2,1,0:T(8,128)(2,1)} custom-call(s32[1]{0:T(128)} %bitcast.place_ref, bf16[4,6,16,128,128]{4,3,2,1,0:T(8,128)(2,1)} %x_ref.11, bf16[4,6,16,128,128]{4,3,2,1,0:T(8,128)(2,1)} %get-tuple-element.55.gate_ref, ...), custom_call_target="tpu_custom_call", output_to_operand_aliasing={{}: (2, {})} | custom-call | tf_op jit(solution)/shard_map/finish_1/pallas_call | solution.py:381
  521.5 9.7 %finish_0.1 = bf16[4,6,16,128,128]{4,3,2,1,0:T(8,128)(2,1)} custom-call(s32[1]{0:T(128)} %bitcast.place_ref, bf16[4,6,16,128,128]{4,3,2,1,0:T(8,128)(2,1)} %x_ref.11, bf16[4,6,16,128,128]{4,3,2,1,0:T(8,128)(2,1)} %finish_1.1.gate_ref, bf16[1,1,6,8,16,128]{5,4,3,2,1,0:T(8,128)(2,1)} %get-tuple-element.75.refs_5_.refs_0_, ...), custom_call_target="tpu_custom_call", output_to_operand_aliasing={{}: (2, {})} | custom-call | tf_op jit(solution)/shard_map/finish_0/pallas_call | solution.py:381
  (221 shorter events, 59.2 us)
Async XLA Ops:
  0.6 197.4 %copy-start = (bf16[512,768]{1,0:T(8,128)(2,1)S(1)}, bf16[512,768]{1,0:T(8,128)(2,1)}, u32[]{:S(2)}) copy-start(bf16[512,768]{1,0:T(8,128)(2,1)} %param.21) | copy-start | bytes 2359300
  2.0 17.3 %collective-permute-start = (bf16[1,96,768]{2,1,0:T(8,128)(2,1)S(1)}, bf16[1,96,768]{2,1,0:T(8,128)(2,1)S(1)}, u32[]{:S(2)}, u32[]{:S(2)}) collective-permute-start(bf16[1,96,768]{2,1,0:T(8,128)(2,1)S(1)} %dynamic-slice_bitcast_fusion), channel_id=1, source_target_pairs={{0,4},{1,5},{2,6},{3,7},{4,0},{5,1},{6,2},{7,3},{8,12},{9,13},{10,... | collective-permute-start | bytes 442376 | tf_op jit(solution)/shard_map/ppermute | solution.py:419
  19.3 40.5 %all-to-all-start = ((bf16[8,1,6,8,16,128]{5,4,3,2,1,0:T(8,128)(2,1)}), bf16[8,1,6,8,16,128]{5,4,3,2,1,0:T(8,128)(2,1)S(1)}, u32[]{:S(2)}, u32[]{:S(2)}) async-start(bf16[8,1,6,8,16,128]{5,4,3,2,1,0:T(8,128)(2,1)} %get-tuple-element.43), calls=%async_computation | async-start | bytes 3145728 | tf_op jit(solution)/shard_map/all_to_all | solution.py:527
  23.1 31.9 %collective-permute-start.1 = (bf16[2,96,768]{2,1,0:T(8,128)(2,1)S(1)}, bf16[2,96,768]{2,1,0:T(8,128)(2,1)S(1)}, u32[]{:S(2)}, u32[]{:S(2)}) collective-permute-start(bf16[2,96,768]{2,1,0:T(8,128)(2,1)S(1)} %pad_maximum_fusion.6), channel_id=1, source_target_pairs={{0,2},{1,3},{2,0},{3,1},{4,6},{5,7},{6,4},{7,5},{8,10},{9,11},{10,... | collective-permute-start | bytes 884744 | tf_op jit(solution)/shard_map/ppermute | solution.py:419
  61.0 121.8 %all-to-all-start.1 = ((bf16[8,3,6,8,16,128]{5,4,3,2,1,0:T(8,128)(2,1)}), bf16[8,3,6,8,16,128]{5,4,3,2,1,0:T(8,128)(2,1)}, u32[]{:S(2)}, u32[]{:S(2)}) async-start(bf16[8,3,6,8,16,128]{5,4,3,2,1,0:T(8,128)(2,1)} %get-tuple-element.45), calls=%async_computation.1 | async-start | bytes 9437184 | tf_op jit(solution)/shard_map/all_to_all | solution.py:527
  65.6 51.5 %collective-permute-start.2 = (bf16[4,96,768]{2,1,0:T(8,128)(2,1)S(1)}, bf16[4,96,768]{2,1,0:T(8,128)(2,1)}, u32[]{:S(2)}, u32[]{:S(2)}) collective-permute-start(bf16[4,96,768]{2,1,0:T(8,128)(2,1)S(1)} %pad_maximum_fusion.4), channel_id=1, source_target_pairs={{0,1},{1,0},{2,3},{3,2},{4,5},{5,4},{6,7},{7,6},{8,9},{9,8},{10,11... | collective-permute-start | bytes 1769480 | tf_op jit(solution)/shard_map/ppermute | solution.py:419
  67.5 52.4 %copy-start.16 = (bf16[4,3,6,8,16,128]{5,4,3,2,1,0:T(8,128)(2,1)S(1)}, bf16[4,3,6,8,16,128]{5,4,3,2,1,0:T(8,128)(2,1)}, u32[]{:S(2)}) copy-start(bf16[4,3,6,8,16,128]{5,4,3,2,1,0:T(8,128)(2,1)} %get-tuple-element.56) | copy-start | bytes 7077892
  118.3 26.7 %collective-permute-start.3 = (bf16[1,8,96,768]{3,2,1,0:T(8,128)(2,1)S(1)}, bf16[1,8,96,768]{3,2,1,0:T(8,128)(2,1)S(1)}, u32[]{:S(2)}, u32[]{:S(2)}) collective-permute-start(bf16[1,8,96,768]{3,2,1,0:T(8,128)(2,1)S(1)} %maximum_bitcast_fusion.1), channel_id=1, source_target_pairs={{0,16},{8,24},{16,0},{24,8},{1,17},{9,25},{17,1},{25,9},{2,18},{10... | collective-permute-start | bytes 3538952 | tf_op jit(solution)/shard_map/ppermute | solution.py:419
  121.4 61.4 %collective-permute-start.10 = (bf16[1,3,6,8,16,128]{5,4,3,2,1,0:T(8,128)(2,1)}, bf16[1,3,6,8,16,128]{5,4,3,2,1,0:T(8,128)(2,1)}, u32[]{:S(2)}, u32[]{:S(2)}) collective-permute-start(bf16[1,3,6,8,16,128]{5,4,3,2,1,0:T(8,128)(2,1)} %get-tuple-element.94), channel_id=1, source_target_pairs={{0,2},{1,3},{2,0},{3,1},{4,6},{5,7},{6,4},{7,5},{8,10},{9,11},{10,... | collective-permute-start | bytes 1769480 | tf_op jit(solution)/shard_map/ppermute | solution.py:552
  121.6 61.1 %collective-permute-start.11 = (bf16[1,3,6,8,16,128]{5,4,3,2,1,0:T(8,128)(2,1)}, bf16[1,3,6,8,16,128]{5,4,3,2,1,0:T(8,128)(2,1)}, u32[]{:S(2)}, u32[]{:S(2)}) collective-permute-start(bf16[1,3,6,8,16,128]{5,4,3,2,1,0:T(8,128)(2,1)} %get-tuple-element.93), channel_id=1, source_target_pairs={{0,3},{1,2},{2,1},{3,0},{4,7},{5,6},{6,5},{7,4},{8,11},{9,10},{10,... | collective-permute-start | bytes 1769480 | tf_op jit(solution)/shard_map/ppermute | solution.py:552
  125.5 57.3 %collective-permute-start.9 = (bf16[1,3,6,8,16,128]{5,4,3,2,1,0:T(8,128)(2,1)}, bf16[1,3,6,8,16,128]{5,4,3,2,1,0:T(8,128)(2,1)}, u32[]{:S(2)}, u32[]{:S(2)}) collective-permute-start(bf16[1,3,6,8,16,128]{5,4,3,2,1,0:T(8,128)(2,1)} %get-tuple-element.95), channel_id=1, source_target_pairs={{0,1},{1,0},{2,3},{3,2},{4,5},{5,4},{6,7},{7,6},{8,9},{9,8},{10,11... | collective-permute-start | bytes 1769480 | tf_op jit(solution)/shard_map/ppermute | solution.py:552
  126.4 35.9 %collective-permute-start.14 = (bf16[1,1,6,8,16,128]{5,4,3,2,1,0:T(8,128)(2,1)}, bf16[1,1,6,8,16,128]{5,4,3,2,1,0:T(8,128)(2,1)S(1)}, u32[]{:S(2)}, u32[]{:S(2)}) collective-permute-start(bf16[1,1,6,8,16,128]{5,4,3,2,1,0:T(8,128)(2,1)} %get-tuple-element.99), channel_id=1, source_target_pairs={{0,1},{1,0},{2,3},{3,2},{4,5},{5,4},{6,7},{7,6},{8,9},{9,8},{10,11... | collective-permute-start | bytes 589832 | tf_op jit(solution)/shard_map/ppermute | solution.py:552
  146.6 26.9 %collective-permute-start.4 = (bf16[2,8,96,768]{3,2,1,0:T(8,128)(2,1)}, bf16[2,8,96,768]{3,2,1,0:T(8,128)(2,1)}, u32[]{:S(2)}, u32[]{:S(2)}) collective-permute-start(bf16[2,8,96,768]{3,2,1,0:T(8,128)(2,1)} %pad_maximum_fusion.1), channel_id=1, source_target_pairs={{0,8},{8,0},{16,24},{24,16},{1,9},{9,1},{17,25},{25,17},{2,10},{10... | collective-permute-start | bytes 7077896 | tf_op jit(solution)/shard_map/ppermute | solution.py:419
  153.7 34.0 %copy-start.32 = (s32[3,2]{1,0:T(4,128)}, s32[3,2]{1,0:T(4,128)S(1)}, u32[]{:S(2)}) copy-start(s32[3,2]{1,0:T(4,128)S(1)} %get-tuple-element.83.row_ref) | copy-start | bytes 76
  156.3 17.2 %copy-start.26 = (bf16[1,1,6,8,16,128]{5,4,3,2,1,0:T(8,128)(2,1)S(1)}, bf16[1,1,6,8,16,128]{5,4,3,2,1,0:T(8,128)(2,1)}, u32[]{:S(2)}) copy-start(bf16[1,1,6,8,16,128]{5,4,3,2,1,0:T(8,128)(2,1)} %get-tuple-element.97) | copy-start | bytes 589828
  162.2 15.0 %copy-start.22 = (bf16[1,1,6,8,16,128]{5,4,3,2,1,0:T(8,128)(2,1)}, bf16[1,1,6,8,16,128]{5,4,3,2,1,0:T(8,128)(2,1)S(1)}, u32[]{:S(2)}) copy-start(bf16[1,1,6,8,16,128]{5,4,3,2,1,0:T(8,128)(2,1)S(1)} %collective-permute-done.14.refs_1_) | copy-start | bytes 589828
  162.3 17.0 %collective-permute-start.15 = (bf16[1,1,6,8,16,128]{5,4,3,2,1,0:T(8,128)(2,1)S(1)}, bf16[1,1,6,8,16,128]{5,4,3,2,1,0:T(8,128)(2,1)S(1)}, u32[]{:S(2)}, u32[]{:S(2)}) collective-permute-start(bf16[1,1,6,8,16,128]{5,4,3,2,1,0:T(8,128)(2,1)S(1)} %copy-done.27), channel_id=1, source_target_pairs={{0,2},{1,3},{2,0},{3,1},{4,6},{5,7},{6,4},{7,5},{8,10},{9,11},{10,... | collective-permute-start | bytes 589832 | tf_op jit(solution)/shard_map/ppermute | solution.py:552
  173.5 8.5 %collective-permute-start.16 = (bf16[1,1,6,8,16,128]{5,4,3,2,1,0:T(8,128)(2,1)S(1)}, bf16[1,1,6,8,16,128]{5,4,3,2,1,0:T(8,128)(2,1)S(1)}, u32[]{:S(2)}, u32[]{:S(2)}) collective-permute-start(bf16[1,1,6,8,16,128]{5,4,3,2,1,0:T(8,128)(2,1)S(1)} %copy-done.26), channel_id=1, source_target_pairs={{0,3},{1,2},{2,1},{3,0},{4,7},{5,6},{6,5},{7,4},{8,11},{9,10},{10,... | collective-permute-start | bytes 589832 | tf_op jit(solution)/shard_map/ppermute | solution.py:552
  182.8 75.1 %all-to-all-start.2 = ((bf16[8,4,6,4,16,128]{5,4,3,2,1,0:T(8,128)(2,1)}), bf16[8,4,6,4,16,128]{5,4,3,2,1,0:T(8,128)(2,1)}, u32[]{:S(2)}, u32[]{:S(2)}) async-start(bf16[8,4,6,4,16,128]{5,4,3,2,1,0:T(8,128)(2,1)} %pad_maximum_fusion), calls=%async_computation.2 | async-start | bytes 6291456 | tf_op jit(solution)/shard_map/all_to_all | solution.py:527
  189.2 15.7 %collective-permute-start.5 = (bf16[2,128,768]{2,1,0:T(8,128)(2,1)S(1)}, bf16[2,128,768]{2,1,0:T(8,128)(2,1)}, u32[]{:S(2)}, u32[]{:S(2)}) collective-permute-start(bf16[2,128,768]{2,1,0:T(8,128)(2,1)S(1)} %gather_fusion.7), channel_id=1, source_target_pairs={{0,8},{8,16},{16,24},{24,0},{1,9},{9,17},{17,25},{25,1},{2,10},{10... | collective-permute-start | bytes 1179656 | tf_op jit(solution)/shard_map/ppermute | solution.py:581
  190.6 14.3 %collective-permute-start.6 = (bf16[2,128,768]{2,1,0:T(8,128)(2,1)}, bf16[2,128,768]{2,1,0:T(8,128)(2,1)}, u32[]{:S(2)}, u32[]{:S(2)}) collective-permute-start(bf16[2,128,768]{2,1,0:T(8,128)(2,1)} %gather_fusion.8), channel_id=1, source_target_pairs={{0,16},{8,24},{16,0},{24,8},{1,17},{9,25},{17,1},{25,9},{2,18},{10... | collective-permute-start | bytes 1179656 | tf_op jit(solution)/shard_map/ppermute | solution.py:581
  193.3 17.0 %collective-permute-start.7 = (bf16[2,128,768]{2,1,0:T(8,128)(2,1)}, bf16[2,128,768]{2,1,0:T(8,128)(2,1)}, u32[]{:S(2)}, u32[]{:S(2)}) collective-permute-start(bf16[2,128,768]{2,1,0:T(8,128)(2,1)} %gather_fusion.9), channel_id=1, source_target_pairs={{0,24},{8,0},{16,8},{24,16},{1,25},{9,1},{17,9},{25,17},{2,26},{10... | collective-permute-start | bytes 1179656 | tf_op jit(solution)/shard_map/ppermute | solution.py:581
  198.0 12.3 %copy-start.8 = (bf16[512,768]{1,0:T(8,128)(2,1)S(1)}, bf16[512,768]{1,0:T(8,128)(2,1)}, u32[]{:S(2)}) copy-start(bf16[512,768]{1,0:T(8,128)(2,1)} %copy-done.7) | copy-start | bytes 2359300
  204.1 27.5 %collective-permute-start.8 = (bf16[8,8,8,16,128]{4,3,2,1,0:T(8,128)(2,1)}, bf16[8,8,8,16,128]{4,3,2,1,0:T(8,128)(2,1)S(1)}, u32[]{:S(2)}, u32[]{:S(2)}) collective-permute-start(bf16[8,8,8,16,128]{4,3,2,1,0:T(8,128)(2,1)} %get-tuple-element.46), channel_id=1, source_target_pairs={{0,8},{8,16},{16,24},{24,0},{1,9},{9,17},{17,25},{25,1},{2,10},{10... | collective-permute-start | bytes 6291464 | tf_op jit(solution)/shard_map/ppermute | solution.py:568
  257.9 58.6 %all-to-all-start.3 = ((bf16[8,3,6,4,16,128]{5,4,3,2,1,0:T(8,128)(2,1)}), bf16[8,3,6,4,16,128]{5,4,3,2,1,0:T(8,128)(2,1)S(1)}, u32[]{:S(2)}, u32[]{:S(2)}) async-start(bf16[8,3,6,4,16,128]{5,4,3,2,1,0:T(8,128)(2,1)} %get-tuple-element.71), calls=%async_computation.3 | async-start | bytes 4718592 | tf_op jit(solution)/shard_map/all_to_all | solution.py:527
  262.4 62.3 %collective-permute-start.12 = (bf16[8,8,8,16,128]{4,3,2,1,0:T(8,128)(2,1)}, bf16[8,8,8,16,128]{4,3,2,1,0:T(8,128)(2,1)}, u32[]{:S(2)}, u32[]{:S(2)}) collective-permute-start(bf16[8,8,8,16,128]{4,3,2,1,0:T(8,128)(2,1)} %get-tuple-element.47), channel_id=1, source_target_pairs={{0,16},{8,24},{16,0},{24,8},{1,17},{9,25},{17,1},{25,9},{2,18},{10... | collective-permute-start | bytes 6291464 | tf_op jit(solution)/shard_map/ppermute | solution.py:568
  263.9 74.8 %collective-permute-start.13 = (bf16[8,8,8,16,128]{4,3,2,1,0:T(8,128)(2,1)}, bf16[8,8,8,16,128]{4,3,2,1,0:T(8,128)(2,1)}, u32[]{:S(2)}, u32[]{:S(2)}) collective-permute-start(bf16[8,8,8,16,128]{4,3,2,1,0:T(8,128)(2,1)} %get-tuple-element.48), channel_id=1, source_target_pairs={{0,24},{8,0},{16,8},{24,16},{1,25},{9,1},{17,9},{25,17},{2,26},{10... | collective-permute-start | bytes 6291464 | tf_op jit(solution)/shard_map/ppermute | solution.py:568
  316.5 58.6 %copy-start.9 = (bf16[8,3,6,4,16,128]{5,4,3,2,1,0:T(8,128)(2,1)}, bf16[8,3,6,4,16,128]{5,4,3,2,1,0:T(8,128)(2,1)S(1)}, u32[]{:S(2)}) copy-start(bf16[8,3,6,4,16,128]{5,4,3,2,1,0:T(8,128)(2,1)S(1)} %all-to-all-done.3.refs_0_) | copy-start | bytes 7077892
  316.5 79.6 %all-to-all-start.4 = ((bf16[8,1,6,4,16,128]{5,4,3,2,1,0:T(8,128)(2,1)}), bf16[8,1,6,4,16,128]{5,4,3,2,1,0:T(8,128)(2,1)S(1)}, u32[]{:S(2)}, u32[]{:S(2)}) async-start(bf16[8,1,6,4,16,128]{5,4,3,2,1,0:T(8,128)(2,1)} %get-tuple-element.73), calls=%async_computation.4 | async-start | bytes 1572864 | tf_op jit(solution)/shard_map/all_to_all | solution.py:527
  322.5 52.6 %collective-permute-start.20 = (bf16[8,8,4,16,128]{4,3,2,1,0:T(8,128)(2,1)}, bf16[8,8,4,16,128]{4,3,2,1,0:T(8,128)(2,1)S(1)}, u32[]{:S(2)}, u32[]{:S(2)}) collective-permute-start(bf16[8,8,4,16,128]{4,3,2,1,0:T(8,128)(2,1)} %get-tuple-element.62.refs_10_), channel_id=1, source_target_pairs={{0,8},{8,16},{16,24},{24,0},{1,9},{9,17},{17,25},{25,1},{2,10},{10... | collective-permute-start | bytes 3145736 | tf_op jit(solution)/shard_map/ppermute | solution.py:637
  322.7 52.4 %collective-permute-start.21 = (bf16[8,8,4,16,128]{4,3,2,1,0:T(8,128)(2,1)}, bf16[8,8,4,16,128]{4,3,2,1,0:T(8,128)(2,1)S(1)}, u32[]{:S(2)}, u32[]{:S(2)}) collective-permute-start(bf16[8,8,4,16,128]{4,3,2,1,0:T(8,128)(2,1)} %get-tuple-element.63.refs_11_), channel_id=1, source_target_pairs={{0,16},{8,24},{16,0},{24,8},{1,17},{9,25},{17,1},{25,9},{2,18},{10... | collective-permute-start | bytes 3145736 | tf_op jit(solution)/shard_map/ppermute | solution.py:637
  323.3 53.1 %collective-permute-start.22 = (bf16[8,8,4,16,128]{4,3,2,1,0:T(8,128)(2,1)}, bf16[8,8,4,16,128]{4,3,2,1,0:T(8,128)(2,1)S(1)}, u32[]{:S(2)}, u32[]{:S(2)}) collective-permute-start(bf16[8,8,4,16,128]{4,3,2,1,0:T(8,128)(2,1)} %get-tuple-element.64.refs_12_), channel_id=1, source_target_pairs={{0,24},{8,0},{16,8},{24,16},{1,25},{9,1},{17,9},{25,17},{2,26},{10... | collective-permute-start | bytes 3145736 | tf_op jit(solution)/shard_map/ppermute | solution.py:637
  397.0 77.5 %all-to-all-start.5 = ((bf16[8,3,6,4,16,128]{5,4,3,2,1,0:T(8,128)(2,1)}), bf16[8,3,6,4,16,128]{5,4,3,2,1,0:T(8,128)(2,1)}, u32[]{:S(2)}, u32[]{:S(2)}) async-start(bf16[8,3,6,4,16,128]{5,4,3,2,1,0:T(8,128)(2,1)} %triangle_1.3.refs_9_), calls=%async_computation.5 | async-start | bytes 4718592 | tf_op jit(solution)/shard_map/all_to_all | solution.py:527
  402.8 22.4 %collective-permute-start.23 = (bf16[1,4,16,768]{3,2,1,0:T(8,128)(2,1)S(1)}, bf16[1,4,16,768]{3,2,1,0:T(8,128)(2,1)S(1)}, u32[]{:S(2)}, u32[]{:S(2)}) collective-permute-start(bf16[1,4,16,768]{3,2,1,0:T(8,128)(2,1)S(1)} %bitcast.104), channel_id=1, source_target_pairs={{0,1},{1,0},{2,3},{3,2},{4,5},{5,4},{6,7},{7,6},{8,9},{9,8},{10,11... | collective-permute-start | bytes 294920 | tf_op jit(solution)/shard_map/ppermute | solution.py:640
  425.2 22.3 %collective-permute-start.24 = (bf16[2,4,16,768]{3,2,1,0:T(8,128)(2,1)S(1)}, bf16[2,4,16,768]{3,2,1,0:T(8,128)(2,1)S(1)}, u32[]{:S(2)}, u32[]{:S(2)}) collective-permute-start(bf16[2,4,16,768]{3,2,1,0:T(8,128)(2,1)S(1)} %pad_maximum_fusion.7), channel_id=1, source_target_pairs={{0,2},{1,3},{2,0},{3,1},{4,6},{5,7},{6,4},{7,5},{8,10},{9,11},{10,... | collective-permute-start | bytes 589832 | tf_op jit(solution)/shard_map/ppermute | solution.py:640
  426.7 43.3 %collective-permute-start.17 = (bf16[1,3,6,8,16,128]{5,4,3,2,1,0:T(8,128)(2,1)}, bf16[1,3,6,8,16,128]{5,4,3,2,1,0:T(8,128)(2,1)S(1)}, u32[]{:S(2)}, u32[]{:S(2)}) collective-permute-start(bf16[1,3,6,8,16,128]{5,4,3,2,1,0:T(8,128)(2,1)} %get-tuple-element.66), channel_id=1, source_target_pairs={{0,1},{1,0},{2,3},{3,2},{4,5},{5,4},{6,7},{7,6},{8,9},{9,8},{10,11... | collective-permute-start | bytes 1769480 | tf_op jit(solution)/shard_map/ppermute | solution.py:552
  429.2 40.8 %collective-permute-start.18 = (bf16[1,3,6,8,16,128]{5,4,3,2,1,0:T(8,128)(2,1)}, bf16[1,3,6,8,16,128]{5,4,3,2,1,0:T(8,128)(2,1)S(1)}, u32[]{:S(2)}, u32[]{:S(2)}) collective-permute-start(bf16[1,3,6,8,16,128]{5,4,3,2,1,0:T(8,128)(2,1)} %get-tuple-element.67), channel_id=1, source_target_pairs={{0,2},{1,3},{2,0},{3,1},{4,6},{5,7},{6,4},{7,5},{8,10},{9,11},{10,... | collective-permute-start | bytes 1769480 | tf_op jit(solution)/shard_map/ppermute | solution.py:552
  429.9 44.6 %collective-permute-start.19 = (bf16[1,3,6,8,16,128]{5,4,3,2,1,0:T(8,128)(2,1)}, bf16[1,3,6,8,16,128]{5,4,3,2,1,0:T(8,128)(2,1)}, u32[]{:S(2)}, u32[]{:S(2)}) collective-permute-start(bf16[1,3,6,8,16,128]{5,4,3,2,1,0:T(8,128)(2,1)} %get-tuple-element.68), channel_id=1, source_target_pairs={{0,3},{1,2},{2,1},{3,0},{4,7},{5,6},{6,5},{7,4},{8,11},{9,10},{10,... | collective-permute-start | bytes 1769480 | tf_op jit(solution)/shard_map/ppermute | solution.py:552
  447.5 14.1 %collective-permute-start.28 = (bf16[4,16,768]{2,1,0:T(8,128)(2,1)S(1)}, bf16[4,16,768]{2,1,0:T(8,128)(2,1)S(1)}, u32[]{:S(2)}, u32[]{:S(2)}) collective-permute-start(bf16[4,16,768]{2,1,0:T(8,128)(2,1)S(1)} %fusion.6), channel_id=1, source_target_pairs={{0,0},{4,1},{1,2},{5,3},{2,4},{6,5},{3,6},{7,7},{8,8},{12,9},{9,10... | collective-permute-start | bytes 294920 | tf_op jit(solution)/shard_map/ppermute | solution.py:650
  462.3 27.4 %copy-start.38 = (bf16[1,1,6,8,16,128]{5,4,3,2,1,0:T(8,128)(2,1)S(1)}, bf16[1,1,6,8,16,128]{5,4,3,2,1,0:T(8,128)(2,1)}, u32[]{:S(2)}) copy-start(bf16[1,1,6,8,16,128]{5,4,3,2,1,0:T(8,128)(2,1)} %get-tuple-element.76) | copy-start | bytes 589828
  462.3 29.4 %copy-start.37 = (bf16[1,1,6,8,16,128]{5,4,3,2,1,0:T(8,128)(2,1)S(1)}, bf16[1,1,6,8,16,128]{5,4,3,2,1,0:T(8,128)(2,1)}, u32[]{:S(2)}) copy-start(bf16[1,1,6,8,16,128]{5,4,3,2,1,0:T(8,128)(2,1)} %get-tuple-element.77) | copy-start | bytes 589828
  462.3 30.8 %copy-start.36 = (bf16[1,1,6,8,16,128]{5,4,3,2,1,0:T(8,128)(2,1)S(1)}, bf16[1,1,6,8,16,128]{5,4,3,2,1,0:T(8,128)(2,1)}, u32[]{:S(2)}) copy-start(bf16[1,1,6,8,16,128]{5,4,3,2,1,0:T(8,128)(2,1)} %get-tuple-element.78) | copy-start | bytes 589828
  462.3 30.9 %copy-start.6 = (bf16[8,1,96,768]{3,2,1,0:T(8,128)(2,1)S(1)}, bf16[8,1,96,768]{3,2,1,0:T(8,128)(2,1)}, u32[]{:S(2)}) copy-start(bf16[8,1,96,768]{3,2,1,0:T(8,128)(2,1)} %copy-done.5) | copy-start | bytes 3538948
  470.0 25.1 %copy-start.19 = (bf16[1,3,6,8,16,128]{5,4,3,2,1,0:T(8,128)(2,1)}, bf16[1,3,6,8,16,128]{5,4,3,2,1,0:T(8,128)(2,1)S(1)}, u32[]{:S(2)}) copy-start(bf16[1,3,6,8,16,128]{5,4,3,2,1,0:T(8,128)(2,1)S(1)} %collective-permute-done.17.refs_1_) | copy-start | bytes 1769476
  474.5 46.0 %all-to-all-start.6 = ((bf16[8,1,6,4,16,128]{5,4,3,2,1,0:T(8,128)(2,1)}), bf16[8,1,6,4,16,128]{5,4,3,2,1,0:T(8,128)(2,1)S(1)}, u32[]{:S(2)}, u32[]{:S(2)}) async-start(bf16[8,1,6,4,16,128]{5,4,3,2,1,0:T(8,128)(2,1)} %triangle_0.3), calls=%async_computation.6 | async-start | bytes 1572864 | tf_op jit(solution)/shard_map/all_to_all | solution.py:527
  489.6 30.9 %collective-permute-start.25 = (bf16[1,1,6,8,16,128]{5,4,3,2,1,0:T(8,128)(2,1)S(1)}, bf16[1,1,6,8,16,128]{5,4,3,2,1,0:T(8,128)(2,1)S(1)}, u32[]{:S(2)}, u32[]{:S(2)}) collective-permute-start(bf16[1,1,6,8,16,128]{5,4,3,2,1,0:T(8,128)(2,1)S(1)} %copy-done.38), channel_id=1, source_target_pairs={{0,1},{1,0},{2,3},{3,2},{4,5},{5,4},{6,7},{7,6},{8,9},{9,8},{10,11... | collective-permute-start | bytes 589832 | tf_op jit(solution)/shard_map/ppermute | solution.py:552
  491.6 28.9 %collective-permute-start.26 = (bf16[1,1,6,8,16,128]{5,4,3,2,1,0:T(8,128)(2,1)S(1)}, bf16[1,1,6,8,16,128]{5,4,3,2,1,0:T(8,128)(2,1)}, u32[]{:S(2)}, u32[]{:S(2)}) collective-permute-start(bf16[1,1,6,8,16,128]{5,4,3,2,1,0:T(8,128)(2,1)S(1)} %copy-done.37), channel_id=1, source_target_pairs={{0,2},{1,3},{2,0},{3,1},{4,6},{5,7},{6,4},{7,5},{8,10},{9,11},{10,... | collective-permute-start | bytes 589832 | tf_op jit(solution)/shard_map/ppermute | solution.py:552
  493.1 27.5 %collective-permute-start.27 = (bf16[1,1,6,8,16,128]{5,4,3,2,1,0:T(8,128)(2,1)S(1)}, bf16[1,1,6,8,16,128]{5,4,3,2,1,0:T(8,128)(2,1)}, u32[]{:S(2)}, u32[]{:S(2)}) collective-permute-start(bf16[1,1,6,8,16,128]{5,4,3,2,1,0:T(8,128)(2,1)S(1)} %copy-done.36), channel_id=1, source_target_pairs={{0,3},{1,2},{2,1},{3,0},{4,7},{5,6},{6,5},{7,4},{8,11},{9,10},{10,... | collective-permute-start | bytes 589832 | tf_op jit(solution)/shard_map/ppermute | solution.py:552
  (27 other events, 107.3 us)
